TPU v7x, 128 devices: a whole 4x4x4 slice. The times are simulated.
128 devices in a mesh: row: 16 (over y_hi, z, core), col: 8 (over y_lo, x).
Axes of the slice: x: 4, y: 4 (y_hi: 2, y_lo: 2; y = y_hi * 2 + y_lo), z: 4, core: 2. Of those that a mesh axis runs over, the one named last changes fastest.
Arguments:
- vectors: bfloat16 [2, 8, 32768], P(None, 'col', 'row'), may hold values from -6 to 6
- lr_left: bfloat16 [16, 8, 32, 8, 4096], P('row', 'col'), may hold values from -0.75 to 0.75
- lr_right: bfloat16 [16, 8, 32, 8, 4096], P('row', 'col'), may hold values from -0.09375 to 0.09375
- tile_rank: int32 [16, 8, 32], P('row', 'col'), may hold values from 0 to 8, as said below
- leaf_values: bfloat16 [16, 8, 8, 512, 512], P('row', 'col'), may hold values from -0.25 to 0.25
- leaf_places: int32 [16, 8, 8, 2], P('row', 'col'), may hold values from 0 to 63, as said below
- cluster_perm: int32 [16, 16384], P('row'), may hold values from 0 to 262143, as said below
- kappa: float32 [64, 32, 128], P('row', 'col'), may hold values from 0.25 to 4
Outputs:
- prior_action: float32 [2, 64, 32, 128], P(None, 'row', 'col')
Inputs may be any that keep to these rules, and one draw needn't show every extreme that they name: `tile_rank`: 0 exactly on the tiles that contain a leaf, 1 to 8 on the others. `leaf_places`: the 8 leaves of a block are distinct; entry 0 indexes rows and entry 1 column of the block in units of 512. `cluster_perm`: a permutation of all brick indices; within each aligned block of 2048 entries, every value of entry // 2048 occurs exactly 32 times or not at all.
All inputs are finite; a program needn't handle non-finite values.
Results may differ from a plain program's by a relative error of at most 0.0023.
Values may be sent and summed in bfloat16 or wider, within the bound.
No kernel may reach another device: no remote copies, remote signals or barrier semaphores. Data moves between devices by JAX's collectives and lax.ppermute only.
A program may use at most 64 MiB of HBM per device.

v0:
```python
import jax
import jax.numpy as jnp
from jax import lax
from jax.sharding import PartitionSpec as P

NVEC = 2
CX = 4
CY = 4
NZ = 128
TILE_ROWS = 4
TILE_COLS = 8
KMAX = 8
LEAF = 512


def copy_for_each(array, axis):
    size = lax.axis_size(axis)
    return lax.all_to_all(
        jnp.broadcast_to(array[None], (size, *array.shape)), axis, 0, 0, tiled=True
    )


def laid_out(blocks, dim):
    shape = list(blocks.shape[1:])
    shape[dim] *= blocks.shape[0]
    return jnp.moveaxis(blocks, 0, dim).reshape(shape)


def gather_directly(array, axis, dim):
    blocks = copy_for_each(array, axis)
    return laid_out(blocks, dim)


def cut_along(array, dim, size):
    before, after = (array.shape[:dim], array.shape[dim + 1 :])
    return jnp.moveaxis(array.reshape(*before, size, -1, *after), dim, 0)


def summed_on_arrival(array, axis, dim):
    blocks = cut_along(array, dim, lax.axis_size(axis))
    arrived = lax.all_to_all(blocks, axis, split_axis=0, concat_axis=0, tiled=True)
    return arrived.sum(axis=0)


def one_exchange(array, axis, axes, splits, concats):
    sizes = [lax.axis_size(a) for a in axes]
    blocks = cut_along(array, splits[0], sizes[0])
    blocks = jnp.moveaxis(cut_along(blocks, splits[1] + 1, sizes[1]), 0, 1)
    inside = blocks.shape[2:]
    blocks = blocks.reshape(-1, *inside)
    blocks = lax.all_to_all(blocks, axis, split_axis=0, concat_axis=0, tiled=True)
    blocks = laid_out(blocks.reshape(*sizes, *inside), concats[0] + 1)
    return laid_out(blocks, concats[1])


def extended(cells, sides, width):
    for axis, dim in sides:
        count = lax.axis_size(axis)
        ends = count - 1
        head = lax.slice_in_dim(cells, 0, width, axis=dim)
        tail = lax.slice_in_dim(cells, cells.shape[dim] - width, cells.shape[dim], axis=dim)
        cells = jnp.concatenate(
            [
                lax.ppermute(tail, axis, [(i, (i + 1) % count) for i in range(ends)]),
                cells,
                lax.ppermute(head, axis, [((i + 1) % count, i) for i in range(ends)]),
            ],
            axis=dim,
        )
    return cells


def prior_step(padded, stiffness):
    center = padded[:, 1:-1, 1:-1, :]
    flat_pad = jnp.pad(center, ((0, 0), (0, 0), (0, 0), (1, 1)))
    beside = padded[:, 2:, 1:-1, :] + padded[:, :-2, 1:-1, :]
    beside = beside + padded[:, 1:-1, 2:, :] + padded[:, 1:-1, :-2, :]
    beside = beside + flat_pad[..., 2:] + flat_pad[..., :-2]
    return ((6.0 + stiffness) * center - beside) * 0.125


def route(values, targets, groups, points, capacity, devices):
    target_dev = targets // points
    places = targets % points
    grouped = target_dev.reshape(groups, points)
    one_hot = (grouped[:, :, None] == jnp.arange(devices)[None, None, :]).astype(jnp.int32)
    running = jnp.cumsum(one_hot, axis=1)
    within = jnp.sum(running * one_hot, axis=2) - 1
    slot_index = jnp.arange(groups)[:, None] * capacity + within
    buffer_at = (grouped * (groups * capacity) + slot_index).reshape(-1)
    buffer_len = devices * groups * capacity
    send_values = jnp.zeros((values.shape[0], buffer_len), jnp.float32).at[:, buffer_at].set(values)
    send_places = jnp.full((1, buffer_len), points, jnp.int32).at[0, buffer_at].set(places)
    return (send_values, send_places)


def per_device(
    vectors, lr_left, lr_right, tile_rank, leaf_values, leaf_places, cluster_perm, kappa
):
    gathered = gather_directly(vectors, "row", 2)
    x_column = gathered[:, 0, :]
    tile_size = lr_left.shape[-1]
    rows_len = tile_size * TILE_ROWS
    x_tiles = x_column.reshape(NVEC, TILE_COLS, tile_size)
    far_right = lr_right[0, 0].reshape(TILE_ROWS, TILE_COLS, KMAX, tile_size)
    projected = jnp.einsum("abkp,vbp->abvk", far_right, x_tiles, preferred_element_type=jnp.float32)
    rank_mask = (
        jnp.arange(KMAX)[None, None, :] < tile_rank[0, 0].reshape(TILE_ROWS, TILE_COLS)[:, :, None]
    ).astype(jnp.float32)
    projected = (projected * rank_mask[:, :, None, :]).astype(jnp.bfloat16)
    far_left = lr_left[0, 0].reshape(TILE_ROWS, TILE_COLS, KMAX, tile_size)
    far_part = jnp.einsum(
        "abkp,abvk->vap", far_left, projected, preferred_element_type=jnp.float32
    ).reshape(NVEC, rows_len)
    leaf_pos = leaf_places[0, 0]
    x_sub = x_column.reshape(NVEC, x_column.shape[1] // LEAF, LEAF)
    picked = jnp.take(x_sub, leaf_pos[:, 1], axis=1)
    near_out = jnp.einsum(
        "lqp,vlp->vlq", leaf_values[0, 0], picked, preferred_element_type=jnp.float32
    )
    selector = (leaf_pos[:, 0][:, None] == jnp.arange(rows_len // LEAF)[None, :]).astype(
        jnp.float32
    )
    near_part = jnp.einsum("vlq,lr->vrq", near_out, selector, precision=lax.Precision.HIGHEST)
    partial_sums = far_part + near_part.reshape(NVEC, rows_len)
    points = vectors.shape[2]
    devices = lax.axis_size("row") * lax.axis_size("col")
    capacity = 2 * points // devices
    summed = summed_on_arrival(partial_sums, "col", 1)
    targets = lax.dynamic_slice_in_dim(cluster_perm[0], lax.axis_index("col") * points, points)
    send_values, send_places = route(summed, targets, 1, points, capacity, devices)
    row_count = lax.axis_size("row")
    value_grid = send_values.reshape(NVEC, row_count, send_values.shape[1] // row_count)
    place_grid = send_places.reshape(1, row_count, send_places.shape[1] // row_count)
    value_grid, place_grid = (
        one_exchange(value_grid, ("row", "col"), ("row", "col"), (1, 2), (1, 2)),
        one_exchange(place_grid, ("row", "col"), ("row", "col"), (1, 2), (1, 2)),
    )
    received_values = value_grid.reshape(NVEC, -1)
    received_places = place_grid.reshape(1, -1)
    field = (
        jnp.zeros((NVEC, points + 1), jnp.float32).at[:, received_places[0]].add(received_values)
    )
    field = field[:, :points].reshape(NVEC, CX, CY, NZ)
    stiff_rim = extended(kappa, (("row", 0), ("col", 1)), 1)
    global_x = lax.axis_index("row") * CX - 1 + jnp.arange(CX + 2)
    global_y = lax.axis_index("col") * CY - 1 + jnp.arange(CY + 2)
    inside_x = (global_x >= 0) & (global_x < CX * lax.axis_size("row"))
    inside_y = (global_y >= 0) & (global_y < CY * lax.axis_size("col"))
    border_mask = (inside_x[:, None] & inside_y[None, :]).astype(jnp.float32)[None, :, :, None]
    for repeat in range(2):
        padded = extended(field, (("row", 1), ("col", 2)), 2)
        middle = prior_step(padded, stiff_rim) * border_mask
        field = prior_step(middle, kappa)
    return field


def solution(mesh):
    in_specs = (
        P(None, "col", "row"),
        P("row", "col", None, None, None),
        P("row", "col", None, None, None),
        P("row", "col", None),
        P("row", "col", None, None, None),
        P("row", "col", None, None),
        P("row", None),
        P("row", "col", None),
    )
    out_specs = P(None, "row", "col", None)
    return jax.shard_map(
        per_device, mesh=mesh, in_specs=in_specs, out_specs=out_specs, check_vma=False
    )
```

profile of v0, /device:TPU:103, one launch (start us, length us, event | category | flops | bytes accessed | tf_op | source)
XLA Modules:
  0.0 172.0 jit_solution(8101093592776933477)
XLA Ops:
  0.0 1.6 broadcast_in_dim.24
  1.6 7.5 %all-to-all-start.1 = ((bf16[16,2,1,2048]{3,1,2,0:T(2,128)(2,1)}), bf16[16,2,1,2048]{3,1,2,0:T(2,128)(2,1)S(1)}, u32[]{:S(2)}, u32[]{:S(2)}) async-start(bf16[16,2,1,2048]{3,1,2,0:T(2,128)(2,1)} %broadcast_in_dim.24), calls=%async_computation.1 | async-start | bytes 262144 | tf_op jit(solution)/shard_map/all_to_all | solution.py:18
  9.0 0.7 fusion.56
  9.7 4.8 %collective-permute-start = (f32[1,4,128]{2,1,0:T(4,128)S(1)}, f32[1,4,128]{2,1,0:T(4,128)S(1)}, u32[]{:S(2)}, u32[]{:S(2)}) collective-permute-start(f32[1,4,128]{2,1,0:T(4,128)S(1)} %get-tuple-element.18), channel_id=1, source_target_pairs={{0,8},{8,16},{16,24},{24,32},{32,40},{40,48},{48,56},{56,64},{64,7... | collective-permute-start | bytes 6152 | tf_op jit(solution)/shard_map/ppermute | solution.py:64
  14.6 1.9 %collective-permute-start.1 = (f32[1,4,128]{2,1,0:T(4,128)S(1)}, f32[1,4,128]{2,1,0:T(4,128)S(1)}, u32[]{:S(2)}, u32[]{:S(2)}) collective-permute-start(f32[1,4,128]{2,1,0:T(4,128)S(1)} %get-tuple-element.17), channel_id=1, source_target_pairs={{8,0},{16,8},{24,16},{32,24},{40,32},{48,40},{56,48},{64,56},{72,6... | collective-permute-start | bytes 6152 | tf_op jit(solution)/shard_map/ppermute | solution.py:66
  16.5 0.7 constant_dynamic-slice_fusion
  17.2 0.3 fusion.12
  17.6 0.0 copy-start.2
  17.6 0.6 fusion.8
  18.2 0.3 copy.40
  18.6 0.0 copy-start.3
  18.6 0.0 copy-start.4
  18.7 0.1 broadcast.257
  18.8 0.6 fusion.7
  19.4 0.8 compare_select_fusion.1
  20.2 0.1 fusion.29
  20.3 0.1 and_reduce_fusion
  20.4 0.5 broadcast.314
  20.9 0.7 reduce.8
  21.6 0.1 lt.78
  21.7 0.1 fusion.40
  21.8 0.1 and_select_fusion.1
  21.8 8.1 %scatter_custom_fusion.2 = s32[4096]{0:T(1024)S(1)} fusion(s32[2048]{0:T(1024)S(1)} %broadcast_select_fusion.2, s32[2048]{0:T(1024)S(1)} %get-tuple-element.19, s32[]{:T(128)} %constant.44.clone.1), kind=kCustom, calls=%fused_computation.100 | custom fusion | bytes 16388
  29.9 0.7 reshape_transpose_transpose_reshape_transpose_reshape_reshape.3
  30.6 9.9 %all-to-all-start = ((s32[128,1,1,32]{3,2,1,0:T(1,128)}), s32[128,1,1,32]{3,2,1,0:T(1,128)S(1)}, u32[]{:S(2)}, u32[]{:S(2)}) async-start(s32[128,1,1,32]{3,2,1,0:T(1,128)} %bitcast.10), calls=%async_computation | async-start | bytes 131072 | tf_op jit(solution)/shard_map/all_to_all | solution.py:51
  40.5 0.6 gather_fusion
  41.1 3.4 %fusion.4 = f32[2,8,512]{2,0,1:T(2,128)S(1)} fusion(bf16[1,1,8,512,512]{4,3,2,1,0:T(8,128)(2,1)} %param.12, bf16[8,2,512]{2,1,0:T(2,128)(2,1)S(1)} %gather_fusion, pred[8]{0:T(512)(128)(4,1)S(1)} %and_bitcast_fusion), kind=kOutput, calls=%fused_computation.10 | convolution fusion | flops 8396800 | bytes 4243464 | tf_op jit(solution)/shard_map/lqp,vlp->vlq/dot_general | solution.py:118
  44.5 0.3 convolution_bitcast_fusion.1
  44.8 0.1 reshape.318
  44.9 6.3 %fusion.2 = f32[8,2,4,8]{3,1,2,0:T(2,128)S(1)} fusion(bf16[2,8,4096,1]{2,0,3,1:T(2,128)(2,1)S(1)} %bitcast.106, bf16[4,8,8,4096]{3,2,1,0:T(8,128)(2,1)} %bitcast.115), kind=kOutput, calls=%fused_computation.7 | convolution fusion | flops 4194304 | bytes 2230272 | tf_op jit(solution)/shard_map/abkp,vbp->abvk/dot_general | solution.py:106
  51.2 0.7 convolution_bitcast_fusion
  51.9 0.1 copy.48
  52.0 0.1 reshape.317
  52.1 0.8 copy.52
  52.8 5.2 %all-to-all-start.2 = ((f32[8,2,2048]{2,1,0:T(2,128)}), f32[8,2,2048]{2,1,0:T(2,128)S(1)}, u32[]{:S(2)}, u32[]{:S(2)}) async-start(f32[8,2,2048]{2,1,0:T(2,128)} %copy.52), calls=%async_computation.2 | async-start | bytes 262144 | tf_op jit(solution)/shard_map/all_to_all | solution.py:41
  58.0 0.1 squeeze_reshape_reshape.3
  58.1 3.8 %all-to-all-done.2 = f32[8,2,2048]{2,1,0:T(2,128)S(1)} async-done(((f32[8,2,2048]{2,1,0:T(2,128)}), f32[8,2,2048]{2,1,0:T(2,128)S(1)}, u32[]{:S(2)}, u32[]{:S(2)}) %all-to-all-start.2) | async-done | bytes 131104 | tf_op jit(solution)/shard_map/all_to_all | solution.py:41
  61.9 0.4 copy.54
  62.3 7.0 %scatter_custom_fusion = f32[2,4096]{0,1:T(8,128)} fusion(s32[2048]{0:T(1024)S(1)} %bitcast.107, f32[2048,2]{1,0:T(8,128)S(1)} %copy.54, f32[]{:T(128)} %constant.43.clone.1), kind=kCustom, calls=%fused_computation.15 | custom fusion | bytes 32772 | tf_op jit(solution)/shard_map/scatter | solution.py:92
  69.3 3.1 %copy.55 = f32[16,2,1,8,32]{4,1,3,0,2:T(2,128)} copy(f32[16,2,1,8,32]{1,4,3,0,2:T(8,128)} %bitcast.97) | data formatting | bytes 65536 | tf_op jit(solution)/shard_map/reshape | solution.py:36
  72.4 10.5 %all-to-all-start.3 = ((f32[128,2,1,32]{3,1,2,0:T(2,128)}), f32[128,2,1,32]{3,1,2,0:T(2,128)S(1)}, u32[]{:S(2)}, u32[]{:S(2)}) async-start(f32[128,2,1,32]{3,1,2,0:T(2,128)} %bitcast.44), calls=%async_computation.3 | async-start | bytes 262144 | tf_op jit(solution)/shard_map/all_to_all | solution.py:51
  82.9 5.7 %all-to-all-done.3 = f32[128,2,1,32]{3,1,2,0:T(2,128)S(1)} async-done(((f32[128,2,1,32]{3,1,2,0:T(2,128)}), f32[128,2,1,32]{3,1,2,0:T(2,128)S(1)}, u32[]{:S(2)}, u32[]{:S(2)}) %all-to-all-start.3) | async-done | bytes 32800 | tf_op jit(solution)/shard_map/all_to_all | solution.py:51
  88.6 2.2 %copy.56 = f32[2,16,8,32]{0,3,2,1:T(8,128)} copy(f32[2,16,8,32]{3,0,2,1:T(2,128)S(1)} %bitcast.103) | data formatting | bytes 65536 | tf_op jit(solution)/shard_map/transpose | solution.py:26
  90.8 25.5 %scatter_custom_fusion.1 = f32[2,2049]{0,1:T(8,128)S(1)} fusion(s32[4096]{0:T(1024)S(1)} %bitcast.111, f32[4096,2]{1,0:T(8,128)} %bitcast.102, f32[]{:T(128)} %constant.43.clone.1), kind=kCustom, calls=%fused_computation.19 | custom fusion | flops 8192 | bytes 16904 | tf_op jit(solution)/shard_map/scatter-add | solution.py:142
  116.3 1.0 slice.190
  117.3 1.6 copy.57
  118.9 5.2 %collective-permute-start.4 = (f32[2,2,4,128]{3,2,1,0:T(4,128)S(1)}, f32[2,2,4,128]{3,2,1,0:T(4,128)S(1)}, u32[]{:S(2)}, u32[]{:S(2)}) collective-permute-start(f32[2,2,4,128]{3,2,1,0:T(4,128)S(1)} %get-tuple-element.11), channel_id=1, source_target_pairs={{0,8},{8,16},{16,24},{24,32},{32,40},{40,48},{48,56},{56,64},{64,7... | collective-permute-start | bytes 24584 | tf_op jit(solution)/shard_map/ppermute | solution.py:64
  124.1 1.9 %collective-permute-start.5 = (f32[2,2,4,128]{3,2,1,0:T(4,128)S(1)}, f32[2,2,4,128]{3,2,1,0:T(4,128)S(1)}, u32[]{:S(2)}, u32[]{:S(2)}) collective-permute-start(f32[2,2,4,128]{3,2,1,0:T(4,128)S(1)} %get-tuple-element.12), channel_id=1, source_target_pairs={{8,0},{16,8},{24,16},{32,24},{40,32},{48,40},{56,48},{64,56},{72,6... | collective-permute-start | bytes 24584 | tf_op jit(solution)/shard_map/ppermute | solution.py:66
  126.0 3.8 %collective-permute-start.2 = (f32[6,1,128]{2,1,0:T(1,128)S(1)}, f32[6,1,128]{2,1,0:T(1,128)S(1)}, u32[]{:S(2)}, u32[]{:S(2)}) collective-permute-start(f32[6,1,128]{2,1,0:T(1,128)S(1)} %get-tuple-element.13), channel_id=1, source_target_pairs={{0,1},{1,2},{2,3},{3,4},{4,5},{5,6},{6,7},{8,9},{9,10},{10,11},{11... | collective-permute-start | bytes 9224 | tf_op jit(solution)/shard_map/ppermute | solution.py:64
  129.8 1.9 %collective-permute-start.3 = (f32[6,1,128]{2,1,0:T(1,128)S(1)}, f32[6,1,128]{2,1,0:T(1,128)S(1)}, u32[]{:S(2)}, u32[]{:S(2)}) collective-permute-start(f32[6,1,128]{2,1,0:T(1,128)S(1)} %get-tuple-element.14), channel_id=1, source_target_pairs={{1,0},{2,1},{3,2},{4,3},{5,4},{6,5},{7,6},{9,8},{10,9},{11,10},{12... | collective-permute-start | bytes 9224 | tf_op jit(solution)/shard_map/ppermute | solution.py:66
  131.8 0.9 collective-permute-done.5
  132.7 4.6 %collective-permute-start.6 = (f32[2,8,2,128]{3,2,1,0:T(2,128)S(1)}, f32[2,8,2,128]{3,2,1,0:T(2,128)S(1)}, u32[]{:S(2)}, u32[]{:S(2)}) collective-permute-start(f32[2,8,2,128]{3,2,1,0:T(2,128)S(1)} %get-tuple-element.7), channel_id=1, source_target_pairs={{0,1},{1,2},{2,3},{3,4},{4,5},{5,6},{6,7},{8,9},{9,10},{10,11},{11... | collective-permute-start | bytes 49160 | tf_op jit(solution)/shard_map/ppermute | solution.py:64
  137.3 1.9 %collective-permute-start.7 = (f32[2,8,2,128]{3,2,1,0:T(2,128)S(1)}, f32[2,8,2,128]{3,2,1,0:T(2,128)S(1)}, u32[]{:S(2)}, u32[]{:S(2)}) collective-permute-start(f32[2,8,2,128]{3,2,1,0:T(2,128)S(1)} %get-tuple-element.8), channel_id=1, source_target_pairs={{1,0},{2,1},{3,2},{4,3},{5,4},{6,5},{7,6},{9,8},{10,9},{11,10},{12... | collective-permute-start | bytes 49160 | tf_op jit(solution)/shard_map/ppermute | solution.py:66
  139.3 5.1 %collective-permute-done.7 = f32[2,8,2,128]{3,2,1,0:T(2,128)S(1)} collective-permute-done((f32[2,8,2,128]{3,2,1,0:T(2,128)S(1)}, f32[2,8,2,128]{3,2,1,0:T(2,128)S(1)}, u32[]{:S(2)}, u32[]{:S(2)}) %collective-permute-start.7) | collective-permute-done | bytes 16416 | tf_op jit(solution)/shard_map/ppermute | solution.py:66
  144.4 0.1 fusion.18
  144.5 0.1 fusion.33
  144.6 9.4 %collective-permute-start.8 = (f32[2,2,4,128]{3,2,1,0:T(4,128)S(1)}, f32[2,2,4,128]{3,2,1,0:T(4,128)S(1)}, u32[]{:S(2)}, u32[]{:S(2)}) collective-permute-start(f32[2,2,4,128]{3,2,1,0:T(4,128)S(1)} %get-tuple-element.9), channel_id=1, source_target_pairs={{0,8},{8,16},{16,24},{24,32},{32,40},{40,48},{48,56},{56,64},{64,7... | collective-permute-start | bytes 24584 | tf_op jit(solution)/shard_map/ppermute | solution.py:64
  154.0 1.9 %collective-permute-start.9 = (f32[2,2,4,128]{3,2,1,0:T(4,128)S(1)}, f32[2,2,4,128]{3,2,1,0:T(4,128)S(1)}, u32[]{:S(2)}, u32[]{:S(2)}) collective-permute-start(f32[2,2,4,128]{3,2,1,0:T(4,128)S(1)} %get-tuple-element.10), channel_id=1, source_target_pairs={{8,0},{16,8},{24,16},{32,24},{40,32},{48,40},{56,48},{64,56},{72,6... | collective-permute-start | bytes 24584 | tf_op jit(solution)/shard_map/ppermute | solution.py:66
  156.0 6.6 %collective-permute-done.9 = f32[2,2,4,128]{3,2,1,0:T(4,128)S(1)} collective-permute-done((f32[2,2,4,128]{3,2,1,0:T(4,128)S(1)}, f32[2,2,4,128]{3,2,1,0:T(4,128)S(1)}, u32[]{:S(2)}, u32[]{:S(2)}) %collective-permute-start.9) | collective-permute-done | bytes 8224 | tf_op jit(solution)/shard_map/ppermute | solution.py:66
  162.6 1.9 %collective-permute-start.10 = (f32[2,8,2,128]{3,2,1,0:T(2,128)S(1)}, f32[2,8,2,128]{3,2,1,0:T(2,128)S(1)}, u32[]{:S(2)}, u32[]{:S(2)}) collective-permute-start(f32[2,8,2,128]{3,2,1,0:T(2,128)S(1)} %get-tuple-element.5), channel_id=1, source_target_pairs={{0,1},{1,2},{2,3},{3,4},{4,5},{5,6},{6,7},{8,9},{9,10},{10,11},{11... | collective-permute-start | bytes 49160 | tf_op jit(solution)/shard_map/ppermute | solution.py:64
  164.6 3.4 %collective-permute-start.11 = (f32[2,8,2,128]{3,2,1,0:T(2,128)S(1)}, f32[2,8,2,128]{3,2,1,0:T(2,128)S(1)}, u32[]{:S(2)}, u32[]{:S(2)}) collective-permute-start(f32[2,8,2,128]{3,2,1,0:T(2,128)S(1)} %get-tuple-element.6), channel_id=1, source_target_pairs={{1,0},{2,1},{3,2},{4,3},{5,4},{6,5},{7,6},{9,8},{10,9},{11,10},{12... | collective-permute-start | bytes 49160 | tf_op jit(solution)/shard_map/ppermute | solution.py:66
  167.9 3.2 %collective-permute-done.11 = f32[2,8,2,128]{3,2,1,0:T(2,128)S(1)} collective-permute-done((f32[2,8,2,128]{3,2,1,0:T(2,128)S(1)}, f32[2,8,2,128]{3,2,1,0:T(2,128)S(1)}, u32[]{:S(2)}, u32[]{:S(2)}) %collective-permute-start.11) | collective-permute-done | bytes 16416 | tf_op jit(solution)/shard_map/ppermute | solution.py:66
  171.2 0.1 fusion.22
  171.3 0.7 fusion.37
  (50 shorter events, 0.4 us)
Async XLA Ops:
  0.0 51.2 %copy-start = (bf16[1,1,32,8,4096]{4,3,2,1,0:T(8,128)(2,1)S(1)}, bf16[1,1,32,8,4096]{4,3,2,1,0:T(8,128)(2,1)}, u32[]{:S(2)}) copy-start(bf16[1,1,32,8,4096]{4,3,2,1,0:T(8,128)(2,1)} %param.9) | copy-start | bytes 6291460
  1.6 29.0 %all-to-all-start.1 = ((bf16[16,2,1,2048]{3,1,2,0:T(2,128)(2,1)}), bf16[16,2,1,2048]{3,1,2,0:T(2,128)(2,1)S(1)}, u32[]{:S(2)}, u32[]{:S(2)}) async-start(bf16[16,2,1,2048]{3,1,2,0:T(2,128)(2,1)} %broadcast_in_dim.24), calls=%async_computation.1 | async-start | bytes 262144 | tf_op jit(solution)/shard_map/all_to_all | solution.py:18
  9.7 20.9 %collective-permute-start = (f32[1,4,128]{2,1,0:T(4,128)S(1)}, f32[1,4,128]{2,1,0:T(4,128)S(1)}, u32[]{:S(2)}, u32[]{:S(2)}) collective-permute-start(f32[1,4,128]{2,1,0:T(4,128)S(1)} %get-tuple-element.18), channel_id=1, source_target_pairs={{0,8},{8,16},{16,24},{24,32},{32,40},{40,48},{48,56},{56,64},{64,7... | collective-permute-start | bytes 6152 | tf_op jit(solution)/shard_map/ppermute | solution.py:64
  14.6 43.4 %collective-permute-start.1 = (f32[1,4,128]{2,1,0:T(4,128)S(1)}, f32[1,4,128]{2,1,0:T(4,128)S(1)}, u32[]{:S(2)}, u32[]{:S(2)}) collective-permute-start(f32[1,4,128]{2,1,0:T(4,128)S(1)} %get-tuple-element.17), channel_id=1, source_target_pairs={{8,0},{16,8},{24,16},{32,24},{40,32},{48,40},{56,48},{64,56},{72,6... | collective-permute-start | bytes 6152 | tf_op jit(solution)/shard_map/ppermute | solution.py:66
  17.6 1.0 copy-start.2
  18.6 1.6 copy-start.3
  18.6 1.7 copy-start.4
  18.6 2.3 %copy-start.5 = (s32[1,1,32]{2,1,0:T(1,128)S(1)}, s32[1,1,32]{2,1,0:T(1,128)}, u32[]{:S(2)}) copy-start(s32[1,1,32]{2,1,0:T(1,128)} %param.11) | copy-start | bytes 388
  30.6 22.2 %all-to-all-start = ((s32[128,1,1,32]{3,2,1,0:T(1,128)}), s32[128,1,1,32]{3,2,1,0:T(1,128)S(1)}, u32[]{:S(2)}, u32[]{:S(2)}) async-start(s32[128,1,1,32]{3,2,1,0:T(1,128)} %bitcast.10), calls=%async_computation | async-start | bytes 131072 | tf_op jit(solution)/shard_map/all_to_all | solution.py:51
  51.2 6.8 %copy-start.1 = (f32[4,4,128]{2,1,0:T(4,128)S(1)}, f32[4,4,128]{2,1,0:T(4,128)}, u32[]{:S(2)}) copy-start(f32[4,4,128]{2,1,0:T(4,128)} %param.15) | copy-start | bytes 24580
  52.8 9.1 %all-to-all-start.2 = ((f32[8,2,2048]{2,1,0:T(2,128)}), f32[8,2,2048]{2,1,0:T(2,128)S(1)}, u32[]{:S(2)}, u32[]{:S(2)}) async-start(f32[8,2,2048]{2,1,0:T(2,128)} %copy.52), calls=%async_computation.2 | async-start | bytes 262144 | tf_op jit(solution)/shard_map/all_to_all | solution.py:41
  72.4 16.2 %all-to-all-start.3 = ((f32[128,2,1,32]{3,1,2,0:T(2,128)}), f32[128,2,1,32]{3,1,2,0:T(2,128)S(1)}, u32[]{:S(2)}, u32[]{:S(2)}) async-start(f32[128,2,1,32]{3,1,2,0:T(2,128)} %bitcast.44), calls=%async_computation.3 | async-start | bytes 262144 | tf_op jit(solution)/shard_map/all_to_all | solution.py:51
  118.9 12.9 %collective-permute-start.4 = (f32[2,2,4,128]{3,2,1,0:T(4,128)S(1)}, f32[2,2,4,128]{3,2,1,0:T(4,128)S(1)}, u32[]{:S(2)}, u32[]{:S(2)}) collective-permute-start(f32[2,2,4,128]{3,2,1,0:T(4,128)S(1)} %get-tuple-element.11), channel_id=1, source_target_pairs={{0,8},{8,16},{16,24},{24,32},{32,40},{40,48},{48,56},{56,64},{64,7... | collective-permute-start | bytes 24584 | tf_op jit(solution)/shard_map/ppermute | solution.py:64
  124.1 8.6 %collective-permute-start.5 = (f32[2,2,4,128]{3,2,1,0:T(4,128)S(1)}, f32[2,2,4,128]{3,2,1,0:T(4,128)S(1)}, u32[]{:S(2)}, u32[]{:S(2)}) collective-permute-start(f32[2,2,4,128]{3,2,1,0:T(4,128)S(1)} %get-tuple-element.12), channel_id=1, source_target_pairs={{8,0},{16,8},{24,16},{32,24},{40,32},{48,40},{56,48},{64,56},{72,6... | collective-permute-start | bytes 24584 | tf_op jit(solution)/shard_map/ppermute | solution.py:66
  126.0 13.2 %collective-permute-start.2 = (f32[6,1,128]{2,1,0:T(1,128)S(1)}, f32[6,1,128]{2,1,0:T(1,128)S(1)}, u32[]{:S(2)}, u32[]{:S(2)}) collective-permute-start(f32[6,1,128]{2,1,0:T(1,128)S(1)} %get-tuple-element.13), channel_id=1, source_target_pairs={{0,1},{1,2},{2,3},{3,4},{4,5},{5,6},{6,7},{8,9},{9,10},{10,11},{11... | collective-permute-start | bytes 9224 | tf_op jit(solution)/shard_map/ppermute | solution.py:64
  129.8 9.4 %collective-permute-start.3 = (f32[6,1,128]{2,1,0:T(1,128)S(1)}, f32[6,1,128]{2,1,0:T(1,128)S(1)}, u32[]{:S(2)}, u32[]{:S(2)}) collective-permute-start(f32[6,1,128]{2,1,0:T(1,128)S(1)} %get-tuple-element.14), channel_id=1, source_target_pairs={{1,0},{2,1},{3,2},{4,3},{5,4},{6,5},{7,6},{9,8},{10,9},{11,10},{12... | collective-permute-start | bytes 9224 | tf_op jit(solution)/shard_map/ppermute | solution.py:66
  132.7 6.6 %collective-permute-start.6 = (f32[2,8,2,128]{3,2,1,0:T(2,128)S(1)}, f32[2,8,2,128]{3,2,1,0:T(2,128)S(1)}, u32[]{:S(2)}, u32[]{:S(2)}) collective-permute-start(f32[2,8,2,128]{3,2,1,0:T(2,128)S(1)} %get-tuple-element.7), channel_id=1, source_target_pairs={{0,1},{1,2},{2,3},{3,4},{4,5},{5,6},{6,7},{8,9},{9,10},{10,11},{11... | collective-permute-start | bytes 49160 | tf_op jit(solution)/shard_map/ppermute | solution.py:64
  137.3 7.0 %collective-permute-start.7 = (f32[2,8,2,128]{3,2,1,0:T(2,128)S(1)}, f32[2,8,2,128]{3,2,1,0:T(2,128)S(1)}, u32[]{:S(2)}, u32[]{:S(2)}) collective-permute-start(f32[2,8,2,128]{3,2,1,0:T(2,128)S(1)} %get-tuple-element.8), channel_id=1, source_target_pairs={{1,0},{2,1},{3,2},{4,3},{5,4},{6,5},{7,6},{9,8},{10,9},{11,10},{12... | collective-permute-start | bytes 49160 | tf_op jit(solution)/shard_map/ppermute | solution.py:66
  144.6 11.3 %collective-permute-start.8 = (f32[2,2,4,128]{3,2,1,0:T(4,128)S(1)}, f32[2,2,4,128]{3,2,1,0:T(4,128)S(1)}, u32[]{:S(2)}, u32[]{:S(2)}) collective-permute-start(f32[2,2,4,128]{3,2,1,0:T(4,128)S(1)} %get-tuple-element.9), channel_id=1, source_target_pairs={{0,8},{8,16},{16,24},{24,32},{32,40},{40,48},{48,56},{56,64},{64,7... | collective-permute-start | bytes 24584 | tf_op jit(solution)/shard_map/ppermute | solution.py:64
  154.0 8.6 %collective-permute-start.9 = (f32[2,2,4,128]{3,2,1,0:T(4,128)S(1)}, f32[2,2,4,128]{3,2,1,0:T(4,128)S(1)}, u32[]{:S(2)}, u32[]{:S(2)}) collective-permute-start(f32[2,2,4,128]{3,2,1,0:T(4,128)S(1)} %get-tuple-element.10), channel_id=1, source_target_pairs={{8,0},{16,8},{24,16},{32,24},{40,32},{48,40},{56,48},{64,56},{72,6... | collective-permute-start | bytes 24584 | tf_op jit(solution)/shard_map/ppermute | solution.py:66
  162.6 5.3 %collective-permute-start.10 = (f32[2,8,2,128]{3,2,1,0:T(2,128)S(1)}, f32[2,8,2,128]{3,2,1,0:T(2,128)S(1)}, u32[]{:S(2)}, u32[]{:S(2)}) collective-permute-start(f32[2,8,2,128]{3,2,1,0:T(2,128)S(1)} %get-tuple-element.5), channel_id=1, source_target_pairs={{0,1},{1,2},{2,3},{3,4},{4,5},{5,6},{6,7},{8,9},{9,10},{10,11},{11... | collective-permute-start | bytes 49160 | tf_op jit(solution)/shard_map/ppermute | solution.py:64
  164.6 6.6 %collective-permute-start.11 = (f32[2,8,2,128]{3,2,1,0:T(2,128)S(1)}, f32[2,8,2,128]{3,2,1,0:T(2,128)S(1)}, u32[]{:S(2)}, u32[]{:S(2)}) collective-permute-start(f32[2,8,2,128]{3,2,1,0:T(2,128)S(1)} %get-tuple-element.6), channel_id=1, source_target_pairs={{1,0},{2,1},{3,2},{4,3},{5,4},{6,5},{7,6},{9,8},{10,9},{11,10},{12... | collective-permute-start | bytes 49160 | tf_op jit(solution)/shard_map/ppermute | solution.py:66
where the time goes:
time: 173 us; the launch traced here: 172 us
  starting transfers between devices  75.8 us (44%)
  other arithmetic  30.2 us (17%)
  local copies, waits for them, and re-layouts  29.7 us (17%)
  waiting for transfers between devices  25.2 us (15%)
  matrix products  10.6 us (6%)
    ppermute x6, starting transfers between devices, extended(): lax.ppermute(tail, axis, [(i, (i + 1) % count) for i in range(ends)])  29.8 us
    scatter-add x1, other arithmetic, per_device(): jnp.zeros((NVEC, points + 1), jnp.float32).at[:, received_places[0]]  25.5 us
    all_to_all x2, starting transfers between devices, one_exchange(): lax.all_to_all(blocks, axis, split_axis=0, concat_axis=0, tiled=True)  20.4 us
    ppermute x6, waiting for transfers between devices, extended(): lax.ppermute(head, axis, [((i + 1) % count, i) for i in range(ends)])  15.8 us
    ppermute x6, starting transfers between devices, extended(): lax.ppermute(head, axis, [((i + 1) % count, i) for i in range(ends)])  13 us
    unnamed x15, local copies, waits for them, and re-layouts  8.6 us
    all_to_all x1, starting transfers between devices, copy_for_each(): lax.all_to_all(jnp.broadcast_to(array[None], (size, *array.shape)), axis,...  7.47 us
    scatter x1, local copies, waits for them, and re-layouts, route(): jnp.zeros((values.shape[0], buffer_len), jnp.float32).at[:, buffer_at]  7.02 us
  transfers between devices with their start and end apart: 16, of which 6 were waited for; matrix products, arithmetic and copies ran while one was open for 16% of the time, Pallas kernels for 0%

commit v1 on v0

v1 whole, which is shorter than its diff:
```python
import jax
import jax.numpy as jnp
from jax import lax
from jax.experimental import pallas as pl
from jax.experimental.pallas import tpu as pltpu
from jax.sharding import PartitionSpec as P

NVEC = 2
CX = 4
CY = 4
NZ = 128
TILE_ROWS = 4
TILE_COLS = 8
KMAX = 8
LEAF = 512
NLEAF = 8
PTS = 2048
ROWS = 16
COLS = 8
TS = 4096
CAP = 32
DEV = ROWS * COLS
SLAB = 16
F32 = jnp.float32
BF16 = jnp.bfloat16
NT = (((1,), (1,)), ((), ()))
MIB = 1 << 20


def iota(shape, dim):
    return lax.broadcasted_iota(jnp.int32, shape, dim)


def rank_kernel(perm_ref, rank_ref, place_ref):
    chunk = 256
    upto = jnp.where(iota((chunk, chunk), 0) <= iota((chunk, chunk), 1), 1.0, 0.0).astype(BF16)
    brick = iota((DEV, chunk), 0)
    carry = jnp.zeros((COLS * DEV, 1), F32)
    for j in range(PTS // chunk):
        masks = [
            (perm_ref[0:1, k * PTS + j * chunk : k * PTS + (j + 1) * chunk] >> 11) == brick
            for k in range(COLS)
        ]
        hot = jnp.concatenate([jnp.where(m, 1.0, 0.0).astype(BF16) for m in masks], axis=0)
        count = jnp.dot(hot, upto, preferred_element_type=F32)
        total = count + carry
        for k in range(COLS):
            at = jnp.where(masks[k], total[k * DEV : (k + 1) * DEV], 0.0)
            rank_ref[0:1, k * PTS + j * chunk : k * PTS + (j + 1) * chunk] = (
                jnp.sum(at, axis=0, keepdims=True) - 1.0
            ).astype(jnp.int32)
        carry = total[:, chunk - 1 : chunk]
    col = lax.axis_index("col")
    start = pl.multiple_of(col * PTS, PTS)
    own = perm_ref[0:1, pl.ds(start, PTS)]
    slot = rank_ref[0:1, pl.ds(start, PTS)] + (col % 4) * CAP
    inside = own & (PTS - 1)
    code = ((NZ + (inside & (NZ - 1))) << (inside >> 7)).astype(F32)
    spread = jnp.where(slot == iota((128, PTS), 0), code, 0.0).astype(BF16)
    hot = jnp.where((own >> 11) == iota((DEV, PTS), 0), 1.0, 0.0).astype(BF16)
    place_ref[...] = lax.dot_general(hot, spread, NT, preferred_element_type=F32)


def send_kernel(
    leaf_at,
    x_ref,
    tile_rank_ref,
    perm_ref,
    rank_ref,
    place_ref,
    right_hbm,
    left_hbm,
    leaf_hbm,
    out_ref,
    right,
    left,
    leaves,
    x_rows,
    sums,
    stage,
    sems,
):
    copies = [
        pltpu.make_async_copy(right_hbm, right, sems.at[0]),
        pltpu.make_async_copy(left_hbm, left, sems.at[1]),
        pltpu.make_async_copy(leaf_hbm, leaves, sems.at[2]),
    ]
    for copy in copies:
        copy.start()
    half = TS // PTS
    for s in range(ROWS):
        b, h = divmod(s, half)
        block = x_ref[s].astype(F32)
        x_rows[b : b + 1, h * PTS : (h + 1) * PTS] = block[0:1]
        x_rows[8 + b : 9 + b, h * PTS : (h + 1) * PTS] = block[1:2]
    terms = TILE_ROWS * TILE_COLS * KMAX
    lane = iota((16, terms), 1)
    sub = iota((16, terms), 0)
    widen = jnp.where(
        iota((TILE_ROWS * TILE_COLS, terms), 1) // KMAX
        == iota((TILE_ROWS * TILE_COLS, terms), 0),
        1.0,
        0.0,
    ).astype(BF16)
    ranks = jnp.broadcast_to(tile_rank_ref[...].astype(F32), (16, TILE_ROWS * TILE_COLS))
    rank_lane = jnp.dot(ranks.astype(BF16), widen, preferred_element_type=F32)
    keep = (sub % 8 == (lane // KMAX) % TILE_COLS) & ((lane % KMAX).astype(F32) < rank_lane)
    x_all = x_rows[...].astype(BF16)
    copies[0].wait()
    projected = lax.dot_general(x_all, right[...], NT, preferred_element_type=F32)
    projected = jnp.where(keep, projected, 0.0)
    first = jnp.sum(projected[0:8], axis=0, keepdims=True)
    second = jnp.sum(projected[8:16], axis=0, keepdims=True)
    by_row = jnp.where(sub < 8, first, second)
    by_row = jnp.where(sub % 8 == lane // (TILE_COLS * KMAX), by_row, 0.0).astype(BF16)
    copies[1].wait()
    sums[...] = jnp.dot(by_row, left[...], preferred_element_type=F32)
    copies[2].wait()
    per_tile = TS // LEAF
    for l in range(NLEAF):
        i, j = leaf_at[l, 0], leaf_at[l, 1]
        from_lane = pl.multiple_of((j % per_tile) * LEAF, LEAF)
        to_lane = pl.multiple_of((i % per_tile) * LEAF, LEAF)
        picked = jnp.concatenate(
            [x_rows[pl.ds(8 * v + j // per_tile, 1), pl.ds(from_lane, LEAF)] for v in range(NVEC)],
            axis=0,
        ).astype(BF16)
        near = lax.dot_general(picked, leaves[l], NT, preferred_element_type=F32)
        for v in range(NVEC):
            at = (pl.ds(8 * v + i // per_tile, 1), pl.ds(to_lane, LEAF))
            sums[at] = sums[at] + near[v : v + 1]
    row = iota((DEV, 128), 0) % COLS

    def put(values, first_row, step):
        below = jnp.where(row != 0, pltpu.roll(values, 1, 0), 0.0)
        above = jnp.where(row != COLS - 1, pltpu.roll(values, DEV - 1, 0), 0.0)
        for j, v in enumerate((below, values, above)):
            stage[pl.ds(first_row + j * step, DEV, stride=SLAB), :] = v

    put(place_ref[...], 12, 1)
    stage[pl.ds(15, DEV, stride=SLAB), :] = jnp.zeros((DEV, 128), F32)
    brick = iota((DEV, PTS), 0)
    slots = iota((CAP, PTS), 0)
    for group in range(2):
        parts = []
        for kk in range(4):
            k = group * 4 + kk
            a, h = divmod(k, half)
            at = slice(k * PTS, (k + 1) * PTS)
            hot = jnp.where((perm_ref[0:1, at] >> 11) == brick, 1.0, 0.0).astype(BF16)
            mask = rank_ref[0:1, at] == slots
            spread = jnp.concatenate(
                [
                    jnp.where(mask, sums[8 * v + a : 8 * v + a + 1, h * PTS : (h + 1) * PTS], 0.0)
                    for v in range(NVEC)
                ],
                axis=0,
            ).astype(BF16)
            parts.append(lax.dot_general(hot, spread, NT, preferred_element_type=F32))
        for v in range(NVEC):
            put(
                jnp.concatenate([p[:, v * CAP : (v + 1) * CAP] for p in parts], axis=1),
                group * 2 + v,
                4,
            )
    out_ref[...] = stage[...].astype(BF16)


def receive_kernel(got_ref, field_ref, first, second, values, where, hots):
    for r in range(ROWS):
        base = r * COLS * SLAB
        halves = []
        for g in range(2):
            total = got_ref[base + g * 64 : base + g * 64 + SLAB, :].astype(F32)
            for c in range(1, 4):
                at = base + g * 64 + c * SLAB
                total = total + got_ref[at : at + SLAB, :].astype(F32)
            halves.append(total)
        first[r * SLAB : (r + 1) * SLAB, :] = halves[0]
        second[r * SLAB : (r + 1) * SLAB, :] = halves[1]
    code_a, code_b = first[...], second[...]
    for code, ref in ((code_a, first), (code_b, second)):
        cell = jnp.zeros_like(code)
        for bits in (8, 4, 2, 1):
            big = code >= float(NZ << bits)
            code = jnp.where(big, code * (0.5**bits), code)
            cell = jnp.where(big, cell + float(bits), cell)
        cell = jnp.where(code > 0.0, cell, -1.0)
        ref[...] = code - float(NZ)
        where[0 if ref is first else 1] = cell
    total = code_a + code_b
    total_ref = values.at[0]
    total_ref[...] = total
    sub = iota((8, 128), 0)
    z_row = iota((NZ, 128), 0).astype(F32)
    for j in range(3):
        for r in range(ROWS):
            for g in range(2):
                lanes = slice((r * 2 + g) * 128, (r * 2 + g + 1) * 128)
                at = r * SLAB + j * 4 + g * 2
                pair = jnp.where(sub < 4, total_ref[at : at + 1, :], total_ref[at + 1 : at + 2, :])
                high = pair.astype(BF16).astype(F32)
                low = pair - high
                p = r * SLAB + 12 + j
                cell = where[g, p : p + 1, :]
                z_at = (first if g == 0 else second)[p : p + 1, :]
                wanted = [cell == ((sub % 4) * CY + y).astype(F32) for y in range(CY)]
                rows = jnp.concatenate(
                    [jnp.where(w, part, 0.0) for part in (high, low) for w in wanted], axis=0
                )
                values_at = hots.at[0]
                values_at[0:64, lanes] = rows.astype(BF16)
                hots[1, :, lanes] = jnp.where(z_at == z_row, 1.0, 0.0).astype(BF16)
        both = lax.dot_general(hots[0, 0:64, :], hots[1], NT, preferred_element_type=F32)
        field_ref[j * 32 : (j + 1) * 32, :] = both[0:32] + both[32:64]


def prior_kernel(field_ref, before_ref, after_ref, kappa_ref, kappa_before, kappa_after, out_ref):
    my_row, my_col = lax.axis_index("row"), lax.axis_index("col")
    wide = 3 * CY
    inside_x = [
        jnp.where(my_row > 0, 1.0, 0.0),
        jnp.float32(1.0),
        jnp.where(my_row < ROWS - 1, 1.0, 0.0),
    ]
    inside_y = [
        jnp.where(my_col > 0, 1.0, 0.0),
        jnp.float32(1.0),
        jnp.where(my_col < COLS - 1, 1.0, 0.0),
    ]
    x_at = iota((8, NZ), 0) % CX
    z_at = iota((8, NZ), 1)
    us = [[ref[y] for y in range(wide)] for ref in (before_ref, field_ref, after_ref)]
    ks = [kappa_before, kappa_ref, kappa_after]
    for step in range(1, 5):
        new = [[None] * wide for _ in range(3)]
        up = [[None if u is None else pltpu.roll(u, 1, 0) for u in us[x]] for x in range(3)]
        down = [[None if u is None else pltpu.roll(u, 7, 0) for u in us[x]] for x in range(3)]
        up4 = [[None if u is None else pltpu.roll(u, 5, 0) for u in us[x]] for x in range(3)]
        down4 = [[None if u is None else pltpu.roll(u, 3, 0) for u in us[x]] for x in range(3)]
        for x in range(3):
            if step == 4 and x != 1:
                continue
            for y in range(step, wide - step):
                u = us[x][y]
                lower = up4[x - 1][y] if x > 0 else jnp.zeros_like(u)
                upper = down4[x + 1][y] if x < 2 else jnp.zeros_like(u)
                beside = us[x][y - 1] + us[x][y + 1]
                beside = beside + jnp.where(x_at == 0, lower, up[x][y])
                beside = beside + jnp.where(x_at == CX - 1, upper, down[x][y])
                beside = beside + jnp.where(z_at == 0, 0.0, pltpu.roll(u, 1, 1))
                beside = beside + jnp.where(z_at == NZ - 1, 0.0, pltpu.roll(u, NZ - 1, 1))
                result = ((6.0 + ks[x][y]) * u - beside) * 0.125
                if step < 4:
                    if x != 1 and y // CY != 1:
                        result = result * (inside_x[x] * inside_y[y // CY])
                    elif x != 1:
                        result = result * inside_x[x]
                    elif y // CY != 1:
                        result = result * inside_y[y // CY]
                new[x][y] = result
        us = new
    for y in range(CY):
        out_ref[y] = us[1][CY + y]


def to_both_sides(array, axis):
    size = lax.axis_size(axis)
    before = lax.ppermute(array, axis, [(i, i + 1) for i in range(size - 1)])
    after = lax.ppermute(array, axis, [(i + 1, i) for i in range(size - 1)])
    return before, after


def cost(flops, size):
    return pl.CostEstimate(flops=flops, bytes_accessed=size, transcendentals=0)


def per_device(
    vectors, lr_left, lr_right, tile_rank, leaf_values, leaf_places, cluster_perm, kappa
):
    vmem = pl.BlockSpec(memory_space=pltpu.VMEM)
    smem = pl.BlockSpec(memory_space=pltpu.SMEM)
    anywhere = pl.BlockSpec(memory_space=pl.ANY)
    points = ROWS // 2 * PTS
    x_all = lax.all_to_all(
        jnp.broadcast_to(vectors[:, 0][None], (ROWS, NVEC, PTS)), "row", 0, 0, tiled=True
    )
    rank, place = pl.pallas_call(
        rank_kernel,
        out_shape=(
            jax.ShapeDtypeStruct((1, points), jnp.int32),
            jax.ShapeDtypeStruct((DEV, 128), F32),
        ),
        in_specs=[vmem],
        out_specs=(vmem, vmem),
        compiler_params=pltpu.CompilerParams(vmem_limit_bytes=24 * MIB),
        cost_estimate=cost(1 << 31, 1 << 20),
        name="slots",
    )(cluster_perm)
    kappa_own = jnp.transpose(kappa, (1, 0, 2))
    kappa_own = jnp.concatenate([kappa_own, kappa_own], axis=1)
    low, high = to_both_sides(kappa_own, "col")
    kappa_own = jnp.concatenate([low, kappa_own, high], axis=0)
    kappa_before, kappa_after = to_both_sides(kappa_own, "row")
    terms = TILE_ROWS * TILE_COLS * KMAX
    send = pl.pallas_call(
        send_kernel,
        out_shape=jax.ShapeDtypeStruct((DEV * SLAB, 128), BF16),
        in_specs=[smem, vmem, vmem, vmem, vmem, vmem, anywhere, anywhere, anywhere],
        out_specs=vmem,
        scratch_shapes=[
            pltpu.VMEM((terms, TS), BF16),
            pltpu.VMEM((terms, TS), BF16),
            pltpu.VMEM((NLEAF, LEAF, LEAF), BF16),
            pltpu.VMEM((16, TS), F32),
            pltpu.VMEM((16, TS), F32),
            pltpu.VMEM((DEV * SLAB, 128), F32),
            pltpu.SemaphoreType.DMA((3,)),
        ],
        compiler_params=pltpu.CompilerParams(vmem_limit_bytes=32 * MIB),
        cost_estimate=cost(1 << 31, 8 << 20),
        name="partial_sums",
    )(
        leaf_places[0, 0],
        x_all,
        tile_rank[0],
        cluster_perm,
        rank,
        place,
        lr_right.reshape(terms, TS),
        lr_left.reshape(terms, TS),
        leaf_values[0, 0],
    )
    got = lax.all_to_all(send.reshape(DEV, SLAB, 128), ("row", "col"), 0, 0, tiled=True)
    field = pl.pallas_call(
        receive_kernel,
        out_shape=jax.ShapeDtypeStruct((3 * CY * NVEC * CX, NZ), F32),
        in_specs=[vmem],
        out_specs=vmem,
        scratch_shapes=[
            pltpu.VMEM((ROWS * SLAB, 128), F32),
            pltpu.VMEM((ROWS * SLAB, 128), F32),
            pltpu.VMEM((1, ROWS * SLAB, 128), F32),
            pltpu.VMEM((2, ROWS * SLAB, 128), F32),
            pltpu.VMEM((2, NZ, 4096), BF16),
        ],
        compiler_params=pltpu.CompilerParams(vmem_limit_bytes=24 * MIB),
        cost_estimate=cost(1 << 30, 1 << 20),
        name="bricks",
    )(got.reshape(DEV * SLAB, 128))
    field = field.reshape(3 * CY, NVEC * CX, NZ)
    before, after = to_both_sides(field, "row")
    out = pl.pallas_call(
        prior_kernel,
        out_shape=jax.ShapeDtypeStruct((CY, NVEC * CX, NZ), F32),
        in_specs=[vmem] * 6,
        out_specs=vmem,
        cost_estimate=cost(1 << 24, 1 << 20),
        name="prior",
    )(field, before, after, kappa_own, kappa_before, kappa_after)
    return jnp.transpose(out.reshape(CY, NVEC, CX, NZ), (1, 2, 0, 3))


def solution(mesh):
    in_specs = (
        P(None, "col", "row"),
        P("row", "col", None, None, None),
        P("row", "col", None, None, None),
        P("row", "col", None),
        P("row", "col", None, None, None),
        P("row", "col", None, None),
        P("row", None),
        P("row", "col", None),
    )
    out_specs = P(None, "row", "col", None)
    return jax.shard_map(
        per_device, mesh=mesh, in_specs=in_specs, out_specs=out_specs, check_vma=False
    )
```

time: 173 us -> 74.9 us (0.43)
  the two profiles are of different devices: /device:TPU:103 before, /device:TPU:105 now
where the time goes in v1:
time: 74.9 us; the launch traced here: 74.2 us
  starting transfers between devices  37.9 us (51%)
  Pallas kernels  13.9 us (19%)
  waiting for transfers between devices  13.5 us (18%)
  local copies, waits for them, and re-layouts  8.75 us (12%)
    ppermute x3, starting transfers between devices, to_both_sides(): before = lax.ppermute(array, axis, [(i, i + 1) for i in range(size - 1)])  14.2 us
    all_to_all x1, starting transfers between devices, per_device(): lax.all_to_all(send.reshape(DEV, SLAB, 128), ('row', 'col'), 0, 0, tiled=...  9.06 us
    ppermute x3, starting transfers between devices, to_both_sides(): after = lax.ppermute(array, axis, [(i + 1, i) for i in range(size - 1)])  8.13 us
    ppermute x3, waiting for transfers between devices, to_both_sides(): after = lax.ppermute(array, axis, [(i + 1, i) for i in range(size - 1)])  8.05 us
    pallas_call x1, Pallas kernels, per_device(): pl.pallas_call(send_kernel, out_shape=jax.ShapeDtypeStruct((DEV * SLAB, 1...  7.22 us
    all_to_all x1, starting transfers between devices, per_device(): lax.all_to_all(jnp.broadcast_to(vectors[:, 0][None], (ROWS, NVEC, PTS)),...  6.57 us
    unnamed x27, local copies, waits for them, and re-layouts  5.25 us
    ppermute x3, waiting for transfers between devices, to_both_sides(): before = lax.ppermute(array, axis, [(i, i + 1) for i in range(size - 1)])  3.65 us
  transfers between devices with their start and end apart: 8, of which 4 were waited for; matrix products, arithmetic and copies ran while one was open for 1% of the time, Pallas kernels for 7%

profile of v1, /device:TPU:105, one launch (start us, length us, event | category | flops | bytes accessed | tf_op | source)
XLA Modules:
  0.0 74.2 jit_solution(2708654360616091348)
XLA Ops:
  0.0 1.4 %broadcast_in_dim.8 = bf16[16,2,2048]{2,1,0:T(2,128)(2,1)} broadcast(bf16[2,2048]{1,0:T(2,128)(2,1)} %bitcast.27), dimensions={1,2} | broadcast | bytes 139264 | tf_op jit(solution)/shard_map/broadcast_in_dim | solution.py:286
  1.4 6.6 %all-to-all-start = ((bf16[16,2,2048]{2,1,0:T(2,128)(2,1)}), bf16[16,2,2048]{2,1,0:T(2,128)(2,1)S(1)}, u32[]{:S(2)}, u32[]{:S(2)}) async-start(bf16[16,2,2048]{2,1,0:T(2,128)(2,1)} %broadcast_in_dim.8), calls=%async_computation | async-start | bytes 262144 | tf_op jit(solution)/shard_map/all_to_all | solution.py:285
  8.0 0.8 %copy.9.leaf_at = s32[8,2]{1,0:T(8,128)S(1)} copy(s32[8,2]{0,1:T(2,128)} %bitcast.28) | data formatting | bytes 128 | tf_op jit(solution)/shard_map/squeeze | solution.py:324
  8.7 0.0 copy-start.3
  8.7 0.8 %copy-done.3 = s32[1,16384]{1,0:T(1,128)S(1)} copy-done((s32[1,16384]{1,0:T(1,128)S(1)}, s32[1,16384]{1,0:T(1,128)}, u32[]{:S(2)}) %copy-start.3) | copy-done | bytes 65560
  9.6 0.0 copy-start.1
  9.6 0.0 copy-start.4
  9.6 0.0 copy-start.6
  9.6 2.8 %slots.1 = (s32[1,16384]{1,0:T(1,128)S(1)}, f32[128,128]{1,0:T(8,128)S(1)}) custom-call(s32[1,16384]{1,0:T(1,128)S(1)} %copy-done.3), custom_call_target="tpu_custom_call" | custom-call | flops 2147483648 | bytes 1048576 | tf_op jit(solution)/shard_map/slots/pallas_call | solution.py:288
  12.4 1.8 %all-to-all-done.x_ref = bf16[16,2,2048]{2,1,0:T(2,128)(2,1)S(1)} async-done(((bf16[16,2,2048]{2,1,0:T(2,128)(2,1)}), bf16[16,2,2048]{2,1,0:T(2,128)(2,1)S(1)}, u32[]{:S(2)}, u32[]{:S(2)}) %all-to-all-start) | async-done | bytes 131104 | tf_op jit(solution)/shard_map/all_to_all | solution.py:285
  14.1 0.0 copy-done.1
  14.1 0.0 copy-done.4
  14.1 0.0 copy-done.6
  14.1 0.0 copy-start
  14.2 2.2 %copy-done = bf16[1,1,8,512,512]{4,3,2,1,0:T(8,128)(2,1)S(1)} copy-done((bf16[1,1,8,512,512]{4,3,2,1,0:T(8,128)(2,1)S(1)}, bf16[1,1,8,512,512]{4,3,2,1,0:T(8,128)(2,1)}, u32[]{:S(2)}) %copy-start) | copy-done | bytes 4194328
  16.3 0.0 copy-start.2
  16.3 1.6 %copy-done.2 = bf16[1,1,32,8,4096]{4,3,2,1,0:T(8,128)(2,1)S(1)} copy-done((bf16[1,1,32,8,4096]{4,3,2,1,0:T(8,128)(2,1)S(1)}, bf16[1,1,32,8,4096]{4,3,2,1,0:T(8,128)(2,1)}, u32[]{:S(2)}) %copy-start.2) | copy-done | bytes 2097176
  17.9 0.0 copy-start.12
  17.9 7.2 %partial_sums.1 = bf16[2048,128]{1,0:T(8,128)(2,1)} custom-call(s32[8,2]{1,0:T(8,128)S(1)} %copy.9.leaf_at, bf16[16,2,2048]{2,1,0:T(2,128)(2,1)S(1)} %all-to-all-done.x_ref, s32[1,32]{1,0:T(1,128)S(1)} %bitcast.23, s32[1,16384]{1,0:T(1,128)S(1)} %copy-done.4, s32[1,16384]{1,0:T(1,128)S(1)} %get-tuple-element.7.rank_ref, ...), custom_call_target="tpu_custom_call" | custom-call | flops 2147483648 | bytes 8388608 | tf_op jit(solution)/shard_map/partial_sums/pallas_call | solution.py:306
  25.2 9.1 %all-to-all-start.1 = ((bf16[128,16,128]{2,1,0:T(8,128)(2,1)}), bf16[128,16,128]{2,1,0:T(8,128)(2,1)S(1)}, u32[]{:S(2)}, u32[]{:S(2)}) async-start(bf16[128,16,128]{2,1,0:T(8,128)(2,1)} %bitcast.6), calls=%async_computation.1 | async-start | bytes 1048576 | tf_op jit(solution)/shard_map/all_to_all | solution.py:334
  34.2 0.0 copy-done.12
  34.3 4.3 %collective-permute-start.3 = (f32[4,8,128]{2,1,0:T(8,128)S(1)}, f32[4,8,128]{2,1,0:T(8,128)S(1)}, u32[]{:S(2)}, u32[]{:S(2)}) collective-permute-start(f32[4,8,128]{2,1,0:T(8,128)S(1)} %pad_maximum_fusion.1), channel_id=1, source_target_pairs={{1,0},{2,1},{3,2},{4,3},{5,4},{6,5},{7,6},{9,8},{10,9},{11,10},{12... | collective-permute-start | bytes 49160 | tf_op jit(solution)/shard_map/ppermute | solution.py:270
  38.6 1.9 %collective-permute-start.2 = (f32[4,8,128]{2,1,0:T(8,128)S(1)}, f32[4,8,128]{2,1,0:T(8,128)S(1)}, u32[]{:S(2)}, u32[]{:S(2)}) collective-permute-start(f32[4,8,128]{2,1,0:T(8,128)S(1)} %pad_maximum_fusion.1), channel_id=1, source_target_pairs={{0,1},{1,2},{2,3},{3,4},{4,5},{5,6},{6,7},{8,9},{9,10},{10,11},{11... | collective-permute-start | bytes 49160 | tf_op jit(solution)/shard_map/ppermute | solution.py:269
  40.5 1.0 %collective-permute-done.3 = f32[4,8,128]{2,1,0:T(8,128)S(1)} collective-permute-done((f32[4,8,128]{2,1,0:T(8,128)S(1)}, f32[4,8,128]{2,1,0:T(8,128)S(1)}, u32[]{:S(2)}, u32[]{:S(2)}) %collective-permute-start.3) | collective-permute-done | bytes 16416 | tf_op jit(solution)/shard_map/ppermute | solution.py:270
  41.5 3.6 %collective-permute-done.2 = f32[4,8,128]{2,1,0:T(8,128)S(1)} collective-permute-done((f32[4,8,128]{2,1,0:T(8,128)S(1)}, f32[4,8,128]{2,1,0:T(8,128)S(1)}, u32[]{:S(2)}, u32[]{:S(2)}) %collective-permute-start.2) | collective-permute-done | bytes 16416 | tf_op jit(solution)/shard_map/ppermute | solution.py:269
  45.2 0.0 copy-start.7
  45.2 5.0 %collective-permute-start.4 = (f32[12,8,128]{2,1,0:T(8,128)S(1)}, f32[12,8,128]{2,1,0:T(8,128)S(1)}, u32[]{:S(2)}, u32[]{:S(2)}) collective-permute-start(f32[12,8,128]{2,1,0:T(8,128)S(1)} %pad_maximum_fusion.kappa_ref), channel_id=1, source_target_pairs={{0,8},{8,16},{16,24},{24,32},{32,40},{40,48},{48,56},{56,64},{64,7... | collective-permute-start | bytes 147464 | tf_op jit(solution)/shard_map/ppermute | solution.py:269
  50.2 1.9 %collective-permute-start.5 = (f32[12,8,128]{2,1,0:T(8,128)S(1)}, f32[12,8,128]{2,1,0:T(8,128)S(1)}, u32[]{:S(2)}, u32[]{:S(2)}) collective-permute-start(f32[12,8,128]{2,1,0:T(8,128)S(1)} %pad_maximum_fusion.kappa_ref), channel_id=1, source_target_pairs={{8,0},{16,8},{24,16},{32,24},{40,32},{48,40},{56,48},{64,56},{72,6... | collective-permute-start | bytes 147464 | tf_op jit(solution)/shard_map/ppermute | solution.py:270
  52.1 0.0 all-to-all-done.1
  52.1 2.0 %bricks.1 = f32[96,128]{1,0:T(8,128)S(1)} custom-call(bf16[2048,128]{1,0:T(8,128)(2,1)S(1)} %bitcast.19), custom_call_target="tpu_custom_call" | custom-call | flops 1073741824 | bytes 1048576 | tf_op jit(solution)/shard_map/bricks/pallas_call | solution.py:335
  54.2 0.0 copy-start.5
  54.2 7.3 %collective-permute-start = (f32[12,8,128]{2,1,0:T(8,128)S(1)}, f32[12,8,128]{2,1,0:T(8,128)S(1)}, u32[]{:S(2)}, u32[]{:S(2)}) collective-permute-start(f32[12,8,128]{2,1,0:T(8,128)S(1)} %bitcast.20), channel_id=1, source_target_pairs={{0,8},{8,16},{16,24},{24,32},{32,40},{40,48},{48,56},{56,64},{64,7... | collective-permute-start | bytes 147464 | tf_op jit(solution)/shard_map/ppermute | solution.py:269
  61.4 1.9 %collective-permute-start.1 = (f32[12,8,128]{2,1,0:T(8,128)S(1)}, f32[12,8,128]{2,1,0:T(8,128)S(1)}, u32[]{:S(2)}, u32[]{:S(2)}) collective-permute-start(f32[12,8,128]{2,1,0:T(8,128)S(1)} %bitcast.21), channel_id=1, source_target_pairs={{8,0},{16,8},{24,16},{32,24},{40,32},{48,40},{56,48},{64,56},{72,6... | collective-permute-start | bytes 147464 | tf_op jit(solution)/shard_map/ppermute | solution.py:270
  63.3 0.0 collective-permute-done.4.kappa_before
  63.4 0.0 copy-start.8
  63.4 0.0 collective-permute-done.5.kappa_after
  63.4 0.0 copy-start.9
  63.4 0.0 collective-permute-done.before_ref
  63.4 0.0 copy-start.10
  63.4 7.0 %collective-permute-done.1.after_ref = f32[12,8,128]{2,1,0:T(8,128)S(1)} collective-permute-done((f32[12,8,128]{2,1,0:T(8,128)S(1)}, f32[12,8,128]{2,1,0:T(8,128)S(1)}, u32[]{:S(2)}, u32[]{:S(2)}) %collective-permute-start.1) | collective-permute-done | bytes 49184 | tf_op jit(solution)/shard_map/ppermute | solution.py:270
  70.4 0.0 copy-done.7
  70.4 0.0 copy-done.5
  70.4 0.0 copy-done.8
  70.5 0.0 copy-done.9
  70.5 0.0 copy-done.10
  70.5 0.0 copy-start.11
  70.5 0.6 copy-done.11
  71.1 1.8 %prior.1 = f32[4,8,128]{2,1,0:T(8,128)} custom-call(f32[12,8,128]{2,1,0:T(8,128)} %bitcast.22, f32[12,8,128]{2,1,0:T(8,128)} %copy-done.10, f32[12,8,128]{2,1,0:T(8,128)} %copy-done.11, f32[12,8,128]{2,1,0:T(8,128)} %copy-done.7, f32[12,8,128]{2,1,0:T(8,128)} %copy-done.8, f32[12,8,128]{2,1,0:T(8,128)} %copy-done.9), custom_call_target="tpu_custom_call" | custom-call | flops 16777216 | bytes 1048576 | tf_op jit(solution)/shard_map/prior/pallas_call | solution.py:353
  72.9 1.3 %copy.14 = f32[4,2,4,128]{3,0,2,1:T(4,128)} copy(f32[4,2,4,128]{3,2,1,0:T(4,128)} %bitcast.26) | data formatting | bytes 32768 | tf_op jit(solution)/shard_map/reshape | solution.py:361
  (3 shorter events, 0.0 us)
Async XLA Ops:
  1.4 12.7 %all-to-all-start = ((bf16[16,2,2048]{2,1,0:T(2,128)(2,1)}), bf16[16,2,2048]{2,1,0:T(2,128)(2,1)S(1)}, u32[]{:S(2)}, u32[]{:S(2)}) async-start(bf16[16,2,2048]{2,1,0:T(2,128)(2,1)} %broadcast_in_dim.8), calls=%async_computation | async-start | bytes 262144 | tf_op jit(solution)/shard_map/all_to_all | solution.py:285
  8.7 0.8 %copy-start.3 = (s32[1,16384]{1,0:T(1,128)S(1)}, s32[1,16384]{1,0:T(1,128)}, u32[]{:S(2)}) copy-start(s32[1,16384]{1,0:T(1,128)} %perm_ref.3) | copy-start | bytes 196612
  9.6 4.6 %copy-start.1 = (bf16[1,1,32,8,4096]{4,3,2,1,0:T(8,128)(2,1)S(1)}, bf16[1,1,32,8,4096]{4,3,2,1,0:T(8,128)(2,1)}, u32[]{:S(2)}) copy-start(bf16[1,1,32,8,4096]{4,3,2,1,0:T(8,128)(2,1)} %param.10) | copy-start | bytes 6291460
  9.6 4.6 %copy-start.4 = (s32[1,16384]{1,0:T(1,128)S(1)}, s32[1,16384]{1,0:T(1,128)}, u32[]{:S(2)}) copy-start(s32[1,16384]{1,0:T(1,128)} %perm_ref.3) | copy-start | bytes 196612
  9.6 4.6 %copy-start.6 = (s32[1,1,32]{2,1,0:T(1,128)S(1)}, s32[1,1,32]{2,1,0:T(1,128)}, u32[]{:S(2)}) copy-start(s32[1,1,32]{2,1,0:T(1,128)} %param.11) | copy-start | bytes 388
  14.1 2.2 %copy-start = (bf16[1,1,8,512,512]{4,3,2,1,0:T(8,128)(2,1)S(1)}, bf16[1,1,8,512,512]{4,3,2,1,0:T(8,128)(2,1)}, u32[]{:S(2)}) copy-start(bf16[1,1,8,512,512]{4,3,2,1,0:T(8,128)(2,1)} %param.12) | copy-start | bytes 12582916
  16.3 1.6 %copy-start.2 = (bf16[1,1,32,8,4096]{4,3,2,1,0:T(8,128)(2,1)S(1)}, bf16[1,1,32,8,4096]{4,3,2,1,0:T(8,128)(2,1)}, u32[]{:S(2)}) copy-start(bf16[1,1,32,8,4096]{4,3,2,1,0:T(8,128)(2,1)} %param.9) | copy-start | bytes 6291460
  17.9 16.3 %copy-start.12 = (f32[4,4,128]{2,1,0:T(4,128)S(1)}, f32[4,4,128]{2,1,0:T(4,128)}, u32[]{:S(2)}) copy-start(f32[4,4,128]{2,1,0:T(4,128)} %param.15) | copy-start | bytes 24580
  25.2 26.9 %all-to-all-start.1 = ((bf16[128,16,128]{2,1,0:T(8,128)(2,1)}), bf16[128,16,128]{2,1,0:T(8,128)(2,1)S(1)}, u32[]{:S(2)}, u32[]{:S(2)}) async-start(bf16[128,16,128]{2,1,0:T(8,128)(2,1)} %bitcast.6), calls=%async_computation.1 | async-start | bytes 1048576 | tf_op jit(solution)/shard_map/all_to_all | solution.py:334
  34.3 7.2 %collective-permute-start.3 = (f32[4,8,128]{2,1,0:T(8,128)S(1)}, f32[4,8,128]{2,1,0:T(8,128)S(1)}, u32[]{:S(2)}, u32[]{:S(2)}) collective-permute-start(f32[4,8,128]{2,1,0:T(8,128)S(1)} %pad_maximum_fusion.1), channel_id=1, source_target_pairs={{1,0},{2,1},{3,2},{4,3},{5,4},{6,5},{7,6},{9,8},{10,9},{11,10},{12... | collective-permute-start | bytes 49160 | tf_op jit(solution)/shard_map/ppermute | solution.py:270
  38.6 6.6 %collective-permute-start.2 = (f32[4,8,128]{2,1,0:T(8,128)S(1)}, f32[4,8,128]{2,1,0:T(8,128)S(1)}, u32[]{:S(2)}, u32[]{:S(2)}) collective-permute-start(f32[4,8,128]{2,1,0:T(8,128)S(1)} %pad_maximum_fusion.1), channel_id=1, source_target_pairs={{0,1},{1,2},{2,3},{3,4},{4,5},{5,6},{6,7},{8,9},{9,10},{10,11},{11... | collective-permute-start | bytes 49160 | tf_op jit(solution)/shard_map/ppermute | solution.py:269
  45.2 25.3 %copy-start.7 = (f32[12,8,128]{2,1,0:T(8,128)}, f32[12,8,128]{2,1,0:T(8,128)S(1)}, u32[]{:S(2)}) copy-start(f32[12,8,128]{2,1,0:T(8,128)S(1)} %pad_maximum_fusion.kappa_ref) | copy-start | bytes 147460
  45.2 18.2 %collective-permute-start.4 = (f32[12,8,128]{2,1,0:T(8,128)S(1)}, f32[12,8,128]{2,1,0:T(8,128)S(1)}, u32[]{:S(2)}, u32[]{:S(2)}) collective-permute-start(f32[12,8,128]{2,1,0:T(8,128)S(1)} %pad_maximum_fusion.kappa_ref), channel_id=1, source_target_pairs={{0,8},{8,16},{16,24},{24,32},{32,40},{40,48},{48,56},{56,64},{64,7... | collective-permute-start | bytes 147464 | tf_op jit(solution)/shard_map/ppermute | solution.py:269
  50.2 13.2 %collective-permute-start.5 = (f32[12,8,128]{2,1,0:T(8,128)S(1)}, f32[12,8,128]{2,1,0:T(8,128)S(1)}, u32[]{:S(2)}, u32[]{:S(2)}) collective-permute-start(f32[12,8,128]{2,1,0:T(8,128)S(1)} %pad_maximum_fusion.kappa_ref), channel_id=1, source_target_pairs={{8,0},{16,8},{24,16},{32,24},{40,32},{48,40},{56,48},{64,56},{72,6... | collective-permute-start | bytes 147464 | tf_op jit(solution)/shard_map/ppermute | solution.py:270
  54.2 16.3 %copy-start.5 = (f32[96,128]{1,0:T(8,128)}, f32[96,128]{1,0:T(8,128)S(1)}, u32[]{:S(2)}) copy-start(f32[96,128]{1,0:T(8,128)S(1)} %bricks.1) | copy-start | bytes 147460
  54.2 9.2 %collective-permute-start = (f32[12,8,128]{2,1,0:T(8,128)S(1)}, f32[12,8,128]{2,1,0:T(8,128)S(1)}, u32[]{:S(2)}, u32[]{:S(2)}) collective-permute-start(f32[12,8,128]{2,1,0:T(8,128)S(1)} %bitcast.20), channel_id=1, source_target_pairs={{0,8},{8,16},{16,24},{24,32},{32,40},{40,48},{48,56},{56,64},{64,7... | collective-permute-start | bytes 147464 | tf_op jit(solution)/shard_map/ppermute | solution.py:269
  61.4 9.0 %collective-permute-start.1 = (f32[12,8,128]{2,1,0:T(8,128)S(1)}, f32[12,8,128]{2,1,0:T(8,128)S(1)}, u32[]{:S(2)}, u32[]{:S(2)}) collective-permute-start(f32[12,8,128]{2,1,0:T(8,128)S(1)} %bitcast.21), channel_id=1, source_target_pairs={{8,0},{16,8},{24,16},{32,24},{40,32},{48,40},{56,48},{64,56},{72,6... | collective-permute-start | bytes 147464 | tf_op jit(solution)/shard_map/ppermute | solution.py:270
  63.4 7.1 %copy-start.8 = (f32[12,8,128]{2,1,0:T(8,128)}, f32[12,8,128]{2,1,0:T(8,128)S(1)}, u32[]{:S(2)}) copy-start(f32[12,8,128]{2,1,0:T(8,128)S(1)} %collective-permute-done.4.kappa_before) | copy-start | bytes 147460
  63.4 7.1 %copy-start.9 = (f32[12,8,128]{2,1,0:T(8,128)}, f32[12,8,128]{2,1,0:T(8,128)S(1)}, u32[]{:S(2)}) copy-start(f32[12,8,128]{2,1,0:T(8,128)S(1)} %collective-permute-done.5.kappa_after) | copy-start | bytes 147460
  63.4 7.1 %copy-start.10 = (f32[12,8,128]{2,1,0:T(8,128)}, f32[12,8,128]{2,1,0:T(8,128)S(1)}, u32[]{:S(2)}) copy-start(f32[12,8,128]{2,1,0:T(8,128)S(1)} %collective-permute-done.before_ref) | copy-start | bytes 147460
  70.5 0.6 copy-start.11

commit v2 on v1

v2 whole, which is shorter than its diff:
```python
import jax
import jax.numpy as jnp
from jax import lax
from jax.experimental import pallas as pl
from jax.experimental.pallas import tpu as pltpu
from jax.sharding import PartitionSpec as P

NVEC = 2
CX = 4
CY = 4
NZ = 128
TILE_ROWS = 4
TILE_COLS = 8
KMAX = 8
LEAF = 512
NLEAF = 8
PTS = 2048
ROWS = 16
COLS = 8
TS = 4096
CAP = 32
DEV = ROWS * COLS
SLAB = 16
F32 = jnp.float32
BF16 = jnp.bfloat16
NT = (((1,), (1,)), ((), ()))
MIB = 1 << 20
LEVELS = 64.0
STEPS = 32000.0
FIELD = 3 * CX * NVEC * CY


def iota(shape, dim):
    return lax.broadcasted_iota(jnp.int32, shape, dim)


def pack_kernel(vectors_ref, kappa_ref, out_ref):
    rows = [kappa_ref[q // CY, q % CY : q % CY + 1, :] for q in range(CX * CY)]
    half = CX * CY // NVEC
    for s in range(ROWS):
        out_ref[s, :, 0:PTS] = vectors_ref[...]
    for q in range(half):
        pair = jnp.concatenate([rows[q], rows[half + q]], axis=0).astype(BF16)
        for s in range(ROWS):
            out_ref[s, :, PTS + q * NZ : PTS + (q + 1) * NZ] = pair


def slots_kernel(
    perm_ref, right_hbm, left_hbm, leaf_hbm, rank_ref, place_ref, right, left, leaves, sems
):
    copies = [
        pltpu.make_async_copy(right_hbm, right, sems.at[0]),
        pltpu.make_async_copy(leaf_hbm, leaves, sems.at[1]),
        pltpu.make_async_copy(left_hbm, left, sems.at[2]),
    ]
    for copy in copies:
        copy.start()
    chunk = 256
    upto = jnp.where(iota((chunk, chunk), 0) <= iota((chunk, chunk), 1), 1.0, 0.0).astype(BF16)
    brick = iota((DEV, chunk), 0)
    carry = jnp.zeros((COLS * DEV, 1), F32)
    for j in range(PTS // chunk):
        masks = [
            (perm_ref[0:1, k * PTS + j * chunk : k * PTS + (j + 1) * chunk] >> 11) == brick
            for k in range(COLS)
        ]
        hot = jnp.concatenate([jnp.where(m, 1.0, 0.0).astype(BF16) for m in masks], axis=0)
        count = jnp.dot(hot, upto, preferred_element_type=F32)
        total = count + carry
        for k in range(COLS):
            at = jnp.where(masks[k], total[k * DEV : (k + 1) * DEV], 0.0)
            rank_ref[0:1, k * PTS + j * chunk : k * PTS + (j + 1) * chunk] = (
                jnp.sum(at, axis=0, keepdims=True) - 1.0
            ).astype(jnp.int32)
        carry = total[:, chunk - 1 : chunk]
    col = lax.axis_index("col")
    start = pl.multiple_of(col * PTS, PTS)
    own = perm_ref[0:1, pl.ds(start, PTS)]
    slot = rank_ref[0:1, pl.ds(start, PTS)] + (col % 4) * CAP
    here = slot == iota((128, PTS), 0)
    inside = own & (PTS - 1)
    coarse = jnp.where(here, (inside & ~(NZ - 1)).astype(F32), 0.0).astype(BF16)
    fine = jnp.where(here, (inside & (NZ - 1)).astype(F32) + 1.0, 0.0).astype(BF16)
    hot = jnp.where((own >> 11) == iota((DEV, PTS), 0), 1.0, 0.0).astype(BF16)
    place_ref[...] = lax.dot_general(
        hot, coarse, NT, preferred_element_type=F32
    ) + lax.dot_general(hot, fine, NT, preferred_element_type=F32)
    for copy in copies:
        copy.wait()


def send_kernel(
    leaf_at,
    x_ref,
    tile_rank_ref,
    perm_ref,
    rank_ref,
    place_ref,
    right,
    left,
    leaves,
    out_ref,
    x_rows,
    sums,
    stage,
):
    half = TS // PTS
    for s in range(ROWS):
        b, h = divmod(s, half)
        block = x_ref[s, :, 0:PTS].astype(F32)
        x_rows[b : b + 1, h * PTS : (h + 1) * PTS] = block[0:1]
        x_rows[8 + b : 9 + b, h * PTS : (h + 1) * PTS] = block[1:2]
    terms = TILE_ROWS * TILE_COLS * KMAX
    lane = iota((16, terms), 1)
    sub = iota((16, terms), 0)
    widen = jnp.where(
        iota((TILE_ROWS * TILE_COLS, terms), 1) // KMAX
        == iota((TILE_ROWS * TILE_COLS, terms), 0),
        1.0,
        0.0,
    ).astype(BF16)
    ranks = jnp.broadcast_to(tile_rank_ref[...].astype(F32), (16, TILE_ROWS * TILE_COLS))
    rank_lane = jnp.dot(ranks.astype(BF16), widen, preferred_element_type=F32)
    keep = (sub % 8 == (lane // KMAX) % TILE_COLS) & ((lane % KMAX).astype(F32) < rank_lane)
    x_all = x_rows[...].astype(BF16)
    projected = lax.dot_general(x_all, right[...], NT, preferred_element_type=F32)
    projected = jnp.where(keep, projected, 0.0)
    first = jnp.sum(projected[0:8], axis=0, keepdims=True)
    second = jnp.sum(projected[8:16], axis=0, keepdims=True)
    by_row = jnp.where(sub < 8, first, second)
    by_row = jnp.where(sub % 8 == lane // (TILE_COLS * KMAX), by_row, 0.0).astype(BF16)
    sums[...] = jnp.dot(by_row, left[...], preferred_element_type=F32)
    per_tile = TS // LEAF
    for l in range(NLEAF):
        i, j = leaf_at[0, 0, l, 0], leaf_at[0, 0, l, 1]
        from_lane = pl.multiple_of((j % per_tile) * LEAF, LEAF)
        to_lane = pl.multiple_of((i % per_tile) * LEAF, LEAF)
        picked = jnp.concatenate(
            [x_rows[pl.ds(8 * v + j // per_tile, 1), pl.ds(from_lane, LEAF)] for v in range(NVEC)],
            axis=0,
        ).astype(BF16)
        near = lax.dot_general(picked, leaves[l], NT, preferred_element_type=F32)
        for v in range(NVEC):
            at = (pl.ds(8 * v + i // per_tile, 1), pl.ds(to_lane, LEAF))
            sums[at] = sums[at] + near[v : v + 1]
    largest = jnp.max(jnp.abs(sums[...]), axis=0, keepdims=True)
    largest = jnp.broadcast_to(jnp.max(largest, axis=1, keepdims=True), (8, 128))
    level = jnp.ceil(jnp.maximum(jnp.log2(largest), -100.0) * LEVELS)
    inverse = (STEPS * jnp.exp2(level * (-1.0 / LEVELS)))[0:1]

    def put(values, first_row, step):
        none = jnp.zeros((COLS, 128), F32)
        stage[pl.ds(first_row, COLS, stride=SLAB), :] = none
        stage[pl.ds(first_row + COLS * SLAB, DEV - COLS, stride=SLAB), :] = values[: DEV - COLS]
        stage[pl.ds(first_row + step, DEV, stride=SLAB), :] = values
        at = first_row + 2 * step
        stage[pl.ds(at, DEV - COLS, stride=SLAB), :] = values[COLS:]
        stage[pl.ds(at + (DEV - COLS) * SLAB, COLS, stride=SLAB), :] = none

    put(place_ref[...], 12, 1)
    stage[pl.ds(15, DEV, stride=SLAB), :] = jnp.broadcast_to(level[0:1], (DEV, 128))
    brick = iota((DEV, PTS), 0)
    slots = iota((CAP, PTS), 0)
    for group in range(2):
        parts = []
        for kk in range(4):
            k = group * 4 + kk
            a, h = divmod(k, half)
            at = slice(k * PTS, (k + 1) * PTS)
            hot = jnp.where((perm_ref[0:1, at] >> 11) == brick, 1.0, 0.0).astype(BF16)
            mask = rank_ref[0:1, at] == slots
            rows = [sums[8 * v + a : 8 * v + a + 1, h * PTS : (h + 1) * PTS] for v in range(NVEC)]
            highs = [row.astype(BF16).astype(F32) for row in rows]
            lows = [row - high for row, high in zip(rows, highs)]
            spread = jnp.concatenate(
                [jnp.where(mask, row, 0.0).astype(BF16) for row in highs + lows], axis=0
            )
            part = lax.dot_general(hot, spread, NT, preferred_element_type=F32)
            parts.append(part + pltpu.roll(part, NVEC * CAP, 1))
        for v in range(NVEC):
            values = jnp.concatenate([p[:, v * CAP : (v + 1) * CAP] for p in parts], axis=1)
            put(jnp.round(values * inverse), group * 2 + v, 4)
    out_ref[...] = stage[...].astype(jnp.int32).astype(jnp.int16)


def bricks_kernel(got_ref, packed_ref, kappa_ref, out_ref, sums, wheres, at_cells, hots):
    for r in range(ROWS):
        for g in range(2):
            total = None
            for c in range(4):
                at = ((r * 2 + g) * 4 + c) * SLAB
                one = got_ref[at : at + SLAB, :].astype(jnp.int32).astype(F32)
                size = jnp.exp2(one[15:16] * (1.0 / LEVELS)) * (1.0 / STEPS)
                one = jnp.where(iota((SLAB, 128), 0) < 12, one * size, one)
                total = one if total is None else total + one
            wheres[g, r * SLAB : (r + 1) * SLAB, :] = total
    sums[...] = wheres[0] + wheres[1]
    for g in range(2):
        place = wheres[g] - 1.0
        cell = jnp.floor(place * (1.0 / NZ))
        at_cells[g] = cell
        wheres[g] = place - cell * NZ
    sub = iota((8, 128), 0)
    z_row = iota((NZ, 128), 0).astype(F32)
    for j in range(3):
        for r in range(ROWS):
            for g in range(2):
                lanes = slice((r * 2 + g) * 128, (r * 2 + g + 1) * 128)
                at = r * SLAB + j * 4 + g * 2
                pair = jnp.where(sub < 4, sums[at : at + 1, :], sums[at + 1 : at + 2, :])
                high = pair.astype(BF16).astype(F32)
                low = pair - high
                p = r * SLAB + 12 + j
                cell = at_cells[g, p : p + 1, :]
                z_at = wheres[g, p : p + 1, :]
                wanted = [cell == (x * CY + sub % CY).astype(F32) for x in range(CX)]
                rows = jnp.concatenate(
                    [jnp.where(w, part, 0.0) for part in (high, low) for w in wanted], axis=0
                )
                hots[0, 0:64, lanes] = rows.astype(BF16)
                hots[1, :, lanes] = jnp.where(z_at == z_row, 1.0, 0.0).astype(BF16)
        both = lax.dot_general(hots[0, 0:64, :], hots[1], NT, preferred_element_type=F32)
        out_ref[j * 32 : (j + 1) * 32, :] = both[0:32] + both[32:64]
    my_row = lax.axis_index("row")
    half = CX * CY // NVEC
    for j, r in ((0, jnp.maximum(my_row - 1, 0)), (2, jnp.minimum(my_row + 1, ROWS - 1))):
        block = packed_ref[r, :, PTS:].astype(F32)
        for q in range(half):
            for v in range(NVEC):
                at = FIELD + j * CX * CY + v * half + q
                out_ref[at : at + 1, :] = block[v : v + 1, q * NZ : (q + 1) * NZ]
    for x in range(CX):
        at = FIELD + CX * CY + x * CY
        out_ref[at : at + CY, :] = kappa_ref[x]


def prior_kernel(own_ref, before_ref, after_ref, out_ref):
    my_row, my_col = lax.axis_index("row"), lax.axis_index("col")
    wide = 3 * CX
    inside_x = [
        jnp.where(my_row > 0, 1.0, 0.0),
        jnp.float32(1.0),
        jnp.where(my_row < ROWS - 1, 1.0, 0.0),
    ]
    inside_y = [
        jnp.where(my_col > 0, 1.0, 0.0),
        jnp.float32(1.0),
        jnp.where(my_col < COLS - 1, 1.0, 0.0),
    ]
    y_at = iota((8, NZ), 0) % CY
    z_at = iota((8, NZ), 1)
    refs = (before_ref, own_ref, after_ref)
    us = [[ref[8 * x : 8 * x + 8, :] for x in range(wide)] for ref in refs]
    ks = []
    for ref in refs:
        rows = [ref[FIELD + CY * x : FIELD + CY * (x + 1), :] for x in range(wide)]
        ks.append([6.0 + jnp.concatenate([row, row], axis=0) for row in rows])
    for step in range(1, 5):
        new = [[None] * wide for _ in range(3)]
        for b in range(3):
            if step == 4 and b != 1:
                continue
            for x in range(step, wide - step):
                u = us[b][x]
                lower = pltpu.roll(us[b - 1][x], 5, 0) if b > 0 else 0.0
                upper = pltpu.roll(us[b + 1][x], 3, 0) if b < 2 else 0.0
                beside = us[b][x - 1] + us[b][x + 1]
                beside = beside + jnp.where(y_at == 0, lower, pltpu.roll(u, 1, 0))
                beside = beside + jnp.where(y_at == CY - 1, upper, pltpu.roll(u, 7, 0))
                beside = beside + jnp.where(z_at == 0, 0.0, pltpu.roll(u, 1, 1))
                beside = beside + jnp.where(z_at == NZ - 1, 0.0, pltpu.roll(u, NZ - 1, 1))
                result = (ks[b][x] * u - beside) * 0.125
                if step < 4:
                    if b != 1 and x // CX != 1:
                        result = result * (inside_y[b] * inside_x[x // CX])
                    elif b != 1:
                        result = result * inside_y[b]
                    elif x // CX != 1:
                        result = result * inside_x[x // CX]
                new[b][x] = result
        us = new
    for x in range(CX):
        for v in range(NVEC):
            out_ref[v, x] = us[1][CX + x][v * CY : (v + 1) * CY]


def to_both_sides(array, axis):
    size = lax.axis_size(axis)
    before = lax.ppermute(array, axis, [(i, i + 1) for i in range(size - 1)])
    after = lax.ppermute(array, axis, [(i + 1, i) for i in range(size - 1)])
    return before, after


def cost(flops, size):
    return pl.CostEstimate(flops=flops, bytes_accessed=size, transcendentals=0)


def params(mib):
    return pltpu.CompilerParams(vmem_limit_bytes=mib * MIB)


def per_device(
    vectors, lr_left, lr_right, tile_rank, leaf_values, leaf_places, cluster_perm, kappa
):
    vmem = pl.BlockSpec(memory_space=pltpu.VMEM)
    smem = pl.BlockSpec(memory_space=pltpu.SMEM)
    hbm = pl.BlockSpec(memory_space=pltpu.HBM)
    points = COLS * PTS
    terms = TILE_ROWS * TILE_COLS * KMAX
    shape = jax.ShapeDtypeStruct
    packed = pl.pallas_call(
        pack_kernel,
        out_shape=shape((ROWS, NVEC, PTS + PTS // NVEC), BF16),
        in_specs=[vmem] * 2,
        out_specs=vmem,
        compiler_params=params(8),
        name="pack",
    )(vectors[:, 0], kappa)
    packed = lax.all_to_all(packed, "row", 0, 0, tiled=True)
    rank, place, right, left, leaves = pl.pallas_call(
        slots_kernel,
        out_shape=(
            shape((1, points), jnp.int32),
            shape((DEV, 128), F32),
            shape((terms, TS), BF16),
            shape((terms, TS), BF16),
            shape((NLEAF, LEAF, LEAF), BF16),
        ),
        in_specs=[vmem, hbm, hbm, hbm],
        out_specs=(vmem,) * 5,
        scratch_shapes=[pltpu.SemaphoreType.DMA((3,))],
        compiler_params=params(20),
        cost_estimate=cost(1 << 31, 1 << 20),
        name="slots",
    )(
        cluster_perm,
        lr_right.reshape(terms, TS),
        lr_left.reshape(terms, TS),
        leaf_values[0, 0],
    )
    send = pl.pallas_call(
        send_kernel,
        out_shape=shape((DEV * SLAB, 128), jnp.int16),
        in_specs=[smem] + [vmem] * 8,
        out_specs=vmem,
        scratch_shapes=[
            pltpu.VMEM((16, TS), F32),
            pltpu.VMEM((16, TS), F32),
            pltpu.VMEM((DEV * SLAB, 128), F32),
        ],
        compiler_params=params(20),
        cost_estimate=cost(1 << 31, 8 << 20),
        name="partial_sums",
    )(leaf_places, packed, tile_rank[0], cluster_perm, rank, place, right, left, leaves)
    got = lax.all_to_all(send.reshape(DEV, SLAB, 128), ("row", "col"), 0, 0, tiled=True)
    own = pl.pallas_call(
        bricks_kernel,
        out_shape=shape((FIELD + 3 * CX * CY, NZ), F32),
        in_specs=[vmem] * 3,
        out_specs=vmem,
        scratch_shapes=[
            pltpu.VMEM((ROWS * SLAB, 128), F32),
            pltpu.VMEM((2, ROWS * SLAB, 128), F32),
            pltpu.VMEM((2, ROWS * SLAB, 128), F32),
            pltpu.VMEM((2, NZ, 4096), BF16),
        ],
        compiler_params=params(16),
        cost_estimate=cost(1 << 30, 1 << 20),
        name="bricks",
    )(got.reshape(DEV * SLAB, 128), packed, kappa)
    before, after = to_both_sides(own, "col")
    return pl.pallas_call(
        prior_kernel,
        out_shape=shape((NVEC, CX, CY, NZ), F32),
        in_specs=[vmem] * 3,
        out_specs=vmem,
        compiler_params=params(8),
        cost_estimate=cost(1 << 24, 1 << 20),
        name="prior",
    )(own, before, after)


def solution(mesh):
    in_specs = (
        P(None, "col", "row"),
        P("row", "col", None, None, None),
        P("row", "col", None, None, None),
        P("row", "col", None),
        P("row", "col", None, None, None),
        P("row", "col", None, None),
        P("row", None),
        P("row", "col", None),
    )
    out_specs = P(None, "row", "col", None)
    return jax.shard_map(
        per_device, mesh=mesh, in_specs=in_specs, out_specs=out_specs, check_vma=False
    )
```

time: 74.9 us -> 71.7 us (0.957)
  the two profiles are of different devices: /device:TPU:105 before, /device:TPU:8 now
where the time goes in v2:
time: 71.7 us; the launch traced here: 71.2 us
  blocking collectives  23.2 us (32%)
  local copies, waits for them, and re-layouts  15.4 us (21%)
  Pallas kernels  13.1 us (18%)
  starting transfers between devices  13 us (18%)
  waiting for transfers between devices  6.38 us (9%)
    all_to_all x1, blocking collectives, per_device(): lax.all_to_all(send.reshape(DEV, SLAB, 128), ('row', 'col'), 0, 0, tiled=...  23.2 us
    unnamed x27, local copies, waits for them, and re-layouts  15.4 us
    all_to_all x1, starting transfers between devices, per_device(): packed = lax.all_to_all(packed, 'row', 0, 0, tiled=True)  7.15 us
    ppermute x1, waiting for transfers between devices, to_both_sides(): before = lax.ppermute(array, axis, [(i, i + 1) for i in range(size - 1)])  5.99 us
    pallas_call x1, Pallas kernels, per_device(): pl.pallas_call(send_kernel, out_shape=shape((DEV * SLAB, 128), jnp.int16)...  5.66 us
    pallas_call x1, Pallas kernels, per_device(): pl.pallas_call(slots_kernel, out_shape=(shape((1, points), jnp.int32), sh...  3.71 us
    ppermute x1, starting transfers between devices, to_both_sides(): after = lax.ppermute(array, axis, [(i + 1, i) for i in range(size - 1)])  3.62 us
    ppermute x1, starting transfers between devices, to_both_sides(): before = lax.ppermute(array, axis, [(i, i + 1) for i in range(size - 1)])  2.23 us
  transfers between devices with their start and end apart: 3, of which 2 were waited for; matrix products, arithmetic and copies ran while one was open for 1% of the time, Pallas kernels for 5%

profile of v2, /device:TPU:8, one launch (start us, length us, event | category | flops | bytes accessed | tf_op | source)
XLA Modules:
  0.0 71.2 jit_solution(6579690250281126842)
XLA Ops:
  0.0 0.0 copy-start.9
  0.0 0.7 copy-done.9
  0.7 0.0 copy-start.10
  0.7 0.7 copy-done.10
  1.4 0.7 %pack.1 = bf16[16,2,3072]{2,1,0:T(2,128)(2,1)} custom-call(bf16[2,2048]{1,0:T(2,128)(2,1)S(1)} %bitcast.12, f32[4,4,128]{2,1,0:T(4,128)S(1)} %copy-done.10), custom_call_target="tpu_custom_call" | custom-call | tf_op jit(solution)/shard_map/pack/pallas_call | solution.py:311
  2.1 7.1 %all-to-all-start = ((bf16[16,2,3072]{2,1,0:T(2,128)(2,1)}), bf16[16,2,3072]{2,1,0:T(2,128)(2,1)S(1)}, u32[]{:S(2)}, u32[]{:S(2)}) async-start(bf16[16,2,3072]{2,1,0:T(2,128)(2,1)} %pack.1), calls=%async_computation | async-start | bytes 393216 | tf_op jit(solution)/shard_map/all_to_all | solution.py:319
  9.3 0.8 %copy.9.leaf_at = s32[1,1,8,2]{3,2,1,0:T(8,128)S(1)} copy(s32[1,1,8,2]{2,3,1,0:T(2,128)} %param.13) | data formatting | bytes 128 | tf_op args[5]
  10.0 0.0 copy-start
  10.0 2.2 %copy-done = bf16[1,1,8,512,512]{4,3,2,1,0:T(8,128)(2,1)S(1)} copy-done((bf16[1,1,8,512,512]{4,3,2,1,0:T(8,128)(2,1)S(1)}, bf16[1,1,8,512,512]{4,3,2,1,0:T(8,128)(2,1)}, u32[]{:S(2)}) %copy-start) | copy-done | bytes 4194328
  12.2 0.0 copy-start.3
  12.2 1.6 %copy-done.3 = bf16[1,1,32,8,4096]{4,3,2,1,0:T(8,128)(2,1)S(1)} copy-done((bf16[1,1,32,8,4096]{4,3,2,1,0:T(8,128)(2,1)S(1)}, bf16[1,1,32,8,4096]{4,3,2,1,0:T(8,128)(2,1)}, u32[]{:S(2)}) %copy-start.3) | copy-done | bytes 2097176
  13.8 0.0 copy-start.4
  13.8 1.6 %copy-done.4 = bf16[1,1,32,8,4096]{4,3,2,1,0:T(8,128)(2,1)S(1)} copy-done((bf16[1,1,32,8,4096]{4,3,2,1,0:T(8,128)(2,1)S(1)}, bf16[1,1,32,8,4096]{4,3,2,1,0:T(8,128)(2,1)}, u32[]{:S(2)}) %copy-start.4) | copy-done | bytes 2097176
  15.4 0.0 copy-start.7
  15.4 0.8 %copy-done.7 = s32[1,16384]{1,0:T(1,128)S(1)} copy-done((s32[1,16384]{1,0:T(1,128)S(1)}, s32[1,16384]{1,0:T(1,128)}, u32[]{:S(2)}) %copy-start.7) | copy-done | bytes 65560
  16.2 0.0 copy-start.8
  16.2 0.0 copy-start.12
  16.2 3.7 %slots.1 = (s32[1,16384]{1,0:T(1,128)S(1)}, f32[128,128]{1,0:T(8,128)S(1)}, bf16[256,4096]{1,0:T(8,128)(2,1)S(1)}, bf16[256,4096]{1,0:T(8,128)(2,1)S(1)}, bf16[8,512,512]{2,1,0:T(8,128)(2,1)S(1)}) custom-call(s32[1,16384]{1,0:T(1,128)S(1)} %copy-done.7, bf16[256,4096]{1,0:T(8,128)(2,1)S(1)} %bitcast.9, bf16[256,4096]{1,0:T(8,128)(2,1)S(1)} %bitcast.10, ...), custom_call_target="tpu_custom_call" | custom-call | flops 2147483648 | bytes 1048576 | tf_op jit(solution)/shard_map/slots/pallas_call | solution.py:320
  20.0 0.0 copy-start.1
  20.0 2.0 %copy-done.1 = bf16[8,512,512]{2,1,0:T(8,128)(2,1)} copy-done((bf16[8,512,512]{2,1,0:T(8,128)(2,1)}, bf16[8,512,512]{2,1,0:T(8,128)(2,1)S(1)}, u32[]{:S(2)}) %copy-start.1) | copy-done | bytes 4194328
  21.9 0.0 copy-start.5
  21.9 1.3 %copy-done.5 = bf16[256,4096]{1,0:T(8,128)(2,1)} copy-done((bf16[256,4096]{1,0:T(8,128)(2,1)}, bf16[256,4096]{1,0:T(8,128)(2,1)S(1)}, u32[]{:S(2)}) %copy-start.5) | copy-done | bytes 2097176
  23.3 0.0 all-to-all-done.x_ref.packed_ref
  23.3 0.0 copy-done.8
  23.3 0.0 copy-done.12
  23.3 0.0 copy-start.2
  23.3 2.2 %copy-done.2 = bf16[8,512,512]{2,1,0:T(8,128)(2,1)S(1)} copy-done((bf16[8,512,512]{2,1,0:T(8,128)(2,1)S(1)}, bf16[8,512,512]{2,1,0:T(8,128)(2,1)}, u32[]{:S(2)}) %copy-start.2) | copy-done | bytes 4194328
  25.5 0.0 copy-start.6
  25.5 1.6 %copy-done.6 = bf16[256,4096]{1,0:T(8,128)(2,1)S(1)} copy-done((bf16[256,4096]{1,0:T(8,128)(2,1)S(1)}, bf16[256,4096]{1,0:T(8,128)(2,1)}, u32[]{:S(2)}) %copy-start.6) | copy-done | bytes 2097176
  27.1 0.0 copy-start.11
  27.1 5.7 %partial_sums.1 = s16[2048,128]{1,0:T(8,128)(2,1)S(1)} custom-call(s32[1,1,8,2]{3,2,1,0:T(8,128)S(1)} %copy.9.leaf_at, bf16[16,2,3072]{2,1,0:T(2,128)(2,1)S(1)} %all-to-all-done.x_ref.packed_ref, s32[1,32]{1,0:T(1,128)S(1)} %bitcast.13, s32[1,16384]{1,0:T(1,128)S(1)} %copy-done.8, s32[1,16384]{1,0:T(1,128)S(1)} %get-tuple-element.10.rank_ref, ...), custom_call_target="tpu_custom_call" | custom-call | flops 2147483648 | bytes 8388608 | tf_op jit(solution)/shard_map/partial_sums/pallas_call | solution.py:341
  32.7 23.2 %all_to_all.10 = s16[128,16,128]{2,1,0:T(8,128)(2,1)S(1)} all-to-all(s16[128,16,128]{2,1,0:T(8,128)(2,1)S(1)} %bitcast.8), channel_id=1, replica_groups=mesh['row'=16,'col'=8] {'row','col'}, dimensions={0} | all-to-all | bytes 1048576 | tf_op jit(solution)/shard_map/all_to_all | solution.py:355
  55.9 0.0 copy-done.11
  55.9 2.1 %bricks.1.own_ref = f32[144,128]{1,0:T(8,128)S(1)} custom-call(s16[2048,128]{1,0:T(8,128)(2,1)S(1)} %bitcast.11, bf16[16,2,3072]{2,1,0:T(2,128)(2,1)S(1)} %all-to-all-done.x_ref.packed_ref, f32[4,4,128]{2,1,0:T(4,128)S(1)} %copy-done.11), custom_call_target="tpu_custom_call" | custom-call | flops 1073741824 | bytes 1048576 | tf_op jit(solution)/shard_map/bricks/pallas_call | solution.py:356
  58.0 3.6 %collective-permute-start.1 = (f32[144,128]{1,0:T(8,128)S(1)}, f32[144,128]{1,0:T(8,128)S(1)}, u32[]{:S(2)}, u32[]{:S(2)}) collective-permute-start(f32[144,128]{1,0:T(8,128)S(1)} %bricks.1.own_ref), channel_id=1, source_target_pairs={{1,0},{2,1},{3,2},{4,3},{5,4},{6,5},{7,6},{9,8},{10,9},{11,10},{12... | collective-permute-start | bytes 221192 | tf_op jit(solution)/shard_map/ppermute | solution.py:290
  61.6 2.2 %collective-permute-start = (f32[144,128]{1,0:T(8,128)S(1)}, f32[144,128]{1,0:T(8,128)S(1)}, u32[]{:S(2)}, u32[]{:S(2)}) collective-permute-start(f32[144,128]{1,0:T(8,128)S(1)} %bricks.1.own_ref), channel_id=1, source_target_pairs={{0,1},{1,2},{2,3},{3,4},{4,5},{5,6},{6,7},{8,9},{9,10},{10,11},{11... | collective-permute-start | bytes 221192 | tf_op jit(solution)/shard_map/ppermute | solution.py:289
  63.9 0.4 collective-permute-done.1.after_ref
  64.3 6.0 %collective-permute-done.before_ref = f32[144,128]{1,0:T(8,128)S(1)} collective-permute-done((f32[144,128]{1,0:T(8,128)S(1)}, f32[144,128]{1,0:T(8,128)S(1)}, u32[]{:S(2)}, u32[]{:S(2)}) %collective-permute-start) | collective-permute-done | bytes 73760 | tf_op jit(solution)/shard_map/ppermute | solution.py:289
  70.2 0.9 %prior.1 = f32[2,4,4,128]{3,2,1,0:T(4,128)} custom-call(f32[144,128]{1,0:T(8,128)S(1)} %bricks.1.own_ref, f32[144,128]{1,0:T(8,128)S(1)} %collective-permute-done.before_ref, f32[144,128]{1,0:T(8,128)S(1)} %collective-permute-done.1.after_ref), custom_call_target="tpu_custom_call" | custom-call | flops 16777216 | bytes 1048576 | tf_op jit(solution)/shard_map/prior/pallas_call | solution.py:372
Async XLA Ops:
  0.0 0.7 copy-start.9
  0.7 0.7 copy-start.10
  2.1 21.2 %all-to-all-start = ((bf16[16,2,3072]{2,1,0:T(2,128)(2,1)}), bf16[16,2,3072]{2,1,0:T(2,128)(2,1)S(1)}, u32[]{:S(2)}, u32[]{:S(2)}) async-start(bf16[16,2,3072]{2,1,0:T(2,128)(2,1)} %pack.1), calls=%async_computation | async-start | bytes 393216 | tf_op jit(solution)/shard_map/all_to_all | solution.py:319
  10.0 2.2 %copy-start = (bf16[1,1,8,512,512]{4,3,2,1,0:T(8,128)(2,1)S(1)}, bf16[1,1,8,512,512]{4,3,2,1,0:T(8,128)(2,1)}, u32[]{:S(2)}) copy-start(bf16[1,1,8,512,512]{4,3,2,1,0:T(8,128)(2,1)} %param.12) | copy-start | bytes 12582916
  12.2 1.6 %copy-start.3 = (bf16[1,1,32,8,4096]{4,3,2,1,0:T(8,128)(2,1)S(1)}, bf16[1,1,32,8,4096]{4,3,2,1,0:T(8,128)(2,1)}, u32[]{:S(2)}) copy-start(bf16[1,1,32,8,4096]{4,3,2,1,0:T(8,128)(2,1)} %param.10) | copy-start | bytes 6291460
  13.8 1.6 %copy-start.4 = (bf16[1,1,32,8,4096]{4,3,2,1,0:T(8,128)(2,1)S(1)}, bf16[1,1,32,8,4096]{4,3,2,1,0:T(8,128)(2,1)}, u32[]{:S(2)}) copy-start(bf16[1,1,32,8,4096]{4,3,2,1,0:T(8,128)(2,1)} %param.9) | copy-start | bytes 6291460
  15.4 0.8 %copy-start.7 = (s32[1,16384]{1,0:T(1,128)S(1)}, s32[1,16384]{1,0:T(1,128)}, u32[]{:S(2)}) copy-start(s32[1,16384]{1,0:T(1,128)} %perm_ref.3) | copy-start | bytes 196612
  16.2 7.0 %copy-start.8 = (s32[1,16384]{1,0:T(1,128)S(1)}, s32[1,16384]{1,0:T(1,128)}, u32[]{:S(2)}) copy-start(s32[1,16384]{1,0:T(1,128)} %perm_ref.3) | copy-start | bytes 196612
  16.2 7.0 %copy-start.12 = (s32[1,1,32]{2,1,0:T(1,128)S(1)}, s32[1,1,32]{2,1,0:T(1,128)}, u32[]{:S(2)}) copy-start(s32[1,1,32]{2,1,0:T(1,128)} %param.11) | copy-start | bytes 388
  20.0 2.0 %copy-start.1 = (bf16[8,512,512]{2,1,0:T(8,128)(2,1)}, bf16[8,512,512]{2,1,0:T(8,128)(2,1)S(1)}, u32[]{:S(2)}) copy-start(bf16[8,512,512]{2,1,0:T(8,128)(2,1)S(1)} %get-tuple-element.14.leaves) | copy-start | bytes 12582916
  21.9 1.4 %copy-start.5 = (bf16[256,4096]{1,0:T(8,128)(2,1)}, bf16[256,4096]{1,0:T(8,128)(2,1)S(1)}, u32[]{:S(2)}) copy-start(bf16[256,4096]{1,0:T(8,128)(2,1)S(1)} %get-tuple-element.13.left) | copy-start | bytes 6291460
  23.3 2.2 %copy-start.2 = (bf16[8,512,512]{2,1,0:T(8,128)(2,1)S(1)}, bf16[8,512,512]{2,1,0:T(8,128)(2,1)}, u32[]{:S(2)}) copy-start(bf16[8,512,512]{2,1,0:T(8,128)(2,1)} %copy-done.1) | copy-start | bytes 12582916
  25.5 1.6 %copy-start.6 = (bf16[256,4096]{1,0:T(8,128)(2,1)S(1)}, bf16[256,4096]{1,0:T(8,128)(2,1)}, u32[]{:S(2)}) copy-start(bf16[256,4096]{1,0:T(8,128)(2,1)} %copy-done.5) | copy-start | bytes 6291460
  27.1 28.8 %copy-start.11 = (f32[4,4,128]{2,1,0:T(4,128)S(1)}, f32[4,4,128]{2,1,0:T(4,128)}, u32[]{:S(2)}) copy-start(f32[4,4,128]{2,1,0:T(4,128)} %kappa_ref.3) | copy-start | bytes 24580
  58.0 6.3 %collective-permute-start.1 = (f32[144,128]{1,0:T(8,128)S(1)}, f32[144,128]{1,0:T(8,128)S(1)}, u32[]{:S(2)}, u32[]{:S(2)}) collective-permute-start(f32[144,128]{1,0:T(8,128)S(1)} %bricks.1.own_ref), channel_id=1, source_target_pairs={{1,0},{2,1},{3,2},{4,3},{5,4},{6,5},{7,6},{9,8},{10,9},{11,10},{12... | collective-permute-start | bytes 221192 | tf_op jit(solution)/shard_map/ppermute | solution.py:290
  61.6 8.6 %collective-permute-start = (f32[144,128]{1,0:T(8,128)S(1)}, f32[144,128]{1,0:T(8,128)S(1)}, u32[]{:S(2)}, u32[]{:S(2)}) collective-permute-start(f32[144,128]{1,0:T(8,128)S(1)} %bricks.1.own_ref), channel_id=1, source_target_pairs={{0,1},{1,2},{2,3},{3,4},{4,5},{5,6},{6,7},{8,9},{9,10},{10,11},{11... | collective-permute-start | bytes 221192 | tf_op jit(solution)/shard_map/ppermute | solution.py:289

commit v3 on v2

--- a/solution.py
+++ b/solution.py
@@ -27,74 +27,116 @@
 MIB = 1 << 20
 LEVELS = 64.0
 STEPS = 32000.0
+KAPPA_STEPS = 8000.0
 FIELD = 3 * CX * NVEC * CY
+HALO = FIELD - 2 * NVEC * CY
 
 
 def iota(shape, dim):
     return lax.broadcasted_iota(jnp.int32, shape, dim)
 
 
-def pack_kernel(vectors_ref, kappa_ref, out_ref):
+def pack_kernel(
+    vectors_hbm, kappa_hbm, perm_hbm, rank_hbm, out_ref, kappa_ref, perm_ref, rank_ref, vectors, sems
+):
+    pairs = (
+        (vectors_hbm, vectors),
+        (kappa_hbm, kappa_ref),
+        (perm_hbm, perm_ref),
+        (rank_hbm, rank_ref),
+    )
+    copies = [pltpu.make_async_copy(a, b, sems.at[i]) for i, (a, b) in enumerate(pairs)]
+    for copy in copies:
+        copy.start()
+    copies[0].wait()
+    for s in range(ROWS):
+        out_ref[s, :, 0:PTS] = vectors[...]
+    copies[1].wait()
     rows = [kappa_ref[q // CY, q % CY : q % CY + 1, :] for q in range(CX * CY)]
     half = CX * CY // NVEC
-    for s in range(ROWS):
-        out_ref[s, :, 0:PTS] = vectors_ref[...]
     for q in range(half):
         pair = jnp.concatenate([rows[q], rows[half + q]], axis=0).astype(BF16)
         for s in range(ROWS):
             out_ref[s, :, PTS + q * NZ : PTS + (q + 1) * NZ] = pair
+    copies[2].wait()
+    copies[3].wait()
 
 
 def slots_kernel(
-    perm_ref, right_hbm, left_hbm, leaf_hbm, rank_ref, place_ref, right, left, leaves, sems
+    perm_ref,
+    right_hbm,
+    left_hbm,
+    leaf_hbm,
+    hot_ref,
+    slot_ref,
+    place_ref,
+    right,
+    left,
+    leaves,
+    sems,
 ):
     copies = [
         pltpu.make_async_copy(right_hbm, right, sems.at[0]),
-        pltpu.make_async_copy(leaf_hbm, leaves, sems.at[1]),
-        pltpu.make_async_copy(left_hbm, left, sems.at[2]),
+        pltpu.make_async_copy(left_hbm, left, sems.at[1]),
+        pltpu.make_async_copy(leaf_hbm, leaves, sems.at[2]),
     ]
     for copy in copies:
         copy.start()
     chunk = 256
     upto = jnp.where(iota((chunk, chunk), 0) <= iota((chunk, chunk), 1), 1.0, 0.0).astype(BF16)
     brick = iota((DEV, chunk), 0)
+    slots = iota((CAP, chunk), 0).astype(F32)
     carry = jnp.zeros((COLS * DEV, 1), F32)
     for j in range(PTS // chunk):
+        lanes = slice(j * chunk, (j + 1) * chunk)
         masks = [
             (perm_ref[0:1, k * PTS + j * chunk : k * PTS + (j + 1) * chunk] >> 11) == brick
             for k in range(COLS)
         ]
         hot = jnp.concatenate([jnp.where(m, 1.0, 0.0).astype(BF16) for m in masks], axis=0)
-        count = jnp.dot(hot, upto, preferred_element_type=F32)
-        total = count + carry
+        hot_ref[:, lanes] = hot
+        total = jnp.dot(hot, upto, preferred_element_type=F32) + carry
         for k in range(COLS):
             at = jnp.where(masks[k], total[k * DEV : (k + 1) * DEV], 0.0)
-            rank_ref[0:1, k * PTS + j * chunk : k * PTS + (j + 1) * chunk] = (
-                jnp.sum(at, axis=0, keepdims=True) - 1.0
-            ).astype(jnp.int32)
+            rank = jnp.sum(at, axis=0, keepdims=True) - 1.0
+            slot_ref[k * CAP : (k + 1) * CAP, lanes] = jnp.where(rank == slots, 1.0, 0.0).astype(
+                BF16
+            )
         carry = total[:, chunk - 1 : chunk]
     col = lax.axis_index("col")
-    start = pl.multiple_of(col * PTS, PTS)
-    own = perm_ref[0:1, pl.ds(start, PTS)]
-    slot = rank_ref[0:1, pl.ds(start, PTS)] + (col % 4) * CAP
-    here = slot == iota((128, PTS), 0)
+    own = perm_ref[0:1, pl.ds(pl.multiple_of(col * PTS, PTS), PTS)]
+    here = slot_ref[pl.ds(pl.multiple_of(col * CAP, CAP), CAP), :]
+    hot = hot_ref[pl.ds(pl.multiple_of(col * DEV, DEV), DEV), :]
     inside = own & (PTS - 1)
-    coarse = jnp.where(here, (inside & ~(NZ - 1)).astype(F32), 0.0).astype(BF16)
-    fine = jnp.where(here, (inside & (NZ - 1)).astype(F32) + 1.0, 0.0).astype(BF16)
-    hot = jnp.where((own >> 11) == iota((DEV, PTS), 0), 1.0, 0.0).astype(BF16)
-    place_ref[...] = lax.dot_general(
-        hot, coarse, NT, preferred_element_type=F32
-    ) + lax.dot_general(hot, fine, NT, preferred_element_type=F32)
+    place = jnp.zeros((DEV, 128), F32)
+    for part in (inside & ~(NZ - 1), (inside & (NZ - 1)) + 1):
+        spread = here * part.astype(F32).astype(BF16)
+        spread = jnp.concatenate(
+            [spread * jnp.where(col % 4 == g, 1.0, 0.0).astype(BF16) for g in range(4)], axis=0
+        )
+        place = place + lax.dot_general(hot, spread, NT, preferred_element_type=F32)
+    place_ref[...] = place
     for copy in copies:
         copy.wait()
 
 
+def level_of(values):
+    largest = jnp.max(jnp.abs(values), axis=0, keepdims=True)
+    largest = jnp.broadcast_to(jnp.max(largest, axis=1, keepdims=True), (8, 128))
+    level = jnp.ceil(jnp.maximum(jnp.log2(largest), -100.0) * LEVELS)
+    return level[0:1], (STEPS * jnp.exp2(level * (-1.0 / LEVELS)))[0:1]
+
+
+def step_at(level):
+    return jnp.exp2(level * (1.0 / LEVELS)) * (1.0 / STEPS)
+
+
 def send_kernel(
-    leaf_at,
+    leaf_hbm,
     x_ref,
     tile_rank_ref,
-    perm_ref,
-    rank_ref,
+    hot_ref,
+    slot_ref,
     place_ref,
     right,
     left,
@@ -103,7 +145,11 @@
     x_rows,
     sums,
     stage,
+    leaf_at,
+    sem,
 ):
+    leaf_copy = pltpu.make_async_copy(leaf_hbm, leaf_at, sem)
+    leaf_copy.start()
     half = TS // PTS
     for s in range(ROWS):
         b, h = divmod(s, half)
@@ -130,9 +176,10 @@
     by_row = jnp.where(sub < 8, first, second)
     by_row = jnp.where(sub % 8 == lane // (TILE_COLS * KMAX), by_row, 0.0).astype(BF16)
     sums[...] = jnp.dot(by_row, left[...], preferred_element_type=F32)
+    leaf_copy.wait()
     per_tile = TS // LEAF
     for l in range(NLEAF):
-        i, j = leaf_at[0, 0, l, 0], leaf_at[0, 0, l, 1]
+        i, j = leaf_at[0, l], leaf_at[1, l]
         from_lane = pl.multiple_of((j % per_tile) * LEAF, LEAF)
         to_lane = pl.multiple_of((i % per_tile) * LEAF, LEAF)
         picked = jnp.concatenate(
@@ -143,10 +190,7 @@
         for v in range(NVEC):
             at = (pl.ds(8 * v + i // per_tile, 1), pl.ds(to_lane, LEAF))
             sums[at] = sums[at] + near[v : v + 1]
-    largest = jnp.max(jnp.abs(sums[...]), axis=0, keepdims=True)
-    largest = jnp.broadcast_to(jnp.max(largest, axis=1, keepdims=True), (8, 128))
-    level = jnp.ceil(jnp.maximum(jnp.log2(largest), -100.0) * LEVELS)
-    inverse = (STEPS * jnp.exp2(level * (-1.0 / LEVELS)))[0:1]
+    level, inverse = level_of(sums[...])
 
     def put(values, first_row, step):
         none = jnp.zeros((COLS, 128), F32)
@@ -158,23 +202,18 @@
         stage[pl.ds(at + (DEV - COLS) * SLAB, COLS, stride=SLAB), :] = none
 
     put(place_ref[...], 12, 1)
-    stage[pl.ds(15, DEV, stride=SLAB), :] = jnp.broadcast_to(level[0:1], (DEV, 128))
-    brick = iota((DEV, PTS), 0)
-    slots = iota((CAP, PTS), 0)
+    stage[pl.ds(15, DEV, stride=SLAB), :] = jnp.broadcast_to(level, (DEV, 128))
     for group in range(2):
         parts = []
         for kk in range(4):
             k = group * 4 + kk
             a, h = divmod(k, half)
-            at = slice(k * PTS, (k + 1) * PTS)
-            hot = jnp.where((perm_ref[0:1, at] >> 11) == brick, 1.0, 0.0).astype(BF16)
-            mask = rank_ref[0:1, at] == slots
+            slot = slot_ref[k * CAP : (k + 1) * CAP, :]
             rows = [sums[8 * v + a : 8 * v + a + 1, h * PTS : (h + 1) * PTS] for v in range(NVEC)]
-            highs = [row.astype(BF16).astype(F32) for row in rows]
-            lows = [row - high for row, high in zip(rows, highs)]
-            spread = jnp.concatenate(
-                [jnp.where(mask, row, 0.0).astype(BF16) for row in highs + lows], axis=0
-            )
+            highs = [row.astype(BF16) for row in rows]
+            lows = [(row - high.astype(F32)).astype(BF16) for row, high in zip(rows, highs)]
+            spread = jnp.concatenate([slot * row for row in highs + lows], axis=0)
+            hot = hot_ref[k * DEV : (k + 1) * DEV, :]
             part = lax.dot_general(hot, spread, NT, preferred_element_type=F32)
             parts.append(part + pltpu.roll(part, NVEC * CAP, 1))
         for v in range(NVEC):
@@ -183,15 +222,16 @@
     out_ref[...] = stage[...].astype(jnp.int32).astype(jnp.int16)
 
 
-def bricks_kernel(got_ref, packed_ref, kappa_ref, out_ref, sums, wheres, at_cells, hots):
+def bricks_kernel(
+    got_ref, packed_ref, kappa_ref, out_ref, halo_ref, sums, wheres, at_cells, hots
+):
     for r in range(ROWS):
         for g in range(2):
             total = None
             for c in range(4):
                 at = ((r * 2 + g) * 4 + c) * SLAB
                 one = got_ref[at : at + SLAB, :].astype(jnp.int32).astype(F32)
-                size = jnp.exp2(one[15:16] * (1.0 / LEVELS)) * (1.0 / STEPS)
-                one = jnp.where(iota((SLAB, 128), 0) < 12, one * size, one)
+                one = jnp.where(iota((SLAB, 128), 0) < 12, one * step_at(one[15:16]), one)
                 total = one if total is None else total + one
             wheres[g, r * SLAB : (r + 1) * SLAB, :] = total
     sums[...] = wheres[0] + wheres[1]
@@ -232,6 +272,16 @@
     for x in range(CX):
         at = FIELD + CX * CY + x * CY
         out_ref[at : at + CY, :] = kappa_ref[x]
+    level, inverse = level_of(out_ref[0:FIELD, :])
+
+    def store(at, values):
+        halo_ref[at : at + values.shape[0], :] = (
+            jnp.round(values).astype(jnp.int32).astype(jnp.int16)
+        )
+
+    store(0, out_ref[8 : FIELD - 8, :] * inverse)
+    store(HALO, out_ref[FIELD + 2 * CY : FIELD + 10 * CY, :] * KAPPA_STEPS)
+    store(HALO + 8 * CY, jnp.broadcast_to(level, (16, 128)))
 
 
 def prior_kernel(own_ref, before_ref, after_ref, out_ref):
@@ -249,21 +299,33 @@
     ]
     y_at = iota((8, NZ), 0) % CY
     z_at = iota((8, NZ), 1)
-    refs = (before_ref, own_ref, after_ref)
-    us = [[ref[8 * x : 8 * x + 8, :] for x in range(wide)] for ref in refs]
-    ks = []
-    for ref in refs:
-        rows = [ref[FIELD + CY * x : FIELD + CY * (x + 1), :] for x in range(wide)]
-        ks.append([6.0 + jnp.concatenate([row, row], axis=0) for row in rows])
+    none = jnp.zeros((8, NZ), F32)
+    us, ks = [], []
+    for ref in (before_ref, own_ref, after_ref):
+        if ref is own_ref:
+            field = [ref[8 * x : 8 * x + 8, :] for x in range(wide)]
+            rows = [ref[FIELD + CY * x : FIELD + CY * (x + 1), :] for x in range(wide)]
+            kappas = [6.0 + jnp.concatenate([row, row], axis=0) for row in rows]
+        else:
+            got = ref[...].astype(jnp.int32).astype(F32)
+            values = got[0:HALO] * step_at(got[HALO + 8 * CY : HALO + 8 * CY + 1])
+            field = [values[8 * x : 8 * x + 8] for x in range(wide - 2)]
+            field = [none] + field + [none]
+            values = got[HALO : HALO + 8 * CY] * (1.0 / KAPPA_STEPS) + 6.0
+            rows = [values[CY * x : CY * (x + 1)] for x in range(8)]
+            kappas = [none] * 2 + [jnp.concatenate([row, row], axis=0) for row in rows] + [none] * 2
+        us.append(field)
+        ks.append(kappas)
     for step in range(1, 5):
         new = [[None] * wide for _ in range(3)]
         for b in range(3):
             if step == 4 and b != 1:
                 continue
-            for x in range(step, wide - step):
+            edge = step if b == 1 else step + 1
+            for x in range(edge, wide - edge):
                 u = us[b][x]
-                lower = pltpu.roll(us[b - 1][x], 5, 0) if b > 0 else 0.0
-                upper = pltpu.roll(us[b + 1][x], 3, 0) if b < 2 else 0.0
+                lower = pltpu.roll(us[b - 1][x], 5, 0) if b > 0 and us[b - 1][x] is not None else 0.0
+                upper = pltpu.roll(us[b + 1][x], 3, 0) if b < 2 and us[b + 1][x] is not None else 0.0
                 beside = us[b][x - 1] + us[b][x + 1]
                 beside = beside + jnp.where(y_at == 0, lower, pltpu.roll(u, 1, 0))
                 beside = beside + jnp.where(y_at == CY - 1, upper, pltpu.roll(u, 7, 0))
@@ -295,6 +357,14 @@
     return pl.CostEstimate(flops=flops, bytes_accessed=size, transcendentals=0)
 
 
+def in_hbm(*arrays):
+    return [pltpu.with_memory_space_constraint(a, pltpu.HBM) for a in arrays]
+
+
+def in_vmem(*arrays):
+    return [pltpu.with_memory_space_constraint(a, pltpu.VMEM) for a in arrays]
+
+
 def params(mib):
     return pltpu.CompilerParams(vmem_limit_bytes=mib * MIB)
 
@@ -303,61 +373,75 @@
     vectors, lr_left, lr_right, tile_rank, leaf_values, leaf_places, cluster_perm, kappa
 ):
     vmem = pl.BlockSpec(memory_space=pltpu.VMEM)
-    smem = pl.BlockSpec(memory_space=pltpu.SMEM)
     hbm = pl.BlockSpec(memory_space=pltpu.HBM)
     points = COLS * PTS
     terms = TILE_ROWS * TILE_COLS * KMAX
-    shape = jax.ShapeDtypeStruct
-    packed = pl.pallas_call(
+    packed_shape = (ROWS, NVEC, PTS + PTS // NVEC)
+    packed, kappa_own, perm, ranks = pl.pallas_call(
         pack_kernel,
-        out_shape=shape((ROWS, NVEC, PTS + PTS // NVEC), BF16),
-        in_specs=[vmem] * 2,
-        out_specs=vmem,
+        out_shape=(
+            pltpu.VMEM(packed_shape, BF16),
+            pltpu.VMEM((CX, CY, NZ), F32),
+            pltpu.VMEM((1, points), jnp.int32),
+            pltpu.VMEM((1, TILE_ROWS * TILE_COLS), jnp.int32),
+        ),
+        in_specs=[hbm] * 4,
+        out_specs=(vmem,) * 4,
+        scratch_shapes=[pltpu.VMEM((NVEC, PTS), BF16), pltpu.SemaphoreType.DMA((4,))],
         compiler_params=params(8),
         name="pack",
-    )(vectors[:, 0], kappa)
+    )(*in_hbm(vectors[:, 0], kappa, cluster_perm, tile_rank[0]))
     packed = lax.all_to_all(packed, "row", 0, 0, tiled=True)
-    rank, place, right, left, leaves = pl.pallas_call(
+    hot, slot, place, right, left, leaves = pl.pallas_call(
         slots_kernel,
         out_shape=(
-            shape((1, points), jnp.int32),
-            shape((DEV, 128), F32),
-            shape((terms, TS), BF16),
-            shape((terms, TS), BF16),
-            shape((NLEAF, LEAF, LEAF), BF16),
+            pltpu.VMEM((COLS * DEV, PTS), BF16),
+            pltpu.VMEM((COLS * CAP, PTS), BF16),
+            pltpu.VMEM((DEV, 128), F32),
+            pltpu.VMEM((terms, TS), BF16),
+            pltpu.VMEM((terms, TS), BF16),
+            pltpu.VMEM((NLEAF, LEAF, LEAF), BF16),
         ),
         in_specs=[vmem, hbm, hbm, hbm],
-        out_specs=(vmem,) * 5,
+        out_specs=(vmem,) * 6,
         scratch_shapes=[pltpu.SemaphoreType.DMA((3,))],
-        compiler_params=params(20),
+        compiler_params=params(16),
         cost_estimate=cost(1 << 31, 1 << 20),
         name="slots",
     )(
-        cluster_perm,
-        lr_right.reshape(terms, TS),
-        lr_left.reshape(terms, TS),
-        leaf_values[0, 0],
+        perm,
+        *in_hbm(
+            lr_right.reshape(terms, TS), lr_left.reshape(terms, TS), leaf_values[0, 0]
+        ),
     )
     send = pl.pallas_call(
         send_kernel,
-        out_shape=shape((DEV * SLAB, 128), jnp.int16),
-        in_specs=[smem] + [vmem] * 8,
+        out_shape=jax.ShapeDtypeStruct((DEV * SLAB, 128), jnp.int16),
+        in_specs=[hbm] + [vmem] * 8,
         out_specs=vmem,
         scratch_shapes=[
             pltpu.VMEM((16, TS), F32),
             pltpu.VMEM((16, TS), F32),
             pltpu.VMEM((DEV * SLAB, 128), F32),
+            pltpu.SMEM((2, NLEAF), jnp.int32),
+            pltpu.SemaphoreType.DMA,
         ],
-        compiler_params=params(20),
+        compiler_params=params(16),
         cost_estimate=cost(1 << 31, 8 << 20),
         name="partial_sums",
-    )(leaf_places, packed, tile_rank[0], cluster_perm, rank, place, right, left, leaves)
+    )(
+        *in_hbm(leaf_places[0, 0].T),
+        *in_vmem(packed, ranks, hot, slot, place, right, left, leaves),
+    )
     got = lax.all_to_all(send.reshape(DEV, SLAB, 128), ("row", "col"), 0, 0, tiled=True)
-    own = pl.pallas_call(
+    own, halo = pl.pallas_call(
         bricks_kernel,
-        out_shape=shape((FIELD + 3 * CX * CY, NZ), F32),
+        out_shape=(
+            pltpu.VMEM((FIELD + 3 * CX * CY, NZ), F32),
+            pltpu.VMEM((HALO + 8 * CY + 16, NZ), jnp.int16),
+        ),
         in_specs=[vmem] * 3,
-        out_specs=vmem,
+        out_specs=(vmem,) * 2,
         scratch_shapes=[
             pltpu.VMEM((ROWS * SLAB, 128), F32),
             pltpu.VMEM((2, ROWS * SLAB, 128), F32),
@@ -367,11 +451,11 @@
         compiler_params=params(16),
         cost_estimate=cost(1 << 30, 1 << 20),
         name="bricks",
-    )(got.reshape(DEV * SLAB, 128), packed, kappa)
-    before, after = to_both_sides(own, "col")
+    )(got.reshape(DEV * SLAB, 128), packed, kappa_own)
+    before, after = to_both_sides(halo, "col")
     return pl.pallas_call(
         prior_kernel,
-        out_shape=shape((NVEC, CX, CY, NZ), F32),
+        out_shape=jax.ShapeDtypeStruct((NVEC, CX, CY, NZ), F32),
         in_specs=[vmem] * 3,
         out_specs=vmem,
         compiler_params=params(8),

time: 71.7 us -> 70.3 us (0.980)
  local copies, waits for them, and re-layouts: 15.4 us -> 11.2 us
  Pallas kernels: 13.1 us -> 16.7 us
    unnamed x27 -> x12, local copies, waits for them, and re-layouts: 15.4 us -> 11.2 us
    pallas_call x5, Pallas kernels: 13.1 us -> 16.7 us  [the longest x1 6.34 us: per_device(): pl.pallas_call(slots_kernel, out_shape=(pltpu.VMEM((COLS * DEV, PTS), BF1...]
  transfers between devices with their start and end apart: 3 -> 3, of which waited for: 2 -> 1; matrix products, arithmetic and copies ran while one was open for 1% -> 0% of each run, Pallas kernels for 5% -> 9%
where the time goes in v3:
time: 70.3 us; the launch traced here: 69.9 us
  blocking collectives  23.2 us (33%)
  Pallas kernels  16.7 us (24%)
  starting transfers between devices  13 us (18%)
  local copies, waits for them, and re-layouts  11.2 us (16%)
  waiting for transfers between devices  5.68 us (8%)
    all_to_all x1, blocking collectives, per_device(): lax.all_to_all(send.reshape(DEV, SLAB, 128), ('row', 'col'), 0, 0, tiled=...  23.2 us
    unnamed x12, local copies, waits for them, and re-layouts  11.2 us
    all_to_all x1, starting transfers between devices, per_device(): packed = lax.all_to_all(packed, 'row', 0, 0, tiled=True)  7.16 us
    pallas_call x1, Pallas kernels, per_device(): pl.pallas_call(slots_kernel, out_shape=(pltpu.VMEM((COLS * DEV, PTS), BF1...  6.34 us
    ppermute x1, waiting for transfers between devices, to_both_sides(): before = lax.ppermute(array, axis, [(i, i + 1) for i in range(size - 1)])  5.67 us
    pallas_call x1, Pallas kernels, per_device(): pl.pallas_call(send_kernel, out_shape=jax.ShapeDtypeStruct((DEV * SLAB, 1...  5.66 us
    ppermute x1, starting transfers between devices, to_both_sides(): after = lax.ppermute(array, axis, [(i + 1, i) for i in range(size - 1)])  3.62 us
    ppermute x1, starting transfers between devices, to_both_sides(): before = lax.ppermute(array, axis, [(i, i + 1) for i in range(size - 1)])  2.23 us
  transfers between devices with their start and end apart: 3, of which 1 were waited for; matrix products, arithmetic and copies ran while one was open for 0% of the time, Pallas kernels for 9%

profile of v3, /device:TPU:8, one launch (start us, length us, event | category | flops | bytes accessed | tf_op | source)
XLA Modules:
  0.0 69.9 jit_solution(12246409045620764694)
XLA Ops:
  0.0 1.6 %pack.1 = (bf16[16,2,3072]{2,1,0:T(2,128)(2,1)}, f32[4,4,128]{2,1,0:T(4,128)S(1)}, s32[1,16384]{1,0:T(1,128)S(1)}, s32[1,32]{1,0:T(1,128)S(1)}) custom-call(bf16[2,2048]{1,0:T(2,128)(2,1)} %bitcast.15, f32[4,4,128]{2,1,0:T(4,128)} %kappa_hbm.1, s32[1,16384]{1,0:T(1,128)} %perm_hbm.1, s32[1,32]{1,0:T(1,128)} %bitcast.17), custom_call_target="tpu_custom_call" | custom-call | tf_op jit(solution)/shard_map/pack/pallas_call | solution.py:380
  1.6 7.2 %all-to-all-start = ((bf16[16,2,3072]{2,1,0:T(2,128)(2,1)}), bf16[16,2,3072]{2,1,0:T(2,128)(2,1)S(1)}, u32[]{:S(2)}, u32[]{:S(2)}) async-start(bf16[16,2,3072]{2,1,0:T(2,128)(2,1)} %get-tuple-element.17), calls=%async_computation | async-start | bytes 393216 | tf_op jit(solution)/shard_map/all_to_all | solution.py:394
  8.8 6.3 %slots.1 = (bf16[1024,2048]{1,0:T(8,128)(2,1)S(1)}, bf16[256,2048]{1,0:T(8,128)(2,1)S(1)}, f32[128,128]{1,0:T(8,128)S(1)}, bf16[256,4096]{1,0:T(8,128)(2,1)S(1)}...) custom-call(s32[1,16384]{1,0:T(1,128)S(1)} %get-tuple-element.19.perm_ref, bf16[256,4096]{1,0:T(8,128)(2,1)} %bitcast.13, ...), custom_call_target="tpu_custom_call" | custom-call | flops 2147483648 | bytes 1048576 | tf_op jit(solution)/shard_map/slots/pallas_call | solution.py:395
  15.1 0.0 copy-start
  15.1 1.9 %copy-done = bf16[1024,2048]{1,0:T(8,128)(2,1)} copy-done((bf16[1024,2048]{1,0:T(8,128)(2,1)}, bf16[1024,2048]{1,0:T(8,128)(2,1)S(1)}, u32[]{:S(2)}) %copy-start) | copy-done | bytes 4194328
  17.1 0.0 copy-start.2
  17.1 2.0 %copy-done.2 = bf16[8,512,512]{2,1,0:T(8,128)(2,1)} copy-done((bf16[8,512,512]{2,1,0:T(8,128)(2,1)}, bf16[8,512,512]{2,1,0:T(8,128)(2,1)S(1)}, u32[]{:S(2)}) %copy-start.2) | copy-done | bytes 4194328
  19.0 0.0 copy-start.4
  19.0 1.4 %copy-done.4 = bf16[256,4096]{1,0:T(8,128)(2,1)} copy-done((bf16[256,4096]{1,0:T(8,128)(2,1)}, bf16[256,4096]{1,0:T(8,128)(2,1)S(1)}, u32[]{:S(2)}) %copy-start.4) | copy-done | bytes 2097176
  20.4 0.0 all-to-all-done.x_ref.packed_ref
  20.4 0.0 copy-start.1
  20.4 2.2 %copy-done.1 = bf16[1024,2048]{1,0:T(8,128)(2,1)S(1)} copy-done((bf16[1024,2048]{1,0:T(8,128)(2,1)S(1)}, bf16[1024,2048]{1,0:T(8,128)(2,1)}, u32[]{:S(2)}) %copy-start.1) | copy-done | bytes 4194328
  22.6 0.0 copy-start.3
  22.6 2.2 %copy-done.3 = bf16[8,512,512]{2,1,0:T(8,128)(2,1)S(1)} copy-done((bf16[8,512,512]{2,1,0:T(8,128)(2,1)S(1)}, bf16[8,512,512]{2,1,0:T(8,128)(2,1)}, u32[]{:S(2)}) %copy-start.3) | copy-done | bytes 4194328
  24.8 0.0 copy-start.5
  24.8 1.6 %copy-done.5 = bf16[256,4096]{1,0:T(8,128)(2,1)S(1)} copy-done((bf16[256,4096]{1,0:T(8,128)(2,1)S(1)}, bf16[256,4096]{1,0:T(8,128)(2,1)}, u32[]{:S(2)}) %copy-start.5) | copy-done | bytes 2097176
  26.4 5.7 %partial_sums.1 = s16[2048,128]{1,0:T(8,128)(2,1)S(1)} custom-call(s32[2,8]{1,0:T(2,128)} %bitcast.16, bf16[16,2,3072]{2,1,0:T(2,128)(2,1)S(1)} %all-to-all-done.x_ref.packed_ref, s32[1,32]{1,0:T(1,128)S(1)} %get-tuple-element.18.tile_rank_ref, bf16[1024,2048]{1,0:T(8,128)(2,1)S(1)} %copy-done.1, bf16[256,2048]{1,0:T(8,128)(2,1)S(1)} %get-tuple-element.21.slot_ref, ...), custom_call_target="tpu_custom_call" | custom-call | flops 2147483648 | bytes 8388608 | tf_op jit(solution)/shard_map/partial_sums/pallas_call | solution.py:417
  32.0 23.2 %all_to_all.10 = s16[128,16,128]{2,1,0:T(8,128)(2,1)S(1)} all-to-all(s16[128,16,128]{2,1,0:T(8,128)(2,1)S(1)} %bitcast.10), channel_id=1, replica_groups=mesh['row'=16,'col'=8] {'row','col'}, dimensions={0} | all-to-all | bytes 1048576 | tf_op jit(solution)/shard_map/all_to_all | solution.py:436
  55.2 2.2 %bricks.1 = (f32[144,128]{1,0:T(8,128)S(1)}, s16[128,128]{1,0:T(8,128)(2,1)S(1)}) custom-call(s16[2048,128]{1,0:T(8,128)(2,1)S(1)} %bitcast.11, bf16[16,2,3072]{2,1,0:T(2,128)(2,1)S(1)} %all-to-all-done.x_ref.packed_ref, f32[4,4,128]{2,1,0:T(4,128)S(1)} %get-tuple-element.26.kappa_ref), custom_call_target="tpu_custom_call" | custom-call | flops 1073741824 | bytes 1048576 | tf_op jit(solution)/shard_map/bricks/pallas_call | solution.py:437
  57.4 3.6 %collective-permute-start.1 = (s16[128,128]{1,0:T(8,128)(2,1)S(1)}, s16[128,128]{1,0:T(8,128)(2,1)S(1)}, u32[]{:S(2)}, u32[]{:S(2)}) collective-permute-start(s16[128,128]{1,0:T(8,128)(2,1)S(1)} %get-tuple-element.28), channel_id=1, source_target_pairs={{1,0},{2,1},{3,2},{4,3},{5,4},{6,5},{7,6},{9,8},{10,9},{11,10},{12... | collective-permute-start | bytes 98312 | tf_op jit(solution)/shard_map/ppermute | solution.py:352
  61.0 2.2 %collective-permute-start = (s16[128,128]{1,0:T(8,128)(2,1)S(1)}, s16[128,128]{1,0:T(8,128)(2,1)S(1)}, u32[]{:S(2)}, u32[]{:S(2)}) collective-permute-start(s16[128,128]{1,0:T(8,128)(2,1)S(1)} %get-tuple-element.28), channel_id=1, source_target_pairs={{0,1},{1,2},{2,3},{3,4},{4,5},{5,6},{6,7},{8,9},{9,10},{10,11},{11... | collective-permute-start | bytes 98312 | tf_op jit(solution)/shard_map/ppermute | solution.py:351
  63.3 0.0 collective-permute-done.1.after_ref
  63.3 5.7 %collective-permute-done.before_ref = s16[128,128]{1,0:T(8,128)(2,1)S(1)} collective-permute-done((s16[128,128]{1,0:T(8,128)(2,1)S(1)}, s16[128,128]{1,0:T(8,128)(2,1)S(1)}, u32[]{:S(2)}, u32[]{:S(2)}) %collective-permute-start) | collective-permute-done | bytes 32800 | tf_op jit(solution)/shard_map/ppermute | solution.py:351
  68.9 0.9 %prior.1 = f32[2,4,4,128]{3,2,1,0:T(4,128)} custom-call(f32[144,128]{1,0:T(8,128)S(1)} %get-tuple-element.27.own_ref, s16[128,128]{1,0:T(8,128)(2,1)S(1)} %collective-permute-done.before_ref, s16[128,128]{1,0:T(8,128)(2,1)S(1)} %collective-permute-done.1.after_ref), custom_call_target="tpu_custom_call" | custom-call | flops 16777216 | bytes 1048576 | tf_op jit(solution)/shard_map/prior/pallas_call | solution.py:456
Async XLA Ops:
  1.6 18.8 %all-to-all-start = ((bf16[16,2,3072]{2,1,0:T(2,128)(2,1)}), bf16[16,2,3072]{2,1,0:T(2,128)(2,1)S(1)}, u32[]{:S(2)}, u32[]{:S(2)}) async-start(bf16[16,2,3072]{2,1,0:T(2,128)(2,1)} %get-tuple-element.17), calls=%async_computation | async-start | bytes 393216 | tf_op jit(solution)/shard_map/all_to_all | solution.py:394
  15.1 2.0 %copy-start = (bf16[1024,2048]{1,0:T(8,128)(2,1)}, bf16[1024,2048]{1,0:T(8,128)(2,1)S(1)}, u32[]{:S(2)}) copy-start(bf16[1024,2048]{1,0:T(8,128)(2,1)S(1)} %get-tuple-element.20.hot_ref) | copy-start | bytes 12582916
  17.1 2.0 %copy-start.2 = (bf16[8,512,512]{2,1,0:T(8,128)(2,1)}, bf16[8,512,512]{2,1,0:T(8,128)(2,1)S(1)}, u32[]{:S(2)}) copy-start(bf16[8,512,512]{2,1,0:T(8,128)(2,1)S(1)} %get-tuple-element.25.leaves) | copy-start | bytes 12582916
  19.0 1.4 %copy-start.4 = (bf16[256,4096]{1,0:T(8,128)(2,1)}, bf16[256,4096]{1,0:T(8,128)(2,1)S(1)}, u32[]{:S(2)}) copy-start(bf16[256,4096]{1,0:T(8,128)(2,1)S(1)} %get-tuple-element.24.left) | copy-start | bytes 6291460
  20.4 2.2 %copy-start.1 = (bf16[1024,2048]{1,0:T(8,128)(2,1)S(1)}, bf16[1024,2048]{1,0:T(8,128)(2,1)}, u32[]{:S(2)}) copy-start(bf16[1024,2048]{1,0:T(8,128)(2,1)} %copy-done) | copy-start | bytes 12582916
  22.6 2.2 %copy-start.3 = (bf16[8,512,512]{2,1,0:T(8,128)(2,1)S(1)}, bf16[8,512,512]{2,1,0:T(8,128)(2,1)}, u32[]{:S(2)}) copy-start(bf16[8,512,512]{2,1,0:T(8,128)(2,1)} %copy-done.2) | copy-start | bytes 12582916
  24.8 1.6 %copy-start.5 = (bf16[256,4096]{1,0:T(8,128)(2,1)S(1)}, bf16[256,4096]{1,0:T(8,128)(2,1)}, u32[]{:S(2)}) copy-start(bf16[256,4096]{1,0:T(8,128)(2,1)} %copy-done.4) | copy-start | bytes 6291460
  57.4 5.9 %collective-permute-start.1 = (s16[128,128]{1,0:T(8,128)(2,1)S(1)}, s16[128,128]{1,0:T(8,128)(2,1)S(1)}, u32[]{:S(2)}, u32[]{:S(2)}) collective-permute-start(s16[128,128]{1,0:T(8,128)(2,1)S(1)} %get-tuple-element.28), channel_id=1, source_target_pairs={{1,0},{2,1},{3,2},{4,3},{5,4},{6,5},{7,6},{9,8},{10,9},{11,10},{12... | collective-permute-start | bytes 98312 | tf_op jit(solution)/shard_map/ppermute | solution.py:352
  61.0 7.9 %collective-permute-start = (s16[128,128]{1,0:T(8,128)(2,1)S(1)}, s16[128,128]{1,0:T(8,128)(2,1)S(1)}, u32[]{:S(2)}, u32[]{:S(2)}) collective-permute-start(s16[128,128]{1,0:T(8,128)(2,1)S(1)} %get-tuple-element.28), channel_id=1, source_target_pairs={{0,1},{1,2},{2,3},{3,4},{4,5},{5,6},{6,7},{8,9},{9,10},{10,11},{11... | collective-permute-start | bytes 98312 | tf_op jit(solution)/shard_map/ppermute | solution.py:351

commit v4 on v3

--- a/solution.py
+++ b/solution.py
@@ -62,62 +62,35 @@
     copies[3].wait()
 
 
-def slots_kernel(
-    perm_ref,
-    right_hbm,
-    left_hbm,
-    leaf_hbm,
-    hot_ref,
-    slot_ref,
-    place_ref,
-    right,
-    left,
-    leaves,
-    sems,
-):
-    copies = [
-        pltpu.make_async_copy(right_hbm, right, sems.at[0]),
-        pltpu.make_async_copy(left_hbm, left, sems.at[1]),
-        pltpu.make_async_copy(leaf_hbm, leaves, sems.at[2]),
-    ]
-    for copy in copies:
-        copy.start()
+def slots_kernel(perm_ref, right_hbm, rank_ref, place_ref, right, sem):
+    copy = pltpu.make_async_copy(right_hbm, right, sem)
+    copy.start()
     chunk = 256
     upto = jnp.where(iota((chunk, chunk), 0) <= iota((chunk, chunk), 1), 1.0, 0.0).astype(BF16)
     brick = iota((DEV, chunk), 0)
-    slots = iota((CAP, chunk), 0).astype(F32)
     carry = jnp.zeros((COLS * DEV, 1), F32)
     for j in range(PTS // chunk):
-        lanes = slice(j * chunk, (j + 1) * chunk)
-        masks = [
-            (perm_ref[0:1, k * PTS + j * chunk : k * PTS + (j + 1) * chunk] >> 11) == brick
-            for k in range(COLS)
-        ]
+        lanes = [slice(k * PTS + j * chunk, k * PTS + (j + 1) * chunk) for k in range(COLS)]
+        masks = [(perm_ref[0:1, at] >> 11) == brick for at in lanes]
         hot = jnp.concatenate([jnp.where(m, 1.0, 0.0).astype(BF16) for m in masks], axis=0)
-        hot_ref[:, lanes] = hot
         total = jnp.dot(hot, upto, preferred_element_type=F32) + carry
         for k in range(COLS):
             at = jnp.where(masks[k], total[k * DEV : (k + 1) * DEV], 0.0)
-            rank = jnp.sum(at, axis=0, keepdims=True) - 1.0
-            slot_ref[k * CAP : (k + 1) * CAP, lanes] = jnp.where(rank == slots, 1.0, 0.0).astype(
-                BF16
-            )
+            rank_ref[0:1, lanes[k]] = jnp.sum(at, axis=0, keepdims=True) - 1.0
         carry = total[:, chunk - 1 : chunk]
     col = lax.axis_index("col")
-    own = perm_ref[0:1, pl.ds(pl.multiple_of(col * PTS, PTS), PTS)]
-    here = slot_ref[pl.ds(pl.multiple_of(col * CAP, CAP), CAP), :]
-    hot = hot_ref[pl.ds(pl.multiple_of(col * DEV, DEV), DEV), :]
+    start = pl.multiple_of(col * PTS, PTS)
+    own = perm_ref[0:1, pl.ds(start, PTS)]
+    slot = rank_ref[0:1, pl.ds(start, PTS)] + ((col % 4) * CAP).astype(F32)
+    here = jnp.where(slot == iota((128, PTS), 0).astype(F32), 1.0, 0.0).astype(BF16)
+    hot = jnp.where((own >> 11) == iota((DEV, PTS), 0), 1.0, 0.0).astype(BF16)
     inside = own & (PTS - 1)
     place = jnp.zeros((DEV, 128), F32)
     for part in (inside & ~(NZ - 1), (inside & (NZ - 1)) + 1):
         spread = here * part.astype(F32).astype(BF16)
-        spread = jnp.concatenate(
-            [spread * jnp.where(col % 4 == g, 1.0, 0.0).astype(BF16) for g in range(4)], axis=0
-        )
         place = place + lax.dot_general(hot, spread, NT, preferred_element_type=F32)
     place_ref[...] = place
-    for copy in copies:
-        copy.wait()
+    copy.wait()
 
 
 def level_of(values):
@@ -132,24 +105,30 @@
 
 
 def send_kernel(
+    leaf_at_hbm,
+    left_hbm,
     leaf_hbm,
     x_ref,
     tile_rank_ref,
-    hot_ref,
-    slot_ref,
+    perm_ref,
+    rank_ref,
     place_ref,
     right,
+    out_ref,
     left,
     leaves,
-    out_ref,
     x_rows,
     sums,
     stage,
+    hots,
+    slots,
     leaf_at,
-    sem,
+    sems,
 ):
-    leaf_copy = pltpu.make_async_copy(leaf_hbm, leaf_at, sem)
-    leaf_copy.start()
+    pairs = ((left_hbm, left), (leaf_hbm, leaves), (leaf_at_hbm, leaf_at))
+    copies = [pltpu.make_async_copy(a, b, sems.at[i]) for i, (a, b) in enumerate(pairs)]
+    for copy in copies:
+        copy.start()
     half = TS // PTS
     for s in range(ROWS):
         b, h = divmod(s, half)
@@ -175,8 +154,16 @@
     second = jnp.sum(projected[8:16], axis=0, keepdims=True)
     by_row = jnp.where(sub < 8, first, second)
     by_row = jnp.where(sub % 8 == lane // (TILE_COLS * KMAX), by_row, 0.0).astype(BF16)
+    for k in range(COLS):
+        at = slice(k * PTS, (k + 1) * PTS)
+        hot = (perm_ref[0:1, at] >> 11) == iota((DEV, PTS), 0)
+        hots[k * DEV : (k + 1) * DEV, :] = jnp.where(hot, 1.0, 0.0).astype(BF16)
+        slot = rank_ref[0:1, at] == iota((CAP, PTS), 0).astype(F32)
+        slots[k * CAP : (k + 1) * CAP, :] = jnp.where(slot, 1.0, 0.0).astype(BF16)
+    copies[0].wait()
     sums[...] = jnp.dot(by_row, left[...], preferred_element_type=F32)
-    leaf_copy.wait()
+    copies[1].wait()
+    copies[2].wait()
     per_tile = TS // LEAF
     for l in range(NLEAF):
         i, j = leaf_at[0, l], leaf_at[1, l]
@@ -208,12 +195,12 @@
         for kk in range(4):
             k = group * 4 + kk
             a, h = divmod(k, half)
-            slot = slot_ref[k * CAP : (k + 1) * CAP, :]
+            slot = slots[k * CAP : (k + 1) * CAP, :]
             rows = [sums[8 * v + a : 8 * v + a + 1, h * PTS : (h + 1) * PTS] for v in range(NVEC)]
             highs = [row.astype(BF16) for row in rows]
             lows = [(row - high.astype(F32)).astype(BF16) for row, high in zip(rows, highs)]
             spread = jnp.concatenate([slot * row for row in highs + lows], axis=0)
-            hot = hot_ref[k * DEV : (k + 1) * DEV, :]
+            hot = hots[k * DEV : (k + 1) * DEV, :]
             part = lax.dot_general(hot, spread, NT, preferred_element_type=F32)
             parts.append(part + pltpu.roll(part, NVEC * CAP, 1))
         for v in range(NVEC):
@@ -392,46 +379,42 @@
         name="pack",
     )(*in_hbm(vectors[:, 0], kappa, cluster_perm, tile_rank[0]))
     packed = lax.all_to_all(packed, "row", 0, 0, tiled=True)
-    hot, slot, place, right, left, leaves = pl.pallas_call(
+    rank, place, right = pl.pallas_call(
         slots_kernel,
         out_shape=(
-            pltpu.VMEM((COLS * DEV, PTS), BF16),
-            pltpu.VMEM((COLS * CAP, PTS), BF16),
+            pltpu.VMEM((1, points), F32),
             pltpu.VMEM((DEV, 128), F32),
             pltpu.VMEM((terms, TS), BF16),
-            pltpu.VMEM((terms, TS), BF16),
-            pltpu.VMEM((NLEAF, LEAF, LEAF), BF16),
         ),
-        in_specs=[vmem, hbm, hbm, hbm],
-        out_specs=(vmem,) * 6,
-        scratch_shapes=[pltpu.SemaphoreType.DMA((3,))],
+        in_specs=[vmem, hbm],
+        out_specs=(vmem,) * 3,
+        scratch_shapes=[pltpu.SemaphoreType.DMA],
         compiler_params=params(16),
         cost_estimate=cost(1 << 31, 1 << 20),
         name="slots",
-    )(
-        perm,
-        *in_hbm(
-            lr_right.reshape(terms, TS), lr_left.reshape(terms, TS), leaf_values[0, 0]
-        ),
-    )
+    )(perm, *in_hbm(lr_right.reshape(terms, TS)))
     send = pl.pallas_call(
         send_kernel,
         out_shape=jax.ShapeDtypeStruct((DEV * SLAB, 128), jnp.int16),
-        in_specs=[hbm] + [vmem] * 8,
+        in_specs=[hbm] * 3 + [vmem] * 6,
         out_specs=vmem,
         scratch_shapes=[
+            pltpu.VMEM((terms, TS), BF16),
+            pltpu.VMEM((NLEAF, LEAF, LEAF), BF16),
             pltpu.VMEM((16, TS), F32),
             pltpu.VMEM((16, TS), F32),
             pltpu.VMEM((DEV * SLAB, 128), F32),
+            pltpu.VMEM((COLS * DEV, PTS), BF16),
+            pltpu.VMEM((COLS * CAP, PTS), BF16),
             pltpu.SMEM((2, NLEAF), jnp.int32),
-            pltpu.SemaphoreType.DMA,
+            pltpu.SemaphoreType.DMA((3,)),
         ],
-        compiler_params=params(16),
+        compiler_params=params(32),
         cost_estimate=cost(1 << 31, 8 << 20),
         name="partial_sums",
     )(
-        *in_hbm(leaf_places[0, 0].T),
-        *in_vmem(packed, ranks, hot, slot, place, right, left, leaves),
+        *in_hbm(leaf_places[0, 0].T, lr_left.reshape(terms, TS), leaf_values[0, 0]),
+        *in_vmem(packed, ranks, perm, rank, place, right),
     )
     got = lax.all_to_all(send.reshape(DEV, SLAB, 128), ("row", "col"), 0, 0, tiled=True)
     own, halo = pl.pallas_call(

time: 70.3 us -> 59.4 us (0.84)
  local copies, waits for them, and re-layouts: 11.2 us -> 0 us
  waiting for transfers between devices: 5.68 us -> 11.4 us
  blocking collectives: 23.2 us -> 18.4 us
    unnamed x12 -> x0, local copies, waits for them, and re-layouts: 11.2 us -> none
    all_to_all x1, waiting for transfers between devices: 0.01 us -> 5.77 us  [per_device(): packed = lax.all_to_all(packed, 'row', 0, 0, tiled=True)]
    all_to_all x1, blocking collectives: 23.2 us -> 18.4 us  [per_device(): lax.all_to_all(send.reshape(DEV, SLAB, 128), ('row', 'col'), 0, 0, tiled=...]
    pallas_call x1, Pallas kernels: 6.34 us -> 3.11 us  [per_device(): pl.pallas_call(slots_kernel, out_shape=(pltpu.VMEM((1, points), F32), plt...]
    pallas_call x1, Pallas kernels: 5.66 us -> 8.36 us  [per_device(): pl.pallas_call(send_kernel, out_shape=jax.ShapeDtypeStruct((DEV * SLAB, 1...]
  transfers between devices with their start and end apart: 3 -> 3, of which waited for: 1 -> 2; matrix products, arithmetic and copies ran while one was open for 0% -> 0% of each run, Pallas kernels for 9% -> 5%
where the time goes in v4:
time: 59.4 us; the launch traced here: 59.1 us
  blocking collectives  18.4 us (31%)
  Pallas kernels  16.2 us (27%)
  starting transfers between devices  13 us (22%)
  waiting for transfers between devices  11.4 us (19%)
    all_to_all x1, blocking collectives, per_device(): lax.all_to_all(send.reshape(DEV, SLAB, 128), ('row', 'col'), 0, 0, tiled=...  18.4 us
    pallas_call x1, Pallas kernels, per_device(): pl.pallas_call(send_kernel, out_shape=jax.ShapeDtypeStruct((DEV * SLAB, 1...  8.36 us
    all_to_all x1, starting transfers between devices, per_device(): packed = lax.all_to_all(packed, 'row', 0, 0, tiled=True)  7.16 us
    all_to_all x1, waiting for transfers between devices, per_device(): packed = lax.all_to_all(packed, 'row', 0, 0, tiled=True)  5.77 us
    ppermute x1, waiting for transfers between devices, to_both_sides(): before = lax.ppermute(array, axis, [(i, i + 1) for i in range(size - 1)])  5.67 us
    ppermute x1, starting transfers between devices, to_both_sides(): after = lax.ppermute(array, axis, [(i + 1, i) for i in range(size - 1)])  3.62 us
    pallas_call x1, Pallas kernels, per_device(): pl.pallas_call(slots_kernel, out_shape=(pltpu.VMEM((1, points), F32), plt...  3.11 us
    ppermute x1, starting transfers between devices, to_both_sides(): before = lax.ppermute(array, axis, [(i, i + 1) for i in range(size - 1)])  2.23 us
  transfers between devices with their start and end apart: 3, of which 2 were waited for; matrix products, arithmetic and copies ran while one was open for 0% of the time, Pallas kernels for 5%

profile of v4, /device:TPU:8, one launch (start us, length us, event | category | flops | bytes accessed | tf_op | source)
XLA Modules:
  0.0 59.1 jit_solution(1922412921192075865)
XLA Ops:
  0.0 1.6 %pack.1 = (bf16[16,2,3072]{2,1,0:T(2,128)(2,1)}, f32[4,4,128]{2,1,0:T(4,128)S(1)}, s32[1,16384]{1,0:T(1,128)S(1)}, s32[1,32]{1,0:T(1,128)S(1)}) custom-call(bf16[2,2048]{1,0:T(2,128)(2,1)} %bitcast.14, f32[4,4,128]{2,1,0:T(4,128)} %kappa_hbm.1, s32[1,16384]{1,0:T(1,128)} %perm_hbm.1, s32[1,32]{1,0:T(1,128)} %bitcast.16), custom_call_target="tpu_custom_call" | custom-call | tf_op jit(solution)/shard_map/pack/pallas_call | solution.py:367
  1.6 7.2 %all-to-all-start = ((bf16[16,2,3072]{2,1,0:T(2,128)(2,1)}), bf16[16,2,3072]{2,1,0:T(2,128)(2,1)S(1)}, u32[]{:S(2)}, u32[]{:S(2)}) async-start(bf16[16,2,3072]{2,1,0:T(2,128)(2,1)} %get-tuple-element.14), calls=%async_computation | async-start | bytes 393216 | tf_op jit(solution)/shard_map/all_to_all | solution.py:381
  8.8 3.1 %slots.1 = (f32[1,16384]{1,0:T(1,128)S(1)}, f32[128,128]{1,0:T(8,128)S(1)}, bf16[256,4096]{1,0:T(8,128)(2,1)S(1)}) custom-call(s32[1,16384]{1,0:T(1,128)S(1)} %get-tuple-element.16.perm_ref, bf16[256,4096]{1,0:T(8,128)(2,1)} %bitcast.17), custom_call_target="tpu_custom_call" | custom-call | flops 2147483648 | bytes 1048576 | tf_op jit(solution)/shard_map/slots/pallas_call | solution.py:382
  11.9 5.8 %all-to-all-done.x_ref.packed_ref = bf16[16,2,3072]{2,1,0:T(2,128)(2,1)S(1)} async-done(((bf16[16,2,3072]{2,1,0:T(2,128)(2,1)}), bf16[16,2,3072]{2,1,0:T(2,128)(2,1)S(1)}, u32[]{:S(2)}, u32[]{:S(2)}) %all-to-all-start) | async-done | bytes 196640 | tf_op jit(solution)/shard_map/all_to_all | solution.py:381
  17.6 8.4 %partial_sums.1 = s16[2048,128]{1,0:T(8,128)(2,1)S(1)} custom-call(s32[2,8]{1,0:T(2,128)} %bitcast.15, bf16[256,4096]{1,0:T(8,128)(2,1)} %bitcast.13, bf16[8,512,512]{2,1,0:T(8,128)(2,1)} %bitcast.12, bf16[16,2,3072]{2,1,0:T(2,128)(2,1)S(1)} %all-to-all-done.x_ref.packed_ref, s32[1,32]{1,0:T(1,128)S(1)} %get-tuple-element.15.tile_rank_ref, ...), custom_call_target="tpu_custom_call" | custom-call | flops 2147483648 | bytes 8388608 | tf_op jit(solution)/shard_map/partial_sums/pallas_call | solution.py:396
  26.0 18.4 %all_to_all.10 = s16[128,16,128]{2,1,0:T(8,128)(2,1)S(1)} all-to-all(s16[128,16,128]{2,1,0:T(8,128)(2,1)S(1)} %bitcast.10), channel_id=1, replica_groups=mesh['row'=16,'col'=8] {'row','col'}, dimensions={0} | all-to-all | bytes 1048576 | tf_op jit(solution)/shard_map/all_to_all | solution.py:419
  44.4 2.2 %bricks.1 = (f32[144,128]{1,0:T(8,128)S(1)}, s16[128,128]{1,0:T(8,128)(2,1)S(1)}) custom-call(s16[2048,128]{1,0:T(8,128)(2,1)S(1)} %bitcast.11, bf16[16,2,3072]{2,1,0:T(2,128)(2,1)S(1)} %all-to-all-done.x_ref.packed_ref, f32[4,4,128]{2,1,0:T(4,128)S(1)} %get-tuple-element.20.kappa_ref), custom_call_target="tpu_custom_call" | custom-call | flops 1073741824 | bytes 1048576 | tf_op jit(solution)/shard_map/bricks/pallas_call | solution.py:420
  46.6 3.6 %collective-permute-start.1 = (s16[128,128]{1,0:T(8,128)(2,1)S(1)}, s16[128,128]{1,0:T(8,128)(2,1)S(1)}, u32[]{:S(2)}, u32[]{:S(2)}) collective-permute-start(s16[128,128]{1,0:T(8,128)(2,1)S(1)} %get-tuple-element.22), channel_id=1, source_target_pairs={{1,0},{2,1},{3,2},{4,3},{5,4},{6,5},{7,6},{9,8},{10,9},{11,10},{12... | collective-permute-start | bytes 98312 | tf_op jit(solution)/shard_map/ppermute | solution.py:339
  50.2 2.2 %collective-permute-start = (s16[128,128]{1,0:T(8,128)(2,1)S(1)}, s16[128,128]{1,0:T(8,128)(2,1)S(1)}, u32[]{:S(2)}, u32[]{:S(2)}) collective-permute-start(s16[128,128]{1,0:T(8,128)(2,1)S(1)} %get-tuple-element.22), channel_id=1, source_target_pairs={{0,1},{1,2},{2,3},{3,4},{4,5},{5,6},{6,7},{8,9},{9,10},{10,11},{11... | collective-permute-start | bytes 98312 | tf_op jit(solution)/shard_map/ppermute | solution.py:338
  52.5 0.0 collective-permute-done.1.after_ref
  52.5 5.7 %collective-permute-done.before_ref = s16[128,128]{1,0:T(8,128)(2,1)S(1)} collective-permute-done((s16[128,128]{1,0:T(8,128)(2,1)S(1)}, s16[128,128]{1,0:T(8,128)(2,1)S(1)}, u32[]{:S(2)}, u32[]{:S(2)}) %collective-permute-start) | collective-permute-done | bytes 32800 | tf_op jit(solution)/shard_map/ppermute | solution.py:338
  58.1 0.9 %prior.1 = f32[2,4,4,128]{3,2,1,0:T(4,128)} custom-call(f32[144,128]{1,0:T(8,128)S(1)} %get-tuple-element.21.own_ref, s16[128,128]{1,0:T(8,128)(2,1)S(1)} %collective-permute-done.before_ref, s16[128,128]{1,0:T(8,128)(2,1)S(1)} %collective-permute-done.1.after_ref), custom_call_target="tpu_custom_call" | custom-call | flops 16777216 | bytes 1048576 | tf_op jit(solution)/shard_map/prior/pallas_call | solution.py:439
Async XLA Ops:
  1.6 16.1 %all-to-all-start = ((bf16[16,2,3072]{2,1,0:T(2,128)(2,1)}), bf16[16,2,3072]{2,1,0:T(2,128)(2,1)S(1)}, u32[]{:S(2)}, u32[]{:S(2)}) async-start(bf16[16,2,3072]{2,1,0:T(2,128)(2,1)} %get-tuple-element.14), calls=%async_computation | async-start | bytes 393216 | tf_op jit(solution)/shard_map/all_to_all | solution.py:381
  46.6 5.9 %collective-permute-start.1 = (s16[128,128]{1,0:T(8,128)(2,1)S(1)}, s16[128,128]{1,0:T(8,128)(2,1)S(1)}, u32[]{:S(2)}, u32[]{:S(2)}) collective-permute-start(s16[128,128]{1,0:T(8,128)(2,1)S(1)} %get-tuple-element.22), channel_id=1, source_target_pairs={{1,0},{2,1},{3,2},{4,3},{5,4},{6,5},{7,6},{9,8},{10,9},{11,10},{12... | collective-permute-start | bytes 98312 | tf_op jit(solution)/shard_map/ppermute | solution.py:339
  50.2 7.9 %collective-permute-start = (s16[128,128]{1,0:T(8,128)(2,1)S(1)}, s16[128,128]{1,0:T(8,128)(2,1)S(1)}, u32[]{:S(2)}, u32[]{:S(2)}) collective-permute-start(s16[128,128]{1,0:T(8,128)(2,1)S(1)} %get-tuple-element.22), channel_id=1, source_target_pairs={{0,1},{1,2},{2,3},{3,4},{4,5},{5,6},{6,7},{8,9},{9,10},{10,11},{11... | collective-permute-start | bytes 98312 | tf_op jit(solution)/shard_map/ppermute | solution.py:338

commit v5 on v4

--- a/solution.py
+++ b/solution.py
@@ -20,6 +20,7 @@
 TS = 4096
 CAP = 32
 DEV = ROWS * COLS
+PIECES = 2
 SLAB = 16
 F32 = jnp.float32
 BF16 = jnp.bfloat16
@@ -30,6 +31,7 @@
 KAPPA_STEPS = 8000.0
 FIELD = 3 * CX * NVEC * CY
 HALO = FIELD - 2 * NVEC * CY
+MESSAGE = HALO + 8 * CY + 16
 
 
 def iota(shape, dim):
@@ -120,15 +122,31 @@
     x_rows,
     sums,
     stage,
-    hots,
-    slots,
     leaf_at,
     sems,
 ):
-    pairs = ((left_hbm, left), (leaf_hbm, leaves), (leaf_at_hbm, leaf_at))
+    pairs = [(leaf_at_hbm, leaf_at)]
+    each, wide = NLEAF // PIECES, TS // PIECES
+    for i in range(PIECES):
+        at = pl.ds(i * wide, wide)
+        pairs.append((left_hbm.at[:, at], left.at[:, at]))
+    for i in range(PIECES):
+        at = pl.ds(i * each, each)
+        pairs.append((leaf_hbm.at[at], leaves.at[at]))
     copies = [pltpu.make_async_copy(a, b, sems.at[i]) for i, (a, b) in enumerate(pairs)]
     for copy in copies:
         copy.start()
+
+    def put(values, first_row, step):
+        none = jnp.zeros((COLS, 128), F32)
+        stage[pl.ds(first_row, COLS, stride=SLAB), :] = none
+        stage[pl.ds(first_row + COLS * SLAB, DEV - COLS, stride=SLAB), :] = values[: DEV - COLS]
+        stage[pl.ds(first_row + step, DEV, stride=SLAB), :] = values
+        at = first_row + 2 * step
+        stage[pl.ds(at, DEV - COLS, stride=SLAB), :] = values[COLS:]
+        stage[pl.ds(at + (DEV - COLS) * SLAB, COLS, stride=SLAB), :] = none
+
+    put(place_ref[...], 12, 1)
     half = TS // PTS
     for s in range(ROWS):
         b, h = divmod(s, half)
@@ -154,18 +172,15 @@
     second = jnp.sum(projected[8:16], axis=0, keepdims=True)
     by_row = jnp.where(sub < 8, first, second)
     by_row = jnp.where(sub % 8 == lane // (TILE_COLS * KMAX), by_row, 0.0).astype(BF16)
-    for k in range(COLS):
-        at = slice(k * PTS, (k + 1) * PTS)
-        hot = (perm_ref[0:1, at] >> 11) == iota((DEV, PTS), 0)
-        hots[k * DEV : (k + 1) * DEV, :] = jnp.where(hot, 1.0, 0.0).astype(BF16)
-        slot = rank_ref[0:1, at] == iota((CAP, PTS), 0).astype(F32)
-        slots[k * CAP : (k + 1) * CAP, :] = jnp.where(slot, 1.0, 0.0).astype(BF16)
+    for i in range(PIECES):
+        copies[1 + i].wait()
+        at = (slice(None), slice(i * wide, (i + 1) * wide))
+        sums[at] = jnp.dot(by_row, left[at], preferred_element_type=F32)
     copies[0].wait()
-    sums[...] = jnp.dot(by_row, left[...], preferred_element_type=F32)
-    copies[1].wait()
-    copies[2].wait()
     per_tile = TS // LEAF
     for l in range(NLEAF):
+        if l % each == 0:
+            copies[1 + PIECES + l // each].wait()
         i, j = leaf_at[0, l], leaf_at[1, l]
         from_lane = pl.multiple_of((j % per_tile) * LEAF, LEAF)
         to_lane = pl.multiple_of((i % per_tile) * LEAF, LEAF)
@@ -179,28 +194,26 @@
             sums[at] = sums[at] + near[v : v + 1]
     level, inverse = level_of(sums[...])
 
-    def put(values, first_row, step):
-        none = jnp.zeros((COLS, 128), F32)
-        stage[pl.ds(first_row, COLS, stride=SLAB), :] = none
-        stage[pl.ds(first_row + COLS * SLAB, DEV - COLS, stride=SLAB), :] = values[: DEV - COLS]
-        stage[pl.ds(first_row + step, DEV, stride=SLAB), :] = values
-        at = first_row + 2 * step
-        stage[pl.ds(at, DEV - COLS, stride=SLAB), :] = values[COLS:]
-        stage[pl.ds(at + (DEV - COLS) * SLAB, COLS, stride=SLAB), :] = none
-
-    put(place_ref[...], 12, 1)
     stage[pl.ds(15, DEV, stride=SLAB), :] = jnp.broadcast_to(level, (DEV, 128))
+    one, none = jnp.ones((), BF16), jnp.zeros((), BF16)
+
+    def numbers(count):
+        return iota((count, PTS), 0).astype(F32).astype(BF16)
+
     for group in range(2):
         parts = []
         for kk in range(4):
             k = group * 4 + kk
             a, h = divmod(k, half)
-            slot = slots[k * CAP : (k + 1) * CAP, :]
+            at = slice(k * PTS, (k + 1) * PTS)
+            slot = rank_ref[0:1, at].astype(BF16) == numbers(CAP)
+            slot = jnp.where(slot, one, none)
             rows = [sums[8 * v + a : 8 * v + a + 1, h * PTS : (h + 1) * PTS] for v in range(NVEC)]
             highs = [row.astype(BF16) for row in rows]
             lows = [(row - high.astype(F32)).astype(BF16) for row, high in zip(rows, highs)]
             spread = jnp.concatenate([slot * row for row in highs + lows], axis=0)
-            hot = hots[k * DEV : (k + 1) * DEV, :]
+            hot = (perm_ref[0:1, at] >> 11).astype(F32).astype(BF16) == numbers(DEV)
+            hot = jnp.where(hot, one, none)
             part = lax.dot_general(hot, spread, NT, preferred_element_type=F32)
             parts.append(part + pltpu.roll(part, NVEC * CAP, 1))
         for v in range(NVEC):
@@ -262,16 +275,16 @@
     level, inverse = level_of(out_ref[0:FIELD, :])
 
     def store(at, values):
-        halo_ref[at : at + values.shape[0], :] = (
-            jnp.round(values).astype(jnp.int32).astype(jnp.int16)
-        )
+        values = jnp.round(values).astype(jnp.int32).astype(jnp.int16)
+        for c in range(COLS):
+            halo_ref[c * MESSAGE + at : c * MESSAGE + at + values.shape[0], :] = values
 
     store(0, out_ref[8 : FIELD - 8, :] * inverse)
     store(HALO, out_ref[FIELD + 2 * CY : FIELD + 10 * CY, :] * KAPPA_STEPS)
     store(HALO + 8 * CY, jnp.broadcast_to(level, (16, 128)))
 
 
-def prior_kernel(own_ref, before_ref, after_ref, out_ref):
+def prior_kernel(own_ref, halo_ref, out_ref):
     my_row, my_col = lax.axis_index("row"), lax.axis_index("col")
     wide = 3 * CX
     inside_x = [
@@ -288,14 +301,16 @@
     z_at = iota((8, NZ), 1)
     none = jnp.zeros((8, NZ), F32)
     us, ks = [], []
-    for ref in (before_ref, own_ref, after_ref):
-        if ref is own_ref:
-            field = [ref[8 * x : 8 * x + 8, :] for x in range(wide)]
-            rows = [ref[FIELD + CY * x : FIELD + CY * (x + 1), :] for x in range(wide)]
+    before, after = jnp.maximum(my_col - 1, 0), jnp.minimum(my_col + 1, COLS - 1)
+    for b, c in enumerate((before, None, after)):
+        if c is None:
+            field = [own_ref[8 * x : 8 * x + 8, :] for x in range(wide)]
+            rows = [own_ref[FIELD + CY * x : FIELD + CY * (x + 1), :] for x in range(wide)]
             kappas = [6.0 + jnp.concatenate([row, row], axis=0) for row in rows]
         else:
-            got = ref[...].astype(jnp.int32).astype(F32)
-            values = got[0:HALO] * step_at(got[HALO + 8 * CY : HALO + 8 * CY + 1])
+            at = pl.multiple_of(c * MESSAGE, MESSAGE)
+            got = halo_ref[pl.ds(at, MESSAGE), :].astype(jnp.int32).astype(F32)
+            values = got[0:HALO] * (step_at(got[HALO + 8 * CY : HALO + 8 * CY + 1]) * inside_y[b])
             field = [values[8 * x : 8 * x + 8] for x in range(wide - 2)]
             field = [none] + field + [none]
             values = got[HALO : HALO + 8 * CY] * (1.0 / KAPPA_STEPS) + 6.0
@@ -331,13 +346,6 @@
     for x in range(CX):
         for v in range(NVEC):
             out_ref[v, x] = us[1][CX + x][v * CY : (v + 1) * CY]
-
-
-def to_both_sides(array, axis):
-    size = lax.axis_size(axis)
-    before = lax.ppermute(array, axis, [(i, i + 1) for i in range(size - 1)])
-    after = lax.ppermute(array, axis, [(i + 1, i) for i in range(size - 1)])
-    return before, after
 
 
 def cost(flops, size):
@@ -404,10 +412,8 @@
             pltpu.VMEM((16, TS), F32),
             pltpu.VMEM((16, TS), F32),
             pltpu.VMEM((DEV * SLAB, 128), F32),
-            pltpu.VMEM((COLS * DEV, PTS), BF16),
-            pltpu.VMEM((COLS * CAP, PTS), BF16),
             pltpu.SMEM((2, NLEAF), jnp.int32),
-            pltpu.SemaphoreType.DMA((3,)),
+            pltpu.SemaphoreType.DMA((1 + 2 * PIECES,)),
         ],
         compiler_params=params(32),
         cost_estimate=cost(1 << 31, 8 << 20),
@@ -421,7 +427,7 @@
         bricks_kernel,
         out_shape=(
             pltpu.VMEM((FIELD + 3 * CX * CY, NZ), F32),
-            pltpu.VMEM((HALO + 8 * CY + 16, NZ), jnp.int16),
+            pltpu.VMEM((COLS * MESSAGE, NZ), jnp.int16),
         ),
         in_specs=[vmem] * 3,
         out_specs=(vmem,) * 2,
@@ -435,16 +441,16 @@
         cost_estimate=cost(1 << 30, 1 << 20),
         name="bricks",
     )(got.reshape(DEV * SLAB, 128), packed, kappa_own)
-    before, after = to_both_sides(halo, "col")
+    halo = lax.all_to_all(halo.reshape(COLS, MESSAGE, NZ), "col", 0, 0, tiled=True)
     return pl.pallas_call(
         prior_kernel,
         out_shape=jax.ShapeDtypeStruct((NVEC, CX, CY, NZ), F32),
-        in_specs=[vmem] * 3,
+        in_specs=[vmem] * 2,
         out_specs=vmem,
         compiler_params=params(8),
         cost_estimate=cost(1 << 24, 1 << 20),
         name="prior",
-    )(own, before, after)
+    )(own, halo.reshape(COLS * MESSAGE, NZ))
 
 
 def solution(mesh):

time: 59.4 us -> 57.3 us (0.965)
  the two profiles are of different devices: /device:TPU:8 before, /device:TPU:0 now
where the time goes in v5:
time: 57.3 us; the launch traced here: 57 us
  blocking collectives  28.6 us (50%)
  Pallas kernels  14.5 us (25%)
  starting transfers between devices  8.14 us (14%)
  waiting for transfers between devices  5.77 us (10%)
    all_to_all x1, blocking collectives, per_device(): lax.all_to_all(send.reshape(DEV, SLAB, 128), ('row', 'col'), 0, 0, tiled=...  18.4 us
    all_to_all x1, blocking collectives, per_device(): lax.all_to_all(halo.reshape(COLS, MESSAGE, NZ), 'col', 0, 0, tiled=True)  10.2 us
    all_to_all x1, starting transfers between devices, per_device(): packed = lax.all_to_all(packed, 'row', 0, 0, tiled=True)  8.14 us
    pallas_call x1, Pallas kernels, per_device(): pl.pallas_call(send_kernel, out_shape=jax.ShapeDtypeStruct((DEV * SLAB, 1...  6.66 us
    all_to_all x1, waiting for transfers between devices, per_device(): packed = lax.all_to_all(packed, 'row', 0, 0, tiled=True)  5.77 us
    pallas_call x1, Pallas kernels, per_device(): pl.pallas_call(slots_kernel, out_shape=(pltpu.VMEM((1, points), F32), plt...  3.11 us
    pallas_call x1, Pallas kernels, per_device(): pl.pallas_call(bricks_kernel, out_shape=(pltpu.VMEM((FIELD + 3 * CX * CY,...  2.22 us
    pallas_call x1, Pallas kernels, per_device(): pl.pallas_call(pack_kernel, out_shape=(pltpu.VMEM(packed_shape, BF16), pl...  1.58 us
  transfers between devices with their start and end apart: 1, of which 1 were waited for; matrix products, arithmetic and copies ran while one was open for 0% of the time, Pallas kernels for 5%

profile of v5, /device:TPU:0, one launch (start us, length us, event | category | flops | bytes accessed | tf_op | source)
XLA Modules:
  0.0 57.0 jit_solution(9714534883247424415)
XLA Ops:
  0.0 1.6 %pack.1 = (bf16[16,2,3072]{2,1,0:T(2,128)(2,1)}, f32[4,4,128]{2,1,0:T(4,128)S(1)}, s32[1,16384]{1,0:T(1,128)S(1)}, s32[1,32]{1,0:T(1,128)S(1)}) custom-call(bf16[2,2048]{1,0:T(2,128)(2,1)} %bitcast.18, f32[4,4,128]{2,1,0:T(4,128)} %kappa_hbm.1, s32[1,16384]{1,0:T(1,128)} %perm_hbm.1, s32[1,32]{1,0:T(1,128)} %bitcast.20), custom_call_target="tpu_custom_call" | custom-call | tf_op jit(solution)/shard_map/pack/pallas_call | solution.py:375
  1.6 8.1 %all-to-all-start = ((bf16[16,2,3072]{2,1,0:T(2,128)(2,1)}), bf16[16,2,3072]{2,1,0:T(2,128)(2,1)S(1)}, u32[]{:S(2)}, u32[]{:S(2)}) async-start(bf16[16,2,3072]{2,1,0:T(2,128)(2,1)} %get-tuple-element.14), calls=%async_computation | async-start | bytes 393216 | tf_op jit(solution)/shard_map/all_to_all | solution.py:389
  9.7 3.1 %slots.1 = (f32[1,16384]{1,0:T(1,128)S(1)}, f32[128,128]{1,0:T(8,128)S(1)}, bf16[256,4096]{1,0:T(8,128)(2,1)S(1)}) custom-call(s32[1,16384]{1,0:T(1,128)S(1)} %get-tuple-element.16.perm_ref, bf16[256,4096]{1,0:T(8,128)(2,1)} %bitcast.21), custom_call_target="tpu_custom_call" | custom-call | flops 2147483648 | bytes 1048576 | tf_op jit(solution)/shard_map/slots/pallas_call | solution.py:390
  12.9 5.8 %all-to-all-done.x_ref.packed_ref = bf16[16,2,3072]{2,1,0:T(2,128)(2,1)S(1)} async-done(((bf16[16,2,3072]{2,1,0:T(2,128)(2,1)}), bf16[16,2,3072]{2,1,0:T(2,128)(2,1)S(1)}, u32[]{:S(2)}, u32[]{:S(2)}) %all-to-all-start) | async-done | bytes 196640 | tf_op jit(solution)/shard_map/all_to_all | solution.py:389
  18.6 6.7 %partial_sums.1 = s16[2048,128]{1,0:T(8,128)(2,1)S(1)} custom-call(s32[2,8]{1,0:T(2,128)} %bitcast.19, bf16[256,4096]{1,0:T(8,128)(2,1)} %bitcast.17, bf16[8,512,512]{2,1,0:T(8,128)(2,1)} %bitcast.16, bf16[16,2,3072]{2,1,0:T(2,128)(2,1)S(1)} %all-to-all-done.x_ref.packed_ref, s32[1,32]{1,0:T(1,128)S(1)} %get-tuple-element.15.tile_rank_ref, ...), custom_call_target="tpu_custom_call" | custom-call | flops 2147483648 | bytes 8388608 | tf_op jit(solution)/shard_map/partial_sums/pallas_call | solution.py:404
  25.3 18.4 %all_to_all.15 = s16[128,16,128]{2,1,0:T(8,128)(2,1)S(1)} all-to-all(s16[128,16,128]{2,1,0:T(8,128)(2,1)S(1)} %bitcast.12), channel_id=1, replica_groups=mesh['row'=16,'col'=8] {'row','col'}, dimensions={0} | all-to-all | bytes 1048576 | tf_op jit(solution)/shard_map/all_to_all | solution.py:425
  43.7 2.2 %bricks.1 = (f32[144,128]{1,0:T(8,128)S(1)}, s16[1024,128]{1,0:T(8,128)(2,1)S(1)}) custom-call(s16[2048,128]{1,0:T(8,128)(2,1)S(1)} %bitcast.14, bf16[16,2,3072]{2,1,0:T(2,128)(2,1)S(1)} %all-to-all-done.x_ref.packed_ref, f32[4,4,128]{2,1,0:T(4,128)S(1)} %get-tuple-element.20.kappa_ref), custom_call_target="tpu_custom_call" | custom-call | flops 1073741824 | bytes 1048576 | tf_op jit(solution)/shard_map/bricks/pallas_call | solution.py:426
  46.0 10.2 %all_to_all.16 = s16[8,128,128]{2,1,0:T(8,128)(2,1)S(1)} all-to-all(s16[8,128,128]{2,1,0:T(8,128)(2,1)S(1)} %bitcast.15), channel_id=1, replica_groups=mesh['row'=16,'col'=8] {'col'}, dimensions={0} | all-to-all | bytes 524288 | tf_op jit(solution)/shard_map/all_to_all | solution.py:444
  56.1 0.9 %prior.1 = f32[2,4,4,128]{3,2,1,0:T(4,128)} custom-call(f32[144,128]{1,0:T(8,128)S(1)} %get-tuple-element.21.own_ref, s16[1024,128]{1,0:T(8,128)(2,1)S(1)} %bitcast.13), custom_call_target="tpu_custom_call" | custom-call | flops 16777216 | bytes 1048576 | tf_op jit(solution)/shard_map/prior/pallas_call | solution.py:445
Async XLA Ops:
  1.6 17.0 %all-to-all-start = ((bf16[16,2,3072]{2,1,0:T(2,128)(2,1)}), bf16[16,2,3072]{2,1,0:T(2,128)(2,1)S(1)}, u32[]{:S(2)}, u32[]{:S(2)}) async-start(bf16[16,2,3072]{2,1,0:T(2,128)(2,1)} %get-tuple-element.14), calls=%async_computation | async-start | bytes 393216 | tf_op jit(solution)/shard_map/all_to_all | solution.py:389

commit v6 on v5

--- a/solution.py
+++ b/solution.py
@@ -275,16 +275,16 @@
     level, inverse = level_of(out_ref[0:FIELD, :])
 
     def store(at, values):
-        values = jnp.round(values).astype(jnp.int32).astype(jnp.int16)
-        for c in range(COLS):
-            halo_ref[c * MESSAGE + at : c * MESSAGE + at + values.shape[0], :] = values
+        halo_ref[at : at + values.shape[0], :] = (
+            jnp.round(values).astype(jnp.int32).astype(jnp.int16)
+        )
 
     store(0, out_ref[8 : FIELD - 8, :] * inverse)
     store(HALO, out_ref[FIELD + 2 * CY : FIELD + 10 * CY, :] * KAPPA_STEPS)
     store(HALO + 8 * CY, jnp.broadcast_to(level, (16, 128)))
 
 
-def prior_kernel(own_ref, halo_ref, out_ref):
+def prior_kernel(own_ref, even_ref, odd_ref, out_ref):
     my_row, my_col = lax.axis_index("row"), lax.axis_index("col")
     wide = 3 * CX
     inside_x = [
@@ -301,15 +301,15 @@
     z_at = iota((8, NZ), 1)
     none = jnp.zeros((8, NZ), F32)
     us, ks = [], []
-    before, after = jnp.maximum(my_col - 1, 0), jnp.minimum(my_col + 1, COLS - 1)
-    for b, c in enumerate((before, None, after)):
-        if c is None:
+    even, odd = (ref[...].astype(jnp.int32).astype(F32) for ref in (even_ref, odd_ref))
+    at_even = jnp.broadcast_to(my_col % 2, (MESSAGE, NZ)) == 0
+    before, after = jnp.where(at_even, odd, even), jnp.where(at_even, even, odd)
+    for b, got in enumerate((before, None, after)):
+        if got is None:
             field = [own_ref[8 * x : 8 * x + 8, :] for x in range(wide)]
             rows = [own_ref[FIELD + CY * x : FIELD + CY * (x + 1), :] for x in range(wide)]
             kappas = [6.0 + jnp.concatenate([row, row], axis=0) for row in rows]
         else:
-            at = pl.multiple_of(c * MESSAGE, MESSAGE)
-            got = halo_ref[pl.ds(at, MESSAGE), :].astype(jnp.int32).astype(F32)
             values = got[0:HALO] * (step_at(got[HALO + 8 * CY : HALO + 8 * CY + 1]) * inside_y[b])
             field = [values[8 * x : 8 * x + 8] for x in range(wide - 2)]
             field = [none] + field + [none]
@@ -346,6 +346,11 @@
     for x in range(CX):
         for v in range(NVEC):
             out_ref[v, x] = us[1][CX + x][v * CY : (v + 1) * CY]
+
+
+def swapped(array, axis, first):
+    pairs = [(i, i + 1) for i in range(first, lax.axis_size(axis) - 1, 2)]
+    return lax.ppermute(array, axis, pairs + [(b, a) for a, b in pairs])
 
 
 def cost(flops, size):
@@ -427,7 +432,7 @@
         bricks_kernel,
         out_shape=(
             pltpu.VMEM((FIELD + 3 * CX * CY, NZ), F32),
-            pltpu.VMEM((COLS * MESSAGE, NZ), jnp.int16),
+            pltpu.VMEM((MESSAGE, NZ), jnp.int16),
         ),
         in_specs=[vmem] * 3,
         out_specs=(vmem,) * 2,
@@ -441,16 +446,17 @@
         cost_estimate=cost(1 << 30, 1 << 20),
         name="bricks",
     )(got.reshape(DEV * SLAB, 128), packed, kappa_own)
-    halo = lax.all_to_all(halo.reshape(COLS, MESSAGE, NZ), "col", 0, 0, tiled=True)
+    odd = swapped(halo, "col", 1)
+    even = swapped(halo, "col", 0)
     return pl.pallas_call(
         prior_kernel,
         out_shape=jax.ShapeDtypeStruct((NVEC, CX, CY, NZ), F32),
-        in_specs=[vmem] * 2,
+        in_specs=[vmem] * 3,
         out_specs=vmem,
         compiler_params=params(8),
         cost_estimate=cost(1 << 24, 1 << 20),
         name="prior",
-    )(own, halo.reshape(COLS * MESSAGE, NZ))
+    )(own, even, odd)
 
 
 def solution(mesh):

time: 57.3 us -> 54 us (0.942)
  the two profiles are of different devices: /device:TPU:0 before, /device:TPU:8 now
where the time goes in v6:
time: 54 us; the launch traced here: 53.7 us
  blocking collectives  18.4 us (34%)
  Pallas kernels  14.5 us (27%)
  starting transfers between devices  10.9 us (20%)
  waiting for transfers between devices  9.97 us (18%)
    all_to_all x1, blocking collectives, per_device(): lax.all_to_all(send.reshape(DEV, SLAB, 128), ('row', 'col'), 0, 0, tiled=...  18.4 us
    all_to_all x1, starting transfers between devices, per_device(): packed = lax.all_to_all(packed, 'row', 0, 0, tiled=True)  7.16 us
    pallas_call x1, Pallas kernels, per_device(): pl.pallas_call(send_kernel, out_shape=jax.ShapeDtypeStruct((DEV * SLAB, 1...  6.67 us
    all_to_all x1, waiting for transfers between devices, per_device(): packed = lax.all_to_all(packed, 'row', 0, 0, tiled=True)  5.77 us
    ppermute x2, waiting for transfers between devices, swapped(): return lax.ppermute(array, axis, pairs + [(b, a) for a, b in pairs])  4.2 us
    ppermute x2, starting transfers between devices, swapped(): return lax.ppermute(array, axis, pairs + [(b, a) for a, b in pairs])  3.7 us
    pallas_call x1, Pallas kernels, per_device(): pl.pallas_call(slots_kernel, out_shape=(pltpu.VMEM((1, points), F32), plt...  3.11 us
    pallas_call x1, Pallas kernels, per_device(): pl.pallas_call(bricks_kernel, out_shape=(pltpu.VMEM((FIELD + 3 * CX * CY,...  2.2 us
  transfers between devices with their start and end apart: 3, of which 2 were waited for; matrix products, arithmetic and copies ran while one was open for 0% of the time, Pallas kernels for 6%

profile of v6, /device:TPU:8, one launch (start us, length us, event | category | flops | bytes accessed | tf_op | source)
XLA Modules:
  0.0 53.7 jit_solution(16537786477942943186)
XLA Ops:
  0.0 1.6 %pack.1 = (bf16[16,2,3072]{2,1,0:T(2,128)(2,1)}, f32[4,4,128]{2,1,0:T(4,128)S(1)}, s32[1,16384]{1,0:T(1,128)S(1)}, s32[1,32]{1,0:T(1,128)S(1)}) custom-call(bf16[2,2048]{1,0:T(2,128)(2,1)} %bitcast.14, f32[4,4,128]{2,1,0:T(4,128)} %kappa_hbm.1, s32[1,16384]{1,0:T(1,128)} %perm_hbm.1, s32[1,32]{1,0:T(1,128)} %bitcast.16), custom_call_target="tpu_custom_call" | custom-call | tf_op jit(solution)/shard_map/pack/pallas_call | solution.py:380
  1.6 7.2 %all-to-all-start = ((bf16[16,2,3072]{2,1,0:T(2,128)(2,1)}), bf16[16,2,3072]{2,1,0:T(2,128)(2,1)S(1)}, u32[]{:S(2)}, u32[]{:S(2)}) async-start(bf16[16,2,3072]{2,1,0:T(2,128)(2,1)} %get-tuple-element.14), calls=%async_computation | async-start | bytes 393216 | tf_op jit(solution)/shard_map/all_to_all | solution.py:394
  8.8 3.1 %slots.1 = (f32[1,16384]{1,0:T(1,128)S(1)}, f32[128,128]{1,0:T(8,128)S(1)}, bf16[256,4096]{1,0:T(8,128)(2,1)S(1)}) custom-call(s32[1,16384]{1,0:T(1,128)S(1)} %get-tuple-element.16.perm_ref, bf16[256,4096]{1,0:T(8,128)(2,1)} %bitcast.17), custom_call_target="tpu_custom_call" | custom-call | flops 2147483648 | bytes 1048576 | tf_op jit(solution)/shard_map/slots/pallas_call | solution.py:395
  11.9 5.8 %all-to-all-done.x_ref.packed_ref = bf16[16,2,3072]{2,1,0:T(2,128)(2,1)S(1)} async-done(((bf16[16,2,3072]{2,1,0:T(2,128)(2,1)}), bf16[16,2,3072]{2,1,0:T(2,128)(2,1)S(1)}, u32[]{:S(2)}, u32[]{:S(2)}) %all-to-all-start) | async-done | bytes 196640 | tf_op jit(solution)/shard_map/all_to_all | solution.py:394
  17.6 6.7 %partial_sums.1 = s16[2048,128]{1,0:T(8,128)(2,1)S(1)} custom-call(s32[2,8]{1,0:T(2,128)} %bitcast.15, bf16[256,4096]{1,0:T(8,128)(2,1)} %bitcast.13, bf16[8,512,512]{2,1,0:T(8,128)(2,1)} %bitcast.12, bf16[16,2,3072]{2,1,0:T(2,128)(2,1)S(1)} %all-to-all-done.x_ref.packed_ref, s32[1,32]{1,0:T(1,128)S(1)} %get-tuple-element.15.tile_rank_ref, ...), custom_call_target="tpu_custom_call" | custom-call | flops 2147483648 | bytes 8388608 | tf_op jit(solution)/shard_map/partial_sums/pallas_call | solution.py:409
  24.3 18.4 %all_to_all.10 = s16[128,16,128]{2,1,0:T(8,128)(2,1)S(1)} all-to-all(s16[128,16,128]{2,1,0:T(8,128)(2,1)S(1)} %bitcast.10), channel_id=1, replica_groups=mesh['row'=16,'col'=8] {'row','col'}, dimensions={0} | all-to-all | bytes 1048576 | tf_op jit(solution)/shard_map/all_to_all | solution.py:430
  42.7 2.2 %bricks.1 = (f32[144,128]{1,0:T(8,128)S(1)}, s16[128,128]{1,0:T(8,128)(2,1)S(1)}) custom-call(s16[2048,128]{1,0:T(8,128)(2,1)S(1)} %bitcast.11, bf16[16,2,3072]{2,1,0:T(2,128)(2,1)S(1)} %all-to-all-done.x_ref.packed_ref, f32[4,4,128]{2,1,0:T(4,128)S(1)} %get-tuple-element.20.kappa_ref), custom_call_target="tpu_custom_call" | custom-call | flops 1073741824 | bytes 1048576 | tf_op jit(solution)/shard_map/bricks/pallas_call | solution.py:431
  44.9 3.6 %collective-permute-start.1 = (s16[128,128]{1,0:T(8,128)(2,1)S(1)}, s16[128,128]{1,0:T(8,128)(2,1)S(1)}, u32[]{:S(2)}, u32[]{:S(2)}) collective-permute-start(s16[128,128]{1,0:T(8,128)(2,1)S(1)} %get-tuple-element.22), channel_id=1, source_target_pairs={{1,2},{3,4},{5,6},{2,1},{4,3},{6,5},{9,10},{11,12},{13,14},{10,9},... | collective-permute-start | bytes 98312 | tf_op jit(solution)/shard_map/ppermute | solution.py:353
  48.5 0.1 collective-permute-start
  48.6 4.2 %collective-permute-done.1.odd_ref = s16[128,128]{1,0:T(8,128)(2,1)S(1)} collective-permute-done((s16[128,128]{1,0:T(8,128)(2,1)S(1)}, s16[128,128]{1,0:T(8,128)(2,1)S(1)}, u32[]{:S(2)}, u32[]{:S(2)}) %collective-permute-start.1) | collective-permute-done | bytes 32800 | tf_op jit(solution)/shard_map/ppermute | solution.py:353
  52.8 0.0 collective-permute-done.even_ref
  52.8 0.9 %prior.1 = f32[2,4,4,128]{3,2,1,0:T(4,128)} custom-call(f32[144,128]{1,0:T(8,128)S(1)} %get-tuple-element.21.own_ref, s16[128,128]{1,0:T(8,128)(2,1)S(1)} %collective-permute-done.even_ref, s16[128,128]{1,0:T(8,128)(2,1)S(1)} %collective-permute-done.1.odd_ref), custom_call_target="tpu_custom_call" | custom-call | flops 16777216 | bytes 1048576 | tf_op jit(solution)/shard_map/prior/pallas_call | solution.py:451
Async XLA Ops:
  1.6 16.1 %all-to-all-start = ((bf16[16,2,3072]{2,1,0:T(2,128)(2,1)}), bf16[16,2,3072]{2,1,0:T(2,128)(2,1)S(1)}, u32[]{:S(2)}, u32[]{:S(2)}) async-start(bf16[16,2,3072]{2,1,0:T(2,128)(2,1)} %get-tuple-element.14), calls=%async_computation | async-start | bytes 393216 | tf_op jit(solution)/shard_map/all_to_all | solution.py:394
  44.9 7.9 %collective-permute-start.1 = (s16[128,128]{1,0:T(8,128)(2,1)S(1)}, s16[128,128]{1,0:T(8,128)(2,1)S(1)}, u32[]{:S(2)}, u32[]{:S(2)}) collective-permute-start(s16[128,128]{1,0:T(8,128)(2,1)S(1)} %get-tuple-element.22), channel_id=1, source_target_pairs={{1,2},{3,4},{5,6},{2,1},{4,3},{6,5},{9,10},{11,12},{13,14},{10,9},... | collective-permute-start | bytes 98312 | tf_op jit(solution)/shard_map/ppermute | solution.py:353
  48.5 4.3 %collective-permute-start = (s16[128,128]{1,0:T(8,128)(2,1)S(1)}, s16[128,128]{1,0:T(8,128)(2,1)S(1)}, u32[]{:S(2)}, u32[]{:S(2)}) collective-permute-start(s16[128,128]{1,0:T(8,128)(2,1)S(1)} %get-tuple-element.22), channel_id=1, source_target_pairs={{0,1},{2,3},{4,5},{6,7},{1,0},{3,2},{5,4},{7,6},{8,9},{10,11},{12,... | collective-permute-start | bytes 98312 | tf_op jit(solution)/shard_map/ppermute | solution.py:353

commit v7 on v6

--- a/solution.py
+++ b/solution.py
@@ -21,6 +21,7 @@
 CAP = 32
 DEV = ROWS * COLS
 PIECES = 2
+LEAF_PIECES = ((0, 2), (2, 4), (4, 6), (6, 8))
 SLAB = 16
 F32 = jnp.float32
 BF16 = jnp.bfloat16
@@ -126,19 +127,20 @@
     sems,
 ):
     pairs = [(leaf_at_hbm, leaf_at)]
-    each, wide = NLEAF // PIECES, TS // PIECES
+    wide = TS // PIECES
     for i in range(PIECES):
         at = pl.ds(i * wide, wide)
         pairs.append((left_hbm.at[:, at], left.at[:, at]))
-    for i in range(PIECES):
-        at = pl.ds(i * each, each)
+    for first, last in LEAF_PIECES:
+        at = pl.ds(first, last - first)
         pairs.append((leaf_hbm.at[at], leaves.at[at]))
     copies = [pltpu.make_async_copy(a, b, sems.at[i]) for i, (a, b) in enumerate(pairs)]
     for copy in copies:
         copy.start()
 
     def put(values, first_row, step):
-        none = jnp.zeros((COLS, 128), F32)
+        values = values.astype(jnp.int32)
+        none = jnp.zeros((COLS, 128), jnp.int32)
         stage[pl.ds(first_row, COLS, stride=SLAB), :] = none
         stage[pl.ds(first_row + COLS * SLAB, DEV - COLS, stride=SLAB), :] = values[: DEV - COLS]
         stage[pl.ds(first_row + step, DEV, stride=SLAB), :] = values
@@ -146,7 +148,6 @@
         stage[pl.ds(at, DEV - COLS, stride=SLAB), :] = values[COLS:]
         stage[pl.ds(at + (DEV - COLS) * SLAB, COLS, stride=SLAB), :] = none
 
-    put(place_ref[...], 12, 1)
     half = TS // PTS
     for s in range(ROWS):
         b, h = divmod(s, half)
@@ -179,8 +180,9 @@
     copies[0].wait()
     per_tile = TS // LEAF
     for l in range(NLEAF):
-        if l % each == 0:
-            copies[1 + PIECES + l // each].wait()
+        for n, (first, _) in enumerate(LEAF_PIECES):
+            if l == first:
+                copies[1 + PIECES + n].wait()
         i, j = leaf_at[0, l], leaf_at[1, l]
         from_lane = pl.multiple_of((j % per_tile) * LEAF, LEAF)
         to_lane = pl.multiple_of((i % per_tile) * LEAF, LEAF)
@@ -192,9 +194,9 @@
         for v in range(NVEC):
             at = (pl.ds(8 * v + i // per_tile, 1), pl.ds(to_lane, LEAF))
             sums[at] = sums[at] + near[v : v + 1]
+    put(place_ref[...], 12, 1)
     level, inverse = level_of(sums[...])
-
-    stage[pl.ds(15, DEV, stride=SLAB), :] = jnp.broadcast_to(level, (DEV, 128))
+    stage[pl.ds(15, DEV, stride=SLAB), :] = jnp.broadcast_to(level.astype(jnp.int32), (DEV, 128))
     one, none = jnp.ones((), BF16), jnp.zeros((), BF16)
 
     def numbers(count):
@@ -219,11 +221,11 @@
         for v in range(NVEC):
             values = jnp.concatenate([p[:, v * CAP : (v + 1) * CAP] for p in parts], axis=1)
             put(jnp.round(values * inverse), group * 2 + v, 4)
-    out_ref[...] = stage[...].astype(jnp.int32).astype(jnp.int16)
+    out_ref[...] = stage[...].astype(jnp.int16)
 
 
 def bricks_kernel(
-    got_ref, packed_ref, kappa_ref, out_ref, halo_ref, sums, wheres, at_cells, hots
+    got_ref, packed_ref, kappa_ref, out_ref, halo_ref, sums, wheres, at_cells
 ):
     for r in range(ROWS):
         for g in range(2):
@@ -241,25 +243,30 @@
         at_cells[g] = cell
         wheres[g] = place - cell * NZ
     sub = iota((8, 128), 0)
-    z_row = iota((NZ, 128), 0).astype(F32)
+    z_row = iota((NZ, 128), 0).astype(F32).astype(BF16)
+    one, none = jnp.ones((), BF16), jnp.zeros((), BF16)
     for j in range(3):
-        for r in range(ROWS):
-            for g in range(2):
-                lanes = slice((r * 2 + g) * 128, (r * 2 + g + 1) * 128)
+        both = jnp.zeros((64, NZ), F32)
+        for some in range(0, ROWS, 4):
+            cells, heights = [], []
+            for r, g in ((r, g) for r in range(some, some + 4) for g in range(2)):
                 at = r * SLAB + j * 4 + g * 2
                 pair = jnp.where(sub < 4, sums[at : at + 1, :], sums[at + 1 : at + 2, :])
                 high = pair.astype(BF16).astype(F32)
                 low = pair - high
                 p = r * SLAB + 12 + j
                 cell = at_cells[g, p : p + 1, :]
-                z_at = wheres[g, p : p + 1, :]
                 wanted = [cell == (x * CY + sub % CY).astype(F32) for x in range(CX)]
-                rows = jnp.concatenate(
-                    [jnp.where(w, part, 0.0) for part in (high, low) for w in wanted], axis=0
-                )
-                hots[0, 0:64, lanes] = rows.astype(BF16)
-                hots[1, :, lanes] = jnp.where(z_at == z_row, 1.0, 0.0).astype(BF16)
-        both = lax.dot_general(hots[0, 0:64, :], hots[1], NT, preferred_element_type=F32)
+                rows = [jnp.where(w, part, 0.0) for part in (high, low) for w in wanted]
+                cells.append(jnp.concatenate(rows, axis=0).astype(BF16))
+                z_at = wheres[g, p : p + 1, :].astype(BF16)
+                heights.append(jnp.where(z_at == z_row, one, none))
+            both = both + lax.dot_general(
+                jnp.concatenate(cells, axis=1),
+                jnp.concatenate(heights, axis=1),
+                NT,
+                preferred_element_type=F32,
+            )
         out_ref[j * 32 : (j + 1) * 32, :] = both[0:32] + both[32:64]
     my_row = lax.axis_index("row")
     half = CX * CY // NVEC
@@ -416,9 +423,9 @@
             pltpu.VMEM((NLEAF, LEAF, LEAF), BF16),
             pltpu.VMEM((16, TS), F32),
             pltpu.VMEM((16, TS), F32),
-            pltpu.VMEM((DEV * SLAB, 128), F32),
+            pltpu.VMEM((DEV * SLAB, 128), jnp.int32),
             pltpu.SMEM((2, NLEAF), jnp.int32),
-            pltpu.SemaphoreType.DMA((1 + 2 * PIECES,)),
+            pltpu.SemaphoreType.DMA((1 + PIECES + len(LEAF_PIECES),)),
         ],
         compiler_params=params(32),
         cost_estimate=cost(1 << 31, 8 << 20),
@@ -440,7 +447,6 @@
             pltpu.VMEM((ROWS * SLAB, 128), F32),
             pltpu.VMEM((2, ROWS * SLAB, 128), F32),
             pltpu.VMEM((2, ROWS * SLAB, 128), F32),
-            pltpu.VMEM((2, NZ, 4096), BF16),
         ],
         compiler_params=params(16),
         cost_estimate=cost(1 << 30, 1 << 20),

time: 54 us -> 53.3 us (0.987)
  Pallas kernels: 14.5 us -> 13.8 us
    pallas_call x1, Pallas kernels: 2.2 us -> 1.49 us  [per_device(): pl.pallas_call(bricks_kernel, out_shape=(pltpu.VMEM((FIELD + 3 * CX * CY,...]
where the time goes in v7:
time: 53.3 us; the launch traced here: 53 us
  blocking collectives  18.4 us (35%)
  Pallas kernels  13.8 us (26%)
  starting transfers between devices  10.9 us (20%)
  waiting for transfers between devices  9.97 us (19%)
    all_to_all x1, blocking collectives, per_device(): lax.all_to_all(send.reshape(DEV, SLAB, 128), ('row', 'col'), 0, 0, tiled=...  18.4 us
    all_to_all x1, starting transfers between devices, per_device(): packed = lax.all_to_all(packed, 'row', 0, 0, tiled=True)  7.16 us
    pallas_call x1, Pallas kernels, per_device(): pl.pallas_call(send_kernel, out_shape=jax.ShapeDtypeStruct((DEV * SLAB, 1...  6.68 us
    all_to_all x1, waiting for transfers between devices, per_device(): packed = lax.all_to_all(packed, 'row', 0, 0, tiled=True)  5.77 us
    ppermute x2, waiting for transfers between devices, swapped(): return lax.ppermute(array, axis, pairs + [(b, a) for a, b in pairs])  4.2 us
    ppermute x2, starting transfers between devices, swapped(): return lax.ppermute(array, axis, pairs + [(b, a) for a, b in pairs])  3.7 us
    pallas_call x1, Pallas kernels, per_device(): pl.pallas_call(slots_kernel, out_shape=(pltpu.VMEM((1, points), F32), plt...  3.11 us
    pallas_call x1, Pallas kernels, per_device(): pl.pallas_call(pack_kernel, out_shape=(pltpu.VMEM(packed_shape, BF16), pl...  1.57 us
  transfers between devices with their start and end apart: 3, of which 2 were waited for; matrix products, arithmetic and copies ran while one was open for 0% of the time, Pallas kernels for 6%

profile of v7, /device:TPU:8, one launch (start us, length us, event | category | flops | bytes accessed | tf_op | source)
XLA Modules:
  0.0 53.0 jit_solution(4086783746719708782)
XLA Ops:
  0.0 1.6 %pack.1 = (bf16[16,2,3072]{2,1,0:T(2,128)(2,1)}, f32[4,4,128]{2,1,0:T(4,128)S(1)}, s32[1,16384]{1,0:T(1,128)S(1)}, s32[1,32]{1,0:T(1,128)S(1)}) custom-call(bf16[2,2048]{1,0:T(2,128)(2,1)} %bitcast.14, f32[4,4,128]{2,1,0:T(4,128)} %kappa_hbm.1, s32[1,16384]{1,0:T(1,128)} %perm_hbm.1, s32[1,32]{1,0:T(1,128)} %bitcast.16), custom_call_target="tpu_custom_call" | custom-call | tf_op jit(solution)/shard_map/pack/pallas_call | solution.py:387
  1.6 7.2 %all-to-all-start = ((bf16[16,2,3072]{2,1,0:T(2,128)(2,1)}), bf16[16,2,3072]{2,1,0:T(2,128)(2,1)S(1)}, u32[]{:S(2)}, u32[]{:S(2)}) async-start(bf16[16,2,3072]{2,1,0:T(2,128)(2,1)} %get-tuple-element.14), calls=%async_computation | async-start | bytes 393216 | tf_op jit(solution)/shard_map/all_to_all | solution.py:401
  8.8 3.1 %slots.1 = (f32[1,16384]{1,0:T(1,128)S(1)}, f32[128,128]{1,0:T(8,128)S(1)}, bf16[256,4096]{1,0:T(8,128)(2,1)S(1)}) custom-call(s32[1,16384]{1,0:T(1,128)S(1)} %get-tuple-element.16.perm_ref, bf16[256,4096]{1,0:T(8,128)(2,1)} %bitcast.17), custom_call_target="tpu_custom_call" | custom-call | flops 2147483648 | bytes 1048576 | tf_op jit(solution)/shard_map/slots/pallas_call | solution.py:402
  11.9 5.8 %all-to-all-done.x_ref.packed_ref = bf16[16,2,3072]{2,1,0:T(2,128)(2,1)S(1)} async-done(((bf16[16,2,3072]{2,1,0:T(2,128)(2,1)}), bf16[16,2,3072]{2,1,0:T(2,128)(2,1)S(1)}, u32[]{:S(2)}, u32[]{:S(2)}) %all-to-all-start) | async-done | bytes 196640 | tf_op jit(solution)/shard_map/all_to_all | solution.py:401
  17.6 6.7 %partial_sums.1 = s16[2048,128]{1,0:T(8,128)(2,1)S(1)} custom-call(s32[2,8]{1,0:T(2,128)} %bitcast.15, bf16[256,4096]{1,0:T(8,128)(2,1)} %bitcast.13, bf16[8,512,512]{2,1,0:T(8,128)(2,1)} %bitcast.12, bf16[16,2,3072]{2,1,0:T(2,128)(2,1)S(1)} %all-to-all-done.x_ref.packed_ref, s32[1,32]{1,0:T(1,128)S(1)} %get-tuple-element.15.tile_rank_ref, ...), custom_call_target="tpu_custom_call" | custom-call | flops 2147483648 | bytes 8388608 | tf_op jit(solution)/shard_map/partial_sums/pallas_call | solution.py:416
  24.3 18.4 %all_to_all.10 = s16[128,16,128]{2,1,0:T(8,128)(2,1)S(1)} all-to-all(s16[128,16,128]{2,1,0:T(8,128)(2,1)S(1)} %bitcast.10), channel_id=1, replica_groups=mesh['row'=16,'col'=8] {'row','col'}, dimensions={0} | all-to-all | bytes 1048576 | tf_op jit(solution)/shard_map/all_to_all | solution.py:437
  42.7 1.5 %bricks.1 = (f32[144,128]{1,0:T(8,128)S(1)}, s16[128,128]{1,0:T(8,128)(2,1)S(1)}) custom-call(s16[2048,128]{1,0:T(8,128)(2,1)S(1)} %bitcast.11, bf16[16,2,3072]{2,1,0:T(2,128)(2,1)S(1)} %all-to-all-done.x_ref.packed_ref, f32[4,4,128]{2,1,0:T(4,128)S(1)} %get-tuple-element.20.kappa_ref), custom_call_target="tpu_custom_call" | custom-call | flops 1073741824 | bytes 1048576 | tf_op jit(solution)/shard_map/bricks/pallas_call | solution.py:438
  44.2 3.6 %collective-permute-start.1 = (s16[128,128]{1,0:T(8,128)(2,1)S(1)}, s16[128,128]{1,0:T(8,128)(2,1)S(1)}, u32[]{:S(2)}, u32[]{:S(2)}) collective-permute-start(s16[128,128]{1,0:T(8,128)(2,1)S(1)} %get-tuple-element.22), channel_id=1, source_target_pairs={{1,2},{3,4},{5,6},{2,1},{4,3},{6,5},{9,10},{11,12},{13,14},{10,9},... | collective-permute-start | bytes 98312 | tf_op jit(solution)/shard_map/ppermute | solution.py:360
  47.8 0.1 collective-permute-start
  47.9 4.2 %collective-permute-done.1.odd_ref = s16[128,128]{1,0:T(8,128)(2,1)S(1)} collective-permute-done((s16[128,128]{1,0:T(8,128)(2,1)S(1)}, s16[128,128]{1,0:T(8,128)(2,1)S(1)}, u32[]{:S(2)}, u32[]{:S(2)}) %collective-permute-start.1) | collective-permute-done | bytes 32800 | tf_op jit(solution)/shard_map/ppermute | solution.py:360
  52.1 0.0 collective-permute-done.even_ref
  52.1 0.9 %prior.1 = f32[2,4,4,128]{3,2,1,0:T(4,128)} custom-call(f32[144,128]{1,0:T(8,128)S(1)} %get-tuple-element.21.own_ref, s16[128,128]{1,0:T(8,128)(2,1)S(1)} %collective-permute-done.even_ref, s16[128,128]{1,0:T(8,128)(2,1)S(1)} %collective-permute-done.1.odd_ref), custom_call_target="tpu_custom_call" | custom-call | flops 16777216 | bytes 1048576 | tf_op jit(solution)/shard_map/prior/pallas_call | solution.py:457
Async XLA Ops:
  1.6 16.1 %all-to-all-start = ((bf16[16,2,3072]{2,1,0:T(2,128)(2,1)}), bf16[16,2,3072]{2,1,0:T(2,128)(2,1)S(1)}, u32[]{:S(2)}, u32[]{:S(2)}) async-start(bf16[16,2,3072]{2,1,0:T(2,128)(2,1)} %get-tuple-element.14), calls=%async_computation | async-start | bytes 393216 | tf_op jit(solution)/shard_map/all_to_all | solution.py:401
  44.2 7.9 %collective-permute-start.1 = (s16[128,128]{1,0:T(8,128)(2,1)S(1)}, s16[128,128]{1,0:T(8,128)(2,1)S(1)}, u32[]{:S(2)}, u32[]{:S(2)}) collective-permute-start(s16[128,128]{1,0:T(8,128)(2,1)S(1)} %get-tuple-element.22), channel_id=1, source_target_pairs={{1,2},{3,4},{5,6},{2,1},{4,3},{6,5},{9,10},{11,12},{13,14},{10,9},... | collective-permute-start | bytes 98312 | tf_op jit(solution)/shard_map/ppermute | solution.py:360
  47.8 4.3 %collective-permute-start = (s16[128,128]{1,0:T(8,128)(2,1)S(1)}, s16[128,128]{1,0:T(8,128)(2,1)S(1)}, u32[]{:S(2)}, u32[]{:S(2)}) collective-permute-start(s16[128,128]{1,0:T(8,128)(2,1)S(1)} %get-tuple-element.22), channel_id=1, source_target_pairs={{0,1},{2,3},{4,5},{6,7},{1,0},{3,2},{5,4},{7,6},{8,9},{10,11},{12,... | collective-permute-start | bytes 98312 | tf_op jit(solution)/shard_map/ppermute | solution.py:360

commit v8 on v7

--- a/solution.py
+++ b/solution.py
@@ -22,7 +22,7 @@
 DEV = ROWS * COLS
 PIECES = 2
 LEAF_PIECES = ((0, 2), (2, 4), (4, 6), (6, 8))
-SLAB = 16
+SLAB = 8
 F32 = jnp.float32
 BF16 = jnp.bfloat16
 NT = (((1,), (1,)), ((), ()))
@@ -40,14 +40,9 @@
 
 
 def pack_kernel(
-    vectors_hbm, kappa_hbm, perm_hbm, rank_hbm, out_ref, kappa_ref, perm_ref, rank_ref, vectors, sems
+    vectors_hbm, kappa_hbm, out_ref, kappa_ref, vectors, sems
 ):
-    pairs = (
-        (vectors_hbm, vectors),
-        (kappa_hbm, kappa_ref),
-        (perm_hbm, perm_ref),
-        (rank_hbm, rank_ref),
-    )
+    pairs = ((vectors_hbm, vectors), (kappa_hbm, kappa_ref))
     copies = [pltpu.make_async_copy(a, b, sems.at[i]) for i, (a, b) in enumerate(pairs)]
     for copy in copies:
         copy.start()
@@ -61,13 +56,16 @@
         pair = jnp.concatenate([rows[q], rows[half + q]], axis=0).astype(BF16)
         for s in range(ROWS):
             out_ref[s, :, PTS + q * NZ : PTS + (q + 1) * NZ] = pair
-    copies[2].wait()
-    copies[3].wait()
-
-
-def slots_kernel(perm_ref, right_hbm, rank_ref, place_ref, right, sem):
-    copy = pltpu.make_async_copy(right_hbm, right, sem)
-    copy.start()
+
+
+def slots_kernel(
+    perm_hbm, tile_hbm, right_hbm, perm_ref, tile_ref, rank_ref, place_ref, right, sems
+):
+    pairs = ((perm_hbm, perm_ref), (tile_hbm, tile_ref), (right_hbm, right))
+    copies = [pltpu.make_async_copy(a, b, sems.at[i]) for i, (a, b) in enumerate(pairs)]
+    for copy in copies:
+        copy.start()
+    copies[0].wait()
     chunk = 256
     upto = jnp.where(iota((chunk, chunk), 0) <= iota((chunk, chunk), 1), 1.0, 0.0).astype(BF16)
     brick = iota((DEV, chunk), 0)
@@ -92,8 +90,9 @@
     for part in (inside & ~(NZ - 1), (inside & (NZ - 1)) + 1):
         spread = here * part.astype(F32).astype(BF16)
         place = place + lax.dot_general(hot, spread, NT, preferred_element_type=F32)
-    place_ref[...] = place
-    copy.wait()
+    place_ref[...] = place.astype(jnp.int32)
+    copies[1].wait()
+    copies[2].wait()
 
 
 def level_of(values):
@@ -122,7 +121,6 @@
     leaves,
     x_rows,
     sums,
-    stage,
     leaf_at,
     sems,
 ):
@@ -138,15 +136,17 @@
     for copy in copies:
         copy.start()
 
-    def put(values, first_row, step):
-        values = values.astype(jnp.int32)
+    def beside(values):
         none = jnp.zeros((COLS, 128), jnp.int32)
-        stage[pl.ds(first_row, COLS, stride=SLAB), :] = none
-        stage[pl.ds(first_row + COLS * SLAB, DEV - COLS, stride=SLAB), :] = values[: DEV - COLS]
-        stage[pl.ds(first_row + step, DEV, stride=SLAB), :] = values
-        at = first_row + 2 * step
-        stage[pl.ds(at, DEV - COLS, stride=SLAB), :] = values[COLS:]
-        stage[pl.ds(at + (DEV - COLS) * SLAB, COLS, stride=SLAB), :] = none
+        last = DEV - COLS
+        return [
+            jnp.concatenate([none, values[:last]], axis=0),
+            values,
+            jnp.concatenate([values[COLS:], none], axis=0),
+        ]
+
+    def pack(low, high):
+        return (high << 16) | (low & 0xFFFF)
 
     half = TS // PTS
     for s in range(ROWS):
@@ -194,9 +194,12 @@
         for v in range(NVEC):
             at = (pl.ds(8 * v + i // per_tile, 1), pl.ds(to_lane, LEAF))
             sums[at] = sums[at] + near[v : v + 1]
-    put(place_ref[...], 12, 1)
+    places = beside(place_ref[...])
     level, inverse = level_of(sums[...])
-    stage[pl.ds(15, DEV, stride=SLAB), :] = jnp.broadcast_to(level.astype(jnp.int32), (DEV, 128))
+    out_ref[pl.ds(6, DEV, stride=SLAB), :] = pack(places[0], places[1])
+    out_ref[pl.ds(7, DEV, stride=SLAB), :] = pack(
+        places[2], jnp.broadcast_to(level.astype(jnp.int32), (DEV, 128))
+    )
     one, none = jnp.ones((), BF16), jnp.zeros((), BF16)
 
     def numbers(count):
@@ -218,30 +221,45 @@
             hot = jnp.where(hot, one, none)
             part = lax.dot_general(hot, spread, NT, preferred_element_type=F32)
             parts.append(part + pltpu.roll(part, NVEC * CAP, 1))
-        for v in range(NVEC):
-            values = jnp.concatenate([p[:, v * CAP : (v + 1) * CAP] for p in parts], axis=1)
-            put(jnp.round(values * inverse), group * 2 + v, 4)
-    out_ref[...] = stage[...].astype(jnp.int16)
+        words = pack(
+            *(
+                jnp.round(
+                    jnp.concatenate([p[:, v * CAP : (v + 1) * CAP] for p in parts], axis=1) * inverse
+                ).astype(jnp.int32)
+                for v in range(NVEC)
+            )
+        )
+        for j, moved in enumerate(beside(words)):
+            out_ref[pl.ds(j * 2 + group, DEV, stride=SLAB), :] = moved
 
 
 def bricks_kernel(
     got_ref, packed_ref, kappa_ref, out_ref, halo_ref, sums, wheres, at_cells
 ):
+    valued = iota((SLAB, 128), 0) < 6
     for r in range(ROWS):
+        at = slice(r * SLAB, (r + 1) * SLAB)
+        halves = []
         for g in range(2):
-            total = None
+            totals = [None, None]
             for c in range(4):
-                at = ((r * 2 + g) * 4 + c) * SLAB
-                one = got_ref[at : at + SLAB, :].astype(jnp.int32).astype(F32)
-                one = jnp.where(iota((SLAB, 128), 0) < 12, one * step_at(one[15:16]), one)
-                total = one if total is None else total + one
-            wheres[g, r * SLAB : (r + 1) * SLAB, :] = total
-    sums[...] = wheres[0] + wheres[1]
-    for g in range(2):
-        place = wheres[g] - 1.0
-        cell = jnp.floor(place * (1.0 / NZ))
-        at_cells[g] = cell
-        wheres[g] = place - cell * NZ
+                start = ((r * 2 + g) * 4 + c) * SLAB
+                words = got_ref[start : start + SLAB, :]
+                pair = [((words << 16) >> 16).astype(F32), (words >> 16).astype(F32)]
+                size = jnp.where(valued, step_at(pair[1][7:8]), 1.0)
+                pair = [one * size for one in pair]
+                totals = [b if a is None else a + b for a, b in zip(totals, pair)]
+            for v in range(NVEC):
+                wheres[v, g, at, :] = totals[v]
+            halves.append(totals)
+        for v in range(NVEC):
+            sums[v, at, :] = halves[0][v] + halves[1][v]
+    for v in range(NVEC):
+        for g in range(2):
+            place = wheres[v, g] - 1.0
+            cell = jnp.floor(place * (1.0 / NZ))
+            at_cells[v, g] = cell
+            wheres[v, g] = place - cell * NZ
     sub = iota((8, 128), 0)
     z_row = iota((NZ, 128), 0).astype(F32).astype(BF16)
     one, none = jnp.ones((), BF16), jnp.zeros((), BF16)
@@ -250,16 +268,16 @@
         for some in range(0, ROWS, 4):
             cells, heights = [], []
             for r, g in ((r, g) for r in range(some, some + 4) for g in range(2)):
-                at = r * SLAB + j * 4 + g * 2
-                pair = jnp.where(sub < 4, sums[at : at + 1, :], sums[at + 1 : at + 2, :])
+                at = r * SLAB + j * 2 + g
+                pair = jnp.where(sub < 4, sums[0, at : at + 1, :], sums[1, at : at + 1, :])
                 high = pair.astype(BF16).astype(F32)
                 low = pair - high
-                p = r * SLAB + 12 + j
-                cell = at_cells[g, p : p + 1, :]
+                v, p = j % 2, r * SLAB + 6 + j // 2
+                cell = at_cells[v, g, p : p + 1, :]
                 wanted = [cell == (x * CY + sub % CY).astype(F32) for x in range(CX)]
                 rows = [jnp.where(w, part, 0.0) for part in (high, low) for w in wanted]
                 cells.append(jnp.concatenate(rows, axis=0).astype(BF16))
-                z_at = wheres[g, p : p + 1, :].astype(BF16)
+                z_at = wheres[v, g, p : p + 1, :].astype(BF16)
                 heights.append(jnp.where(z_at == z_row, one, none))
             both = both + lax.dot_general(
                 jnp.concatenate(cells, axis=1),
@@ -384,38 +402,38 @@
     points = COLS * PTS
     terms = TILE_ROWS * TILE_COLS * KMAX
     packed_shape = (ROWS, NVEC, PTS + PTS // NVEC)
-    packed, kappa_own, perm, ranks = pl.pallas_call(
+    packed, kappa_own = pl.pallas_call(
         pack_kernel,
         out_shape=(
             pltpu.VMEM(packed_shape, BF16),
             pltpu.VMEM((CX, CY, NZ), F32),
+        ),
+        in_specs=[hbm] * 2,
+        out_specs=(vmem,) * 2,
+        scratch_shapes=[pltpu.VMEM((NVEC, PTS), BF16), pltpu.SemaphoreType.DMA((2,))],
+        compiler_params=params(8),
+        name="pack",
+    )(*in_hbm(vectors[:, 0], kappa))
+    packed = lax.all_to_all(packed, "row", 0, 0, tiled=True)
+    perm, ranks, rank, place, right = pl.pallas_call(
+        slots_kernel,
+        out_shape=(
             pltpu.VMEM((1, points), jnp.int32),
             pltpu.VMEM((1, TILE_ROWS * TILE_COLS), jnp.int32),
-        ),
-        in_specs=[hbm] * 4,
-        out_specs=(vmem,) * 4,
-        scratch_shapes=[pltpu.VMEM((NVEC, PTS), BF16), pltpu.SemaphoreType.DMA((4,))],
-        compiler_params=params(8),
-        name="pack",
-    )(*in_hbm(vectors[:, 0], kappa, cluster_perm, tile_rank[0]))
-    packed = lax.all_to_all(packed, "row", 0, 0, tiled=True)
-    rank, place, right = pl.pallas_call(
-        slots_kernel,
-        out_shape=(
             pltpu.VMEM((1, points), F32),
-            pltpu.VMEM((DEV, 128), F32),
+            pltpu.VMEM((DEV, 128), jnp.int32),
             pltpu.VMEM((terms, TS), BF16),
         ),
-        in_specs=[vmem, hbm],
-        out_specs=(vmem,) * 3,
-        scratch_shapes=[pltpu.SemaphoreType.DMA],
+        in_specs=[hbm] * 3,
+        out_specs=(vmem,) * 5,
+        scratch_shapes=[pltpu.SemaphoreType.DMA((3,))],
         compiler_params=params(16),
         cost_estimate=cost(1 << 31, 1 << 20),
         name="slots",
-    )(perm, *in_hbm(lr_right.reshape(terms, TS)))
+    )(*in_hbm(cluster_perm, tile_rank[0], lr_right.reshape(terms, TS)))
     send = pl.pallas_call(
         send_kernel,
-        out_shape=jax.ShapeDtypeStruct((DEV * SLAB, 128), jnp.int16),
+        out_shape=jax.ShapeDtypeStruct((DEV * SLAB, 128), jnp.int32),
         in_specs=[hbm] * 3 + [vmem] * 6,
         out_specs=vmem,
         scratch_shapes=[
@@ -423,7 +441,6 @@
             pltpu.VMEM((NLEAF, LEAF, LEAF), BF16),
             pltpu.VMEM((16, TS), F32),
             pltpu.VMEM((16, TS), F32),
-            pltpu.VMEM((DEV * SLAB, 128), jnp.int32),
             pltpu.SMEM((2, NLEAF), jnp.int32),
             pltpu.SemaphoreType.DMA((1 + PIECES + len(LEAF_PIECES),)),
         ],
@@ -444,9 +461,9 @@
         in_specs=[vmem] * 3,
         out_specs=(vmem,) * 2,
         scratch_shapes=[
-            pltpu.VMEM((ROWS * SLAB, 128), F32),
-            pltpu.VMEM((2, ROWS * SLAB, 128), F32),
-            pltpu.VMEM((2, ROWS * SLAB, 128), F32),
+            pltpu.VMEM((NVEC, ROWS * SLAB, 128), F32),
+            pltpu.VMEM((NVEC, 2, ROWS * SLAB, 128), F32),
+            pltpu.VMEM((NVEC, 2, ROWS * SLAB, 128), F32),
         ],
         compiler_params=params(16),
         cost_estimate=cost(1 << 30, 1 << 20),

time: 53.3 us -> 53.1 us (level)
  waiting for transfers between devices: 9.97 us -> 9.11 us
    pallas_call x1, Pallas kernels: 3.11 us -> 3.96 us  [per_device(): pl.pallas_call(slots_kernel, out_shape=(pltpu.VMEM((1, points), jnp.int32...]
    all_to_all x1, waiting for transfers between devices: 5.77 us -> 4.91 us  [per_device(): packed = lax.all_to_all(packed, 'row', 0, 0, tiled=True)]
  transfers between devices with their start and end apart: 3 -> 3, of which waited for: 2 -> 2; matrix products, arithmetic and copies ran while one was open for 0% -> 0% of each run, Pallas kernels for 6% -> 8%
where the time goes in v8:
time: 53.1 us; the launch traced here: 52.7 us
  blocking collectives  18.4 us (35%)
  Pallas kernels  14.3 us (27%)
  starting transfers between devices  10.9 us (21%)
  waiting for transfers between devices  9.11 us (17%)
    all_to_all x1, blocking collectives, per_device(): lax.all_to_all(send.reshape(DEV, SLAB, 128), ('row', 'col'), 0, 0, tiled=...  18.4 us
    all_to_all x1, starting transfers between devices, per_device(): packed = lax.all_to_all(packed, 'row', 0, 0, tiled=True)  7.16 us
    pallas_call x1, Pallas kernels, per_device(): pl.pallas_call(send_kernel, out_shape=jax.ShapeDtypeStruct((DEV * SLAB, 1...  6.49 us
    all_to_all x1, waiting for transfers between devices, per_device(): packed = lax.all_to_all(packed, 'row', 0, 0, tiled=True)  4.91 us
    ppermute x2, waiting for transfers between devices, swapped(): return lax.ppermute(array, axis, pairs + [(b, a) for a, b in pairs])  4.2 us
    pallas_call x1, Pallas kernels, per_device(): pl.pallas_call(slots_kernel, out_shape=(pltpu.VMEM((1, points), jnp.int32...  3.96 us
    ppermute x2, starting transfers between devices, swapped(): return lax.ppermute(array, axis, pairs + [(b, a) for a, b in pairs])  3.7 us
    pallas_call x1, Pallas kernels, per_device(): pl.pallas_call(bricks_kernel, out_shape=(pltpu.VMEM((FIELD + 3 * CX * CY,...  1.47 us
  transfers between devices with their start and end apart: 3, of which 2 were waited for; matrix products, arithmetic and copies ran while one was open for 0% of the time, Pallas kernels for 8%

profile of v8, /device:TPU:8, one launch (start us, length us, event | category | flops | bytes accessed | tf_op | source)
XLA Modules:
  0.0 52.7 jit_solution(5926070922892989832)
XLA Ops:
  0.0 1.4 %pack.1 = (bf16[16,2,3072]{2,1,0:T(2,128)(2,1)}, f32[4,4,128]{2,1,0:T(4,128)S(1)}) custom-call(bf16[2,2048]{1,0:T(2,128)(2,1)} %bitcast.14, f32[4,4,128]{2,1,0:T(4,128)} %kappa_hbm.1), custom_call_target="tpu_custom_call" | custom-call | tf_op jit(solution)/shard_map/pack/pallas_call | solution.py:405
  1.4 7.2 %all-to-all-start = ((bf16[16,2,3072]{2,1,0:T(2,128)(2,1)}), bf16[16,2,3072]{2,1,0:T(2,128)(2,1)S(1)}, u32[]{:S(2)}, u32[]{:S(2)}) async-start(bf16[16,2,3072]{2,1,0:T(2,128)(2,1)} %get-tuple-element.14), calls=%async_computation | async-start | bytes 393216 | tf_op jit(solution)/shard_map/all_to_all | solution.py:417
  8.6 4.0 %slots.1 = (s32[1,16384]{1,0:T(1,128)S(1)}, s32[1,32]{1,0:T(1,128)S(1)}, f32[1,16384]{1,0:T(1,128)S(1)}, s32[128,128]{1,0:T(8,128)S(1)}, bf16[256,4096]{1,0:T(8,128)(2,1)S(1)}) custom-call(s32[1,16384]{1,0:T(1,128)} %perm_hbm.1, s32[1,32]{1,0:T(1,128)} %bitcast.17, bf16[256,4096]{1,0:T(8,128)(2,1)} %bitcast.16), custom_call_target="tpu_custom_call" | custom-call | flops 2147483648 | bytes 1048576 | tf_op jit(solution)/shard_map/slots/pallas_call | solution.py:418
  12.6 4.9 %all-to-all-done.x_ref.packed_ref = bf16[16,2,3072]{2,1,0:T(2,128)(2,1)S(1)} async-done(((bf16[16,2,3072]{2,1,0:T(2,128)(2,1)}), bf16[16,2,3072]{2,1,0:T(2,128)(2,1)S(1)}, u32[]{:S(2)}, u32[]{:S(2)}) %all-to-all-start) | async-done | bytes 196640 | tf_op jit(solution)/shard_map/all_to_all | solution.py:417
  17.5 6.5 %partial_sums.1 = s32[1024,128]{1,0:T(8,128)S(1)} custom-call(s32[2,8]{1,0:T(2,128)} %bitcast.15, bf16[256,4096]{1,0:T(8,128)(2,1)} %bitcast.13, bf16[8,512,512]{2,1,0:T(8,128)(2,1)} %bitcast.12, bf16[16,2,3072]{2,1,0:T(2,128)(2,1)S(1)} %all-to-all-done.x_ref.packed_ref, s32[1,32]{1,0:T(1,128)S(1)} %get-tuple-element.15.tile_rank_ref, ...), custom_call_target="tpu_custom_call" | custom-call | flops 2147483648 | bytes 8388608 | tf_op jit(solution)/shard_map/partial_sums/pallas_call | solution.py:434
  24.0 18.4 %all_to_all.10 = s32[128,8,128]{2,1,0:T(8,128)S(1)} all-to-all(s32[128,8,128]{2,1,0:T(8,128)S(1)} %bitcast.10), channel_id=1, replica_groups=mesh['row'=16,'col'=8] {'row','col'}, dimensions={0} | all-to-all | bytes 1048576 | tf_op jit(solution)/shard_map/all_to_all | solution.py:454
  42.4 1.5 %bricks.1 = (f32[144,128]{1,0:T(8,128)S(1)}, s16[128,128]{1,0:T(8,128)(2,1)S(1)}) custom-call(s32[1024,128]{1,0:T(8,128)S(1)} %bitcast.11, bf16[16,2,3072]{2,1,0:T(2,128)(2,1)S(1)} %all-to-all-done.x_ref.packed_ref, f32[4,4,128]{2,1,0:T(4,128)S(1)} %get-tuple-element.20.kappa_ref), custom_call_target="tpu_custom_call" | custom-call | flops 1073741824 | bytes 1048576 | tf_op jit(solution)/shard_map/bricks/pallas_call | solution.py:455
  43.9 3.6 %collective-permute-start.1 = (s16[128,128]{1,0:T(8,128)(2,1)S(1)}, s16[128,128]{1,0:T(8,128)(2,1)S(1)}, u32[]{:S(2)}, u32[]{:S(2)}) collective-permute-start(s16[128,128]{1,0:T(8,128)(2,1)S(1)} %get-tuple-element.22), channel_id=1, source_target_pairs={{1,2},{3,4},{5,6},{2,1},{4,3},{6,5},{9,10},{11,12},{13,14},{10,9},... | collective-permute-start | bytes 98312 | tf_op jit(solution)/shard_map/ppermute | solution.py:378
  47.5 0.1 collective-permute-start
  47.6 4.2 %collective-permute-done.1.odd_ref = s16[128,128]{1,0:T(8,128)(2,1)S(1)} collective-permute-done((s16[128,128]{1,0:T(8,128)(2,1)S(1)}, s16[128,128]{1,0:T(8,128)(2,1)S(1)}, u32[]{:S(2)}, u32[]{:S(2)}) %collective-permute-start.1) | collective-permute-done | bytes 32800 | tf_op jit(solution)/shard_map/ppermute | solution.py:378
  51.8 0.0 collective-permute-done.even_ref
  51.8 0.9 %prior.1 = f32[2,4,4,128]{3,2,1,0:T(4,128)} custom-call(f32[144,128]{1,0:T(8,128)S(1)} %get-tuple-element.21.own_ref, s16[128,128]{1,0:T(8,128)(2,1)S(1)} %collective-permute-done.even_ref, s16[128,128]{1,0:T(8,128)(2,1)S(1)} %collective-permute-done.1.odd_ref), custom_call_target="tpu_custom_call" | custom-call | flops 16777216 | bytes 1048576 | tf_op jit(solution)/shard_map/prior/pallas_call | solution.py:474
Async XLA Ops:
  1.4 16.1 %all-to-all-start = ((bf16[16,2,3072]{2,1,0:T(2,128)(2,1)}), bf16[16,2,3072]{2,1,0:T(2,128)(2,1)S(1)}, u32[]{:S(2)}, u32[]{:S(2)}) async-start(bf16[16,2,3072]{2,1,0:T(2,128)(2,1)} %get-tuple-element.14), calls=%async_computation | async-start | bytes 393216 | tf_op jit(solution)/shard_map/all_to_all | solution.py:417
  43.9 7.9 %collective-permute-start.1 = (s16[128,128]{1,0:T(8,128)(2,1)S(1)}, s16[128,128]{1,0:T(8,128)(2,1)S(1)}, u32[]{:S(2)}, u32[]{:S(2)}) collective-permute-start(s16[128,128]{1,0:T(8,128)(2,1)S(1)} %get-tuple-element.22), channel_id=1, source_target_pairs={{1,2},{3,4},{5,6},{2,1},{4,3},{6,5},{9,10},{11,12},{13,14},{10,9},... | collective-permute-start | bytes 98312 | tf_op jit(solution)/shard_map/ppermute | solution.py:378
  47.5 4.3 %collective-permute-start = (s16[128,128]{1,0:T(8,128)(2,1)S(1)}, s16[128,128]{1,0:T(8,128)(2,1)S(1)}, u32[]{:S(2)}, u32[]{:S(2)}) collective-permute-start(s16[128,128]{1,0:T(8,128)(2,1)S(1)} %get-tuple-element.22), channel_id=1, source_target_pairs={{0,1},{2,3},{4,5},{6,7},{1,0},{3,2},{5,4},{7,6},{8,9},{10,11},{12,... | collective-permute-start | bytes 98312 | tf_op jit(solution)/shard_map/ppermute | solution.py:378

commit v9 on v8

--- a/solution.py
+++ b/solution.py
@@ -22,7 +22,7 @@
 DEV = ROWS * COLS
 PIECES = 2
 LEAF_PIECES = ((0, 2), (2, 4), (4, 6), (6, 8))
-SLAB = 8
+SLAB = 7
 F32 = jnp.float32
 BF16 = jnp.bfloat16
 NT = (((1,), (1,)), ((), ()))
@@ -56,6 +56,16 @@
         pair = jnp.concatenate([rows[q], rows[half + q]], axis=0).astype(BF16)
         for s in range(ROWS):
             out_ref[s, :, PTS + q * NZ : PTS + (q + 1) * NZ] = pair
+
+
+def beside(values):
+    none = jnp.zeros((COLS, values.shape[1]), jnp.int32)
+    last = DEV - COLS
+    return [
+        jnp.concatenate([none, values[:last]], axis=0),
+        values,
+        jnp.concatenate([values[COLS:], none], axis=0),
+    ]
 
 
 def slots_kernel(
@@ -82,15 +92,16 @@
     col = lax.axis_index("col")
     start = pl.multiple_of(col * PTS, PTS)
     own = perm_ref[0:1, pl.ds(start, PTS)]
-    slot = rank_ref[0:1, pl.ds(start, PTS)] + ((col % 4) * CAP).astype(F32)
-    here = jnp.where(slot == iota((128, PTS), 0).astype(F32), 1.0, 0.0).astype(BF16)
+    slot = rank_ref[0:1, pl.ds(start, PTS)]
+    here = jnp.where(slot == iota((CAP, PTS), 0).astype(F32), 1.0, 0.0).astype(BF16)
     hot = jnp.where((own >> 11) == iota((DEV, PTS), 0), 1.0, 0.0).astype(BF16)
     inside = own & (PTS - 1)
-    place = jnp.zeros((DEV, 128), F32)
+    place = jnp.zeros((DEV, CAP), F32)
     for part in (inside & ~(NZ - 1), (inside & (NZ - 1)) + 1):
         spread = here * part.astype(F32).astype(BF16)
         place = place + lax.dot_general(hot, spread, NT, preferred_element_type=F32)
-    place_ref[...] = place.astype(jnp.int32)
+    place = place.astype(jnp.int32)
+    place_ref[...] = jnp.concatenate(beside(place) + [jnp.zeros((DEV, CAP), jnp.int32)], axis=1)
     copies[1].wait()
     copies[2].wait()
 
@@ -135,15 +146,6 @@
     copies = [pltpu.make_async_copy(a, b, sems.at[i]) for i, (a, b) in enumerate(pairs)]
     for copy in copies:
         copy.start()
-
-    def beside(values):
-        none = jnp.zeros((COLS, 128), jnp.int32)
-        last = DEV - COLS
-        return [
-            jnp.concatenate([none, values[:last]], axis=0),
-            values,
-            jnp.concatenate([values[COLS:], none], axis=0),
-        ]
 
     def pack(low, high):
         return (high << 16) | (low & 0xFFFF)
@@ -194,11 +196,9 @@
         for v in range(NVEC):
             at = (pl.ds(8 * v + i // per_tile, 1), pl.ds(to_lane, LEAF))
             sums[at] = sums[at] + near[v : v + 1]
-    places = beside(place_ref[...])
     level, inverse = level_of(sums[...])
-    out_ref[pl.ds(6, DEV, stride=SLAB), :] = pack(places[0], places[1])
-    out_ref[pl.ds(7, DEV, stride=SLAB), :] = pack(
-        places[2], jnp.broadcast_to(level.astype(jnp.int32), (DEV, 128))
+    out_ref[pl.ds(6, DEV, stride=SLAB), :] = jnp.where(
+        iota((DEV, 128), 1) < 3 * CAP, place_ref[...], level.astype(jnp.int32)
     )
     one, none = jnp.ones((), BF16), jnp.zeros((), BF16)
 
@@ -236,30 +236,31 @@
 def bricks_kernel(
     got_ref, packed_ref, kappa_ref, out_ref, halo_ref, sums, wheres, at_cells
 ):
-    valued = iota((SLAB, 128), 0) < 6
-    for r in range(ROWS):
-        at = slice(r * SLAB, (r + 1) * SLAB)
-        halves = []
-        for g in range(2):
-            totals = [None, None]
-            for c in range(4):
-                start = ((r * 2 + g) * 4 + c) * SLAB
-                words = got_ref[start : start + SLAB, :]
-                pair = [((words << 16) >> 16).astype(F32), (words >> 16).astype(F32)]
-                size = jnp.where(valued, step_at(pair[1][7:8]), 1.0)
-                pair = [one * size for one in pair]
-                totals = [b if a is None else a + b for a, b in zip(totals, pair)]
-            for v in range(NVEC):
-                wheres[v, g, at, :] = totals[v]
-            halves.append(totals)
+    def of_all_rows(c, q):
+        return got_ref[pl.ds(c * SLAB + q, ROWS, stride=COLS * SLAB), :]
+
+    last = [of_all_rows(c, 6).astype(F32) for c in range(COLS)]
+    sizes = [
+        step_at(jnp.broadcast_to(one[:, 3 * CAP : 3 * CAP + 1], (ROWS, 128))) for one in last
+    ]
+    for q in range(6):
+        totals = [jnp.zeros((ROWS, 128), F32)] * NVEC
+        for c in range(COLS):
+            words = of_all_rows(c, q)
+            pair = ((words << 16) >> 16, words >> 16)
+            totals = [t + w.astype(F32) * sizes[c] for t, w in zip(totals, pair)]
         for v in range(NVEC):
-            sums[v, at, :] = halves[0][v] + halves[1][v]
-    for v in range(NVEC):
-        for g in range(2):
-            place = wheres[v, g] - 1.0
+            sums[v, q * ROWS : (q + 1) * ROWS, :] = totals[v]
+    part = iota((ROWS, 128), 1) // CAP
+    for g in range(2):
+        for j in range(3):
+            place = jnp.full((ROWS, 128), -1.0, F32)
+            for kk in range(4):
+                moved = pltpu.roll(last[g * 4 + kk], (kk - j) * CAP % 128, 1)
+                place = place + jnp.where(part == kk, moved, 0.0)
             cell = jnp.floor(place * (1.0 / NZ))
-            at_cells[v, g] = cell
-            wheres[v, g] = place - cell * NZ
+            at_cells[g, j * ROWS : (j + 1) * ROWS, :] = cell
+            wheres[g, j * ROWS : (j + 1) * ROWS, :] = place - cell * NZ
     sub = iota((8, 128), 0)
     z_row = iota((NZ, 128), 0).astype(F32).astype(BF16)
     one, none = jnp.ones((), BF16), jnp.zeros((), BF16)
@@ -268,16 +269,16 @@
         for some in range(0, ROWS, 4):
             cells, heights = [], []
             for r, g in ((r, g) for r in range(some, some + 4) for g in range(2)):
-                at = r * SLAB + j * 2 + g
+                at = (j * 2 + g) * ROWS + r
                 pair = jnp.where(sub < 4, sums[0, at : at + 1, :], sums[1, at : at + 1, :])
                 high = pair.astype(BF16).astype(F32)
                 low = pair - high
-                v, p = j % 2, r * SLAB + 6 + j // 2
-                cell = at_cells[v, g, p : p + 1, :]
+                p = j * ROWS + r
+                cell = at_cells[g, p : p + 1, :]
                 wanted = [cell == (x * CY + sub % CY).astype(F32) for x in range(CX)]
                 rows = [jnp.where(w, part, 0.0) for part in (high, low) for w in wanted]
                 cells.append(jnp.concatenate(rows, axis=0).astype(BF16))
-                z_at = wheres[v, g, p : p + 1, :].astype(BF16)
+                z_at = wheres[g, p : p + 1, :].astype(BF16)
                 heights.append(jnp.where(z_at == z_row, one, none))
             both = both + lax.dot_general(
                 jnp.concatenate(cells, axis=1),
@@ -451,7 +452,7 @@
         *in_hbm(leaf_places[0, 0].T, lr_left.reshape(terms, TS), leaf_values[0, 0]),
         *in_vmem(packed, ranks, perm, rank, place, right),
     )
-    got = lax.all_to_all(send.reshape(DEV, SLAB, 128), ("row", "col"), 0, 0, tiled=True)
+    got = lax.all_to_all(send.reshape(DEV, SLAB, 1, 128), ("row", "col"), 0, 0, tiled=True)
     own, halo = pl.pallas_call(
         bricks_kernel,
         out_shape=(
@@ -461,9 +462,9 @@
         in_specs=[vmem] * 3,
         out_specs=(vmem,) * 2,
         scratch_shapes=[
-            pltpu.VMEM((NVEC, ROWS * SLAB, 128), F32),
-            pltpu.VMEM((NVEC, 2, ROWS * SLAB, 128), F32),
-            pltpu.VMEM((NVEC, 2, ROWS * SLAB, 128), F32),
+            pltpu.VMEM((NVEC, 6 * ROWS, 128), F32),
+            pltpu.VMEM((2, 3 * ROWS, 128), F32),
+            pltpu.VMEM((2, 3 * ROWS, 128), F32),
         ],
         compiler_params=params(16),
         cost_estimate=cost(1 << 30, 1 << 20),

time: 53.1 us -> 52.4 us (0.987)
  blocking collectives: 18.4 us -> 17.8 us
    all_to_all x1, blocking collectives: 18.4 us -> 17.8 us  [per_device(): lax.all_to_all(send.reshape(DEV, SLAB, 1, 128), ('row', 'col'), 0, 0, til...]
where the time goes in v9:
time: 52.4 us; the launch traced here: 52 us
  blocking collectives  17.8 us (34%)
  Pallas kernels  14.2 us (27%)
  starting transfers between devices  10.9 us (21%)
  waiting for transfers between devices  9.06 us (17%)
    all_to_all x1, blocking collectives, per_device(): lax.all_to_all(send.reshape(DEV, SLAB, 1, 128), ('row', 'col'), 0, 0, til...  17.8 us
    all_to_all x1, starting transfers between devices, per_device(): packed = lax.all_to_all(packed, 'row', 0, 0, tiled=True)  7.16 us
    pallas_call x1, Pallas kernels, per_device(): pl.pallas_call(send_kernel, out_shape=jax.ShapeDtypeStruct((DEV * SLAB, 1...  6.43 us
    all_to_all x1, waiting for transfers between devices, per_device(): packed = lax.all_to_all(packed, 'row', 0, 0, tiled=True)  4.86 us
    ppermute x2, waiting for transfers between devices, swapped(): return lax.ppermute(array, axis, pairs + [(b, a) for a, b in pairs])  4.19 us
    pallas_call x1, Pallas kernels, per_device(): pl.pallas_call(slots_kernel, out_shape=(pltpu.VMEM((1, points), jnp.int32...  4.01 us
    ppermute x2, starting transfers between devices, swapped(): return lax.ppermute(array, axis, pairs + [(b, a) for a, b in pairs])  3.71 us
    pallas_call x1, Pallas kernels, per_device(): pl.pallas_call(bricks_kernel, out_shape=(pltpu.VMEM((FIELD + 3 * CX * CY,...  1.44 us
  transfers between devices with their start and end apart: 3, of which 2 were waited for; matrix products, arithmetic and copies ran while one was open for 0% of the time, Pallas kernels for 8%

profile of v9, /device:TPU:8, one launch (start us, length us, event | category | flops | bytes accessed | tf_op | source)
XLA Modules:
  0.0 52.0 jit_solution(15754851236357515522)
XLA Ops:
  0.0 1.4 %pack.1 = (bf16[16,2,3072]{2,1,0:T(2,128)(2,1)}, f32[4,4,128]{2,1,0:T(4,128)S(1)}) custom-call(bf16[2,2048]{1,0:T(2,128)(2,1)} %bitcast.14, f32[4,4,128]{2,1,0:T(4,128)} %kappa_hbm.1), custom_call_target="tpu_custom_call" | custom-call | tf_op jit(solution)/shard_map/pack/pallas_call | solution.py:406
  1.4 7.2 %all-to-all-start = ((bf16[16,2,3072]{2,1,0:T(2,128)(2,1)}), bf16[16,2,3072]{2,1,0:T(2,128)(2,1)S(1)}, u32[]{:S(2)}, u32[]{:S(2)}) async-start(bf16[16,2,3072]{2,1,0:T(2,128)(2,1)} %get-tuple-element.14), calls=%async_computation | async-start | bytes 393216 | tf_op jit(solution)/shard_map/all_to_all | solution.py:418
  8.6 4.0 %slots.1 = (s32[1,16384]{1,0:T(1,128)S(1)}, s32[1,32]{1,0:T(1,128)S(1)}, f32[1,16384]{1,0:T(1,128)S(1)}, s32[128,128]{1,0:T(8,128)S(1)}, bf16[256,4096]{1,0:T(8,128)(2,1)S(1)}) custom-call(s32[1,16384]{1,0:T(1,128)} %perm_hbm.1, s32[1,32]{1,0:T(1,128)} %bitcast.17, bf16[256,4096]{1,0:T(8,128)(2,1)} %bitcast.16), custom_call_target="tpu_custom_call" | custom-call | flops 2147483648 | bytes 1048576 | tf_op jit(solution)/shard_map/slots/pallas_call | solution.py:419
  12.6 4.9 %all-to-all-done.x_ref.packed_ref = bf16[16,2,3072]{2,1,0:T(2,128)(2,1)S(1)} async-done(((bf16[16,2,3072]{2,1,0:T(2,128)(2,1)}), bf16[16,2,3072]{2,1,0:T(2,128)(2,1)S(1)}, u32[]{:S(2)}, u32[]{:S(2)}) %all-to-all-start) | async-done | bytes 196640 | tf_op jit(solution)/shard_map/all_to_all | solution.py:418
  17.5 6.4 %partial_sums.1 = s32[896,128]{1,0:T(8,128)S(1)} custom-call(s32[2,8]{1,0:T(2,128)} %bitcast.15, bf16[256,4096]{1,0:T(8,128)(2,1)} %bitcast.13, bf16[8,512,512]{2,1,0:T(8,128)(2,1)} %bitcast.12, bf16[16,2,3072]{2,1,0:T(2,128)(2,1)S(1)} %all-to-all-done.x_ref.packed_ref, s32[1,32]{1,0:T(1,128)S(1)} %get-tuple-element.15.tile_rank_ref, ...), custom_call_target="tpu_custom_call" | custom-call | flops 2147483648 | bytes 8388608 | tf_op jit(solution)/shard_map/partial_sums/pallas_call | solution.py:435
  23.9 17.8 %all_to_all.10 = s32[128,7,1,128]{3,2,1,0:T(1,128)S(1)} all-to-all(s32[128,7,1,128]{3,2,1,0:T(1,128)S(1)} %bitcast.10), channel_id=1, replica_groups=mesh['row'=16,'col'=8] {'row','col'}, dimensions={0} | all-to-all | bytes 917504 | tf_op jit(solution)/shard_map/all_to_all | solution.py:455
  41.8 1.4 %bricks.1 = (f32[144,128]{1,0:T(8,128)S(1)}, s16[128,128]{1,0:T(8,128)(2,1)S(1)}) custom-call(s32[896,128]{1,0:T(8,128)S(1)} %bitcast.11, bf16[16,2,3072]{2,1,0:T(2,128)(2,1)S(1)} %all-to-all-done.x_ref.packed_ref, f32[4,4,128]{2,1,0:T(4,128)S(1)} %get-tuple-element.20.kappa_ref), custom_call_target="tpu_custom_call" | custom-call | flops 1073741824 | bytes 1048576 | tf_op jit(solution)/shard_map/bricks/pallas_call | solution.py:456
  43.2 3.6 %collective-permute-start.1 = (s16[128,128]{1,0:T(8,128)(2,1)S(1)}, s16[128,128]{1,0:T(8,128)(2,1)S(1)}, u32[]{:S(2)}, u32[]{:S(2)}) collective-permute-start(s16[128,128]{1,0:T(8,128)(2,1)S(1)} %get-tuple-element.22), channel_id=1, source_target_pairs={{1,2},{3,4},{5,6},{2,1},{4,3},{6,5},{9,10},{11,12},{13,14},{10,9},... | collective-permute-start | bytes 98312 | tf_op jit(solution)/shard_map/ppermute | solution.py:379
  46.8 0.1 collective-permute-start
  46.9 4.2 %collective-permute-done.1.odd_ref = s16[128,128]{1,0:T(8,128)(2,1)S(1)} collective-permute-done((s16[128,128]{1,0:T(8,128)(2,1)S(1)}, s16[128,128]{1,0:T(8,128)(2,1)S(1)}, u32[]{:S(2)}, u32[]{:S(2)}) %collective-permute-start.1) | collective-permute-done | bytes 32800 | tf_op jit(solution)/shard_map/ppermute | solution.py:379
  51.1 0.0 collective-permute-done.even_ref
  51.1 0.9 %prior.1 = f32[2,4,4,128]{3,2,1,0:T(4,128)} custom-call(f32[144,128]{1,0:T(8,128)S(1)} %get-tuple-element.21.own_ref, s16[128,128]{1,0:T(8,128)(2,1)S(1)} %collective-permute-done.even_ref, s16[128,128]{1,0:T(8,128)(2,1)S(1)} %collective-permute-done.1.odd_ref), custom_call_target="tpu_custom_call" | custom-call | flops 16777216 | bytes 1048576 | tf_op jit(solution)/shard_map/prior/pallas_call | solution.py:475
Async XLA Ops:
  1.4 16.1 %all-to-all-start = ((bf16[16,2,3072]{2,1,0:T(2,128)(2,1)}), bf16[16,2,3072]{2,1,0:T(2,128)(2,1)S(1)}, u32[]{:S(2)}, u32[]{:S(2)}) async-start(bf16[16,2,3072]{2,1,0:T(2,128)(2,1)} %get-tuple-element.14), calls=%async_computation | async-start | bytes 393216 | tf_op jit(solution)/shard_map/all_to_all | solution.py:418
  43.2 7.9 %collective-permute-start.1 = (s16[128,128]{1,0:T(8,128)(2,1)S(1)}, s16[128,128]{1,0:T(8,128)(2,1)S(1)}, u32[]{:S(2)}, u32[]{:S(2)}) collective-permute-start(s16[128,128]{1,0:T(8,128)(2,1)S(1)} %get-tuple-element.22), channel_id=1, source_target_pairs={{1,2},{3,4},{5,6},{2,1},{4,3},{6,5},{9,10},{11,12},{13,14},{10,9},... | collective-permute-start | bytes 98312 | tf_op jit(solution)/shard_map/ppermute | solution.py:379
  46.8 4.3 %collective-permute-start = (s16[128,128]{1,0:T(8,128)(2,1)S(1)}, s16[128,128]{1,0:T(8,128)(2,1)S(1)}, u32[]{:S(2)}, u32[]{:S(2)}) collective-permute-start(s16[128,128]{1,0:T(8,128)(2,1)S(1)} %get-tuple-element.22), channel_id=1, source_target_pairs={{0,1},{2,3},{4,5},{6,7},{1,0},{3,2},{5,4},{7,6},{8,9},{10,11},{12,... | collective-permute-start | bytes 98312 | tf_op jit(solution)/shard_map/ppermute | solution.py:379

commit v10 on v9

--- a/solution.py
+++ b/solution.py
@@ -251,6 +251,7 @@
             totals = [t + w.astype(F32) * sizes[c] for t, w in zip(totals, pair)]
         for v in range(NVEC):
             sums[v, q * ROWS : (q + 1) * ROWS, :] = totals[v]
+    level, inverse = level_of(jnp.maximum(jnp.abs(sums[0]), jnp.abs(sums[1])))
     part = iota((ROWS, 128), 1) // CAP
     for g in range(2):
         for j in range(3):
@@ -271,13 +272,13 @@
             for r, g in ((r, g) for r in range(some, some + 4) for g in range(2)):
                 at = (j * 2 + g) * ROWS + r
                 pair = jnp.where(sub < 4, sums[0, at : at + 1, :], sums[1, at : at + 1, :])
-                high = pair.astype(BF16).astype(F32)
-                low = pair - high
                 p = j * ROWS + r
                 cell = at_cells[g, p : p + 1, :]
                 wanted = [cell == (x * CY + sub % CY).astype(F32) for x in range(CX)]
-                rows = [jnp.where(w, part, 0.0) for part in (high, low) for w in wanted]
-                cells.append(jnp.concatenate(rows, axis=0).astype(BF16))
+                rows = jnp.concatenate([jnp.where(w, pair, 0.0) for w in wanted], axis=0)
+                high = rows.astype(BF16)
+                low = (rows - high.astype(F32)).astype(BF16)
+                cells.append(jnp.concatenate([high, low], axis=0))
                 z_at = wheres[g, p : p + 1, :].astype(BF16)
                 heights.append(jnp.where(z_at == z_row, one, none))
             both = both + lax.dot_general(
@@ -298,7 +299,6 @@
     for x in range(CX):
         at = FIELD + CX * CY + x * CY
         out_ref[at : at + CY, :] = kappa_ref[x]
-    level, inverse = level_of(out_ref[0:FIELD, :])
 
     def store(at, values):
         halo_ref[at : at + values.shape[0], :] = (

time: 52.4 us -> 52.4 us (level)
  no operation moved by 1% of the time
where the time goes in v10:
time: 52.4 us; the launch traced here: 52 us
  blocking collectives  17.8 us (34%)
  Pallas kernels  14.2 us (27%)
  starting transfers between devices  10.9 us (21%)
  waiting for transfers between devices  9.06 us (17%)
    all_to_all x1, blocking collectives, per_device(): lax.all_to_all(send.reshape(DEV, SLAB, 1, 128), ('row', 'col'), 0, 0, til...  17.8 us
    all_to_all x1, starting transfers between devices, per_device(): packed = lax.all_to_all(packed, 'row', 0, 0, tiled=True)  7.16 us
    pallas_call x1, Pallas kernels, per_device(): pl.pallas_call(send_kernel, out_shape=jax.ShapeDtypeStruct((DEV * SLAB, 1...  6.43 us
    all_to_all x1, waiting for transfers between devices, per_device(): packed = lax.all_to_all(packed, 'row', 0, 0, tiled=True)  4.86 us
    ppermute x2, waiting for transfers between devices, swapped(): return lax.ppermute(array, axis, pairs + [(b, a) for a, b in pairs])  4.2 us
    pallas_call x1, Pallas kernels, per_device(): pl.pallas_call(slots_kernel, out_shape=(pltpu.VMEM((1, points), jnp.int32...  4.01 us
    ppermute x2, starting transfers between devices, swapped(): return lax.ppermute(array, axis, pairs + [(b, a) for a, b in pairs])  3.71 us
    pallas_call x1, Pallas kernels, per_device(): pl.pallas_call(pack_kernel, out_shape=(pltpu.VMEM(packed_shape, BF16), pl...  1.43 us
  transfers between devices with their start and end apart: 3, of which 2 were waited for; matrix products, arithmetic and copies ran while one was open for 0% of the time, Pallas kernels for 8%

profile of v10, /device:TPU:8, one launch (start us, length us, event | category | flops | bytes accessed | tf_op | source)
XLA Modules:
  0.0 52.0 jit_solution(9378151194539230292)
XLA Ops:
  0.0 1.4 %pack.1 = (bf16[16,2,3072]{2,1,0:T(2,128)(2,1)}, f32[4,4,128]{2,1,0:T(4,128)S(1)}) custom-call(bf16[2,2048]{1,0:T(2,128)(2,1)} %bitcast.14, f32[4,4,128]{2,1,0:T(4,128)} %kappa_hbm.1), custom_call_target="tpu_custom_call" | custom-call | tf_op jit(solution)/shard_map/pack/pallas_call | solution.py:406
  1.4 7.2 %all-to-all-start = ((bf16[16,2,3072]{2,1,0:T(2,128)(2,1)}), bf16[16,2,3072]{2,1,0:T(2,128)(2,1)S(1)}, u32[]{:S(2)}, u32[]{:S(2)}) async-start(bf16[16,2,3072]{2,1,0:T(2,128)(2,1)} %get-tuple-element.14), calls=%async_computation | async-start | bytes 393216 | tf_op jit(solution)/shard_map/all_to_all | solution.py:418
  8.6 4.0 %slots.1 = (s32[1,16384]{1,0:T(1,128)S(1)}, s32[1,32]{1,0:T(1,128)S(1)}, f32[1,16384]{1,0:T(1,128)S(1)}, s32[128,128]{1,0:T(8,128)S(1)}, bf16[256,4096]{1,0:T(8,128)(2,1)S(1)}) custom-call(s32[1,16384]{1,0:T(1,128)} %perm_hbm.1, s32[1,32]{1,0:T(1,128)} %bitcast.17, bf16[256,4096]{1,0:T(8,128)(2,1)} %bitcast.16), custom_call_target="tpu_custom_call" | custom-call | flops 2147483648 | bytes 1048576 | tf_op jit(solution)/shard_map/slots/pallas_call | solution.py:419
  12.6 4.9 %all-to-all-done.x_ref.packed_ref = bf16[16,2,3072]{2,1,0:T(2,128)(2,1)S(1)} async-done(((bf16[16,2,3072]{2,1,0:T(2,128)(2,1)}), bf16[16,2,3072]{2,1,0:T(2,128)(2,1)S(1)}, u32[]{:S(2)}, u32[]{:S(2)}) %all-to-all-start) | async-done | bytes 196640 | tf_op jit(solution)/shard_map/all_to_all | solution.py:418
  17.5 6.4 %partial_sums.1 = s32[896,128]{1,0:T(8,128)S(1)} custom-call(s32[2,8]{1,0:T(2,128)} %bitcast.15, bf16[256,4096]{1,0:T(8,128)(2,1)} %bitcast.13, bf16[8,512,512]{2,1,0:T(8,128)(2,1)} %bitcast.12, bf16[16,2,3072]{2,1,0:T(2,128)(2,1)S(1)} %all-to-all-done.x_ref.packed_ref, s32[1,32]{1,0:T(1,128)S(1)} %get-tuple-element.15.tile_rank_ref, ...), custom_call_target="tpu_custom_call" | custom-call | flops 2147483648 | bytes 8388608 | tf_op jit(solution)/shard_map/partial_sums/pallas_call | solution.py:435
  23.9 17.8 %all_to_all.10 = s32[128,7,1,128]{3,2,1,0:T(1,128)S(1)} all-to-all(s32[128,7,1,128]{3,2,1,0:T(1,128)S(1)} %bitcast.10), channel_id=1, replica_groups=mesh['row'=16,'col'=8] {'row','col'}, dimensions={0} | all-to-all | bytes 917504 | tf_op jit(solution)/shard_map/all_to_all | solution.py:455
  41.8 1.4 %bricks.1 = (f32[144,128]{1,0:T(8,128)S(1)}, s16[128,128]{1,0:T(8,128)(2,1)S(1)}) custom-call(s32[896,128]{1,0:T(8,128)S(1)} %bitcast.11, bf16[16,2,3072]{2,1,0:T(2,128)(2,1)S(1)} %all-to-all-done.x_ref.packed_ref, f32[4,4,128]{2,1,0:T(4,128)S(1)} %get-tuple-element.20.kappa_ref), custom_call_target="tpu_custom_call" | custom-call | flops 1073741824 | bytes 1048576 | tf_op jit(solution)/shard_map/bricks/pallas_call | solution.py:456
  43.2 3.6 %collective-permute-start.1 = (s16[128,128]{1,0:T(8,128)(2,1)S(1)}, s16[128,128]{1,0:T(8,128)(2,1)S(1)}, u32[]{:S(2)}, u32[]{:S(2)}) collective-permute-start(s16[128,128]{1,0:T(8,128)(2,1)S(1)} %get-tuple-element.22), channel_id=1, source_target_pairs={{1,2},{3,4},{5,6},{2,1},{4,3},{6,5},{9,10},{11,12},{13,14},{10,9},... | collective-permute-start | bytes 98312 | tf_op jit(solution)/shard_map/ppermute | solution.py:379
  46.8 0.1 collective-permute-start
  46.9 4.2 %collective-permute-done.1.odd_ref = s16[128,128]{1,0:T(8,128)(2,1)S(1)} collective-permute-done((s16[128,128]{1,0:T(8,128)(2,1)S(1)}, s16[128,128]{1,0:T(8,128)(2,1)S(1)}, u32[]{:S(2)}, u32[]{:S(2)}) %collective-permute-start.1) | collective-permute-done | bytes 32800 | tf_op jit(solution)/shard_map/ppermute | solution.py:379
  51.1 0.0 collective-permute-done.even_ref
  51.1 0.9 %prior.1 = f32[2,4,4,128]{3,2,1,0:T(4,128)} custom-call(f32[144,128]{1,0:T(8,128)S(1)} %get-tuple-element.21.own_ref, s16[128,128]{1,0:T(8,128)(2,1)S(1)} %collective-permute-done.even_ref, s16[128,128]{1,0:T(8,128)(2,1)S(1)} %collective-permute-done.1.odd_ref), custom_call_target="tpu_custom_call" | custom-call | flops 16777216 | bytes 1048576 | tf_op jit(solution)/shard_map/prior/pallas_call | solution.py:475
Async XLA Ops:
  1.4 16.1 %all-to-all-start = ((bf16[16,2,3072]{2,1,0:T(2,128)(2,1)}), bf16[16,2,3072]{2,1,0:T(2,128)(2,1)S(1)}, u32[]{:S(2)}, u32[]{:S(2)}) async-start(bf16[16,2,3072]{2,1,0:T(2,128)(2,1)} %get-tuple-element.14), calls=%async_computation | async-start | bytes 393216 | tf_op jit(solution)/shard_map/all_to_all | solution.py:418
  43.2 7.9 %collective-permute-start.1 = (s16[128,128]{1,0:T(8,128)(2,1)S(1)}, s16[128,128]{1,0:T(8,128)(2,1)S(1)}, u32[]{:S(2)}, u32[]{:S(2)}) collective-permute-start(s16[128,128]{1,0:T(8,128)(2,1)S(1)} %get-tuple-element.22), channel_id=1, source_target_pairs={{1,2},{3,4},{5,6},{2,1},{4,3},{6,5},{9,10},{11,12},{13,14},{10,9},... | collective-permute-start | bytes 98312 | tf_op jit(solution)/shard_map/ppermute | solution.py:379
  46.8 4.3 %collective-permute-start = (s16[128,128]{1,0:T(8,128)(2,1)S(1)}, s16[128,128]{1,0:T(8,128)(2,1)S(1)}, u32[]{:S(2)}, u32[]{:S(2)}) collective-permute-start(s16[128,128]{1,0:T(8,128)(2,1)S(1)} %get-tuple-element.22), channel_id=1, source_target_pairs={{0,1},{2,3},{4,5},{6,7},{1,0},{3,2},{5,4},{7,6},{8,9},{10,11},{12,... | collective-permute-start | bytes 98312 | tf_op jit(solution)/shard_map/ppermute | solution.py:379
